TPU v7x, 256 devices: a whole 4x4x8 slice. The times are simulated.
256 devices in a mesh: dp: 32 (over x, y, core), vocab: 8 (over z).
Axes of the slice: x: 4, y: 4, z: 8, core: 2. Of those that a mesh axis runs over, the one named last changes fastest.
Arguments:
- student_hidden: bfloat16 [768, 3584], P('dp'), may hold values from -110 to 110
- teacher_hidden: bfloat16 [768, 4608], P('dp'), may hold values from -110 to 110
- student_head: bfloat16 [3584, 131072], P(None, ('dp', 'vocab')), may hold values from -0.09375 to 0.09375
- teacher_head: bfloat16 [4608, 131072], P(None, ('dp', 'vocab')), may hold values from -0.09375 to 0.09375
- live_count: int32 [32], P('dp'), may hold values from 1 to 24, as said below
- teacher_count: int32 [32], P('dp'), may hold values from 1 to 24, as said below
- teacher_dest: int32 [768], P('dp'), may hold values from 0 to 767, as said below
Outputs:
- distill_loss: float32 [], replicated
- grad_hidden: bfloat16 [768, 3584], P('dp', 'vocab')
- grad_head: bfloat16 [3584, 131072], P(None, ('dp', 'vocab'))
Inputs may be any that keep to these rules, and one draw needn't show every extreme that they name: Shard s's covered tokens are its first live_count[s] tokens; the counts sum to 384. Data shard j's filled teacher row slots are its first teacher_count[j] slots; the counts sum to 384. `teacher_dest`: A filled slot names the global index of a covered token; every covered token is named by exactly one filled slot. Unfilled slots hold arbitrary indices.
All inputs are finite; a program needn't handle non-finite values.
Results may differ from a plain program's by a relative error of at most 0.014.
Values may be sent and summed in bfloat16 or wider, within the bound.
No kernel may reach another device: no remote copies, remote signals or barrier semaphores. Data moves between devices by JAX's collectives and lax.ppermute only.
A program may use at most 128 MiB of HBM per device.

v0:
```python
import jax
import jax.numpy as jnp
from jax import lax
from jax.sharding import PartitionSpec as P

loss_scale = 65536.0


def per_device(
    student_hidden,
    teacher_hidden,
    student_head,
    teacher_head,
    live_count,
    teacher_count,
    teacher_dest,
):
    tok_dev = student_hidden.shape[0]
    data_size = lax.axis_size("dp")
    token_count = tok_dev * data_size
    live_total = token_count // 2
    grad_scale = loss_scale / live_total
    live_all, teach_all, dest_all = (
        lax.all_gather(live_count, "dp", axis=0, tiled=True),
        lax.all_gather(teacher_count, "dp", axis=0, tiled=True),
        lax.all_gather(teacher_dest, "dp", axis=0, tiled=True),
    )
    position = lax.broadcasted_iota(jnp.int32, (data_size, tok_dev), 1)
    live_flag = (position < live_all[:, None]).reshape(-1)
    slot_ok = (position < teach_all[:, None]).reshape(-1)
    gathered = lax.all_gather(student_hidden, "dp", axis=0, tiled=True)
    vocab_rows = student_head.shape[1]
    student_logits = jnp.dot(gathered, student_head, preferred_element_type=jnp.float32)
    packed = jnp.dot(
        lax.all_gather(teacher_hidden, "dp", axis=0, tiled=True),
        teacher_head,
        preferred_element_type=jnp.float32,
    )
    target = jnp.where(slot_ok, dest_all, token_count)
    teacher_logits = (
        jnp.zeros((token_count, vocab_rows), jnp.float32).at[target].set(packed, mode="drop")
    )
    teacher_top, student_top = lax.pmax(
        (jnp.max(teacher_logits, axis=1), jnp.max(student_logits, axis=1)), ("dp", "vocab")
    )
    teacher_weights = jnp.exp(teacher_logits - teacher_top[:, None])
    teacher_sum, student_sum, cross_sum = lax.psum(
        (
            jnp.sum(teacher_weights, axis=1),
            jnp.sum(jnp.exp(student_logits - student_top[:, None]), axis=1),
            jnp.sum(teacher_weights * (teacher_logits - student_logits), axis=1),
        ),
        ("dp", "vocab"),
    )
    teacher_norm = teacher_top + jnp.log(teacher_sum)
    student_norm = student_top + jnp.log(student_sum)
    divergence = cross_sum / teacher_sum - teacher_norm + student_norm
    distill_loss = jnp.sum(jnp.where(live_flag, divergence, 0.0)) / live_total
    probs_gap = jnp.exp(student_logits - student_norm[:, None]) - jnp.exp(
        teacher_logits - teacher_norm[:, None]
    )
    logit_grad = jnp.where(live_flag[:, None], probs_gap * grad_scale, 0.0).astype(jnp.bfloat16)
    grad_head = lax.dot_general(
        gathered, logit_grad, (((0,), (0,)), ((), ())), preferred_element_type=jnp.float32
    ).astype(jnp.bfloat16)
    columns = student_head.shape[0] // lax.axis_size("vocab")
    summed = lax.psum(
        lax.dot_general(
            logit_grad, student_head, (((1,), (1,)), ((), ())), preferred_element_type=jnp.float32
        ),
        ("dp", "vocab"),
    )
    own_block = lax.dynamic_slice(
        summed,
        (lax.axis_index("dp") * tok_dev, lax.axis_index("vocab") * columns),
        (tok_dev, columns),
    )
    return (distill_loss, own_block.astype(jnp.bfloat16), grad_head)


def solution(mesh):
    return jax.shard_map(
        per_device,
        mesh=mesh,
        in_specs=(
            P("dp", None),
            P("dp", None),
            P(None, ("dp", "vocab")),
            P(None, ("dp", "vocab")),
            P("dp"),
            P("dp"),
            P("dp"),
        ),
        out_specs=(P(), P("dp", "vocab"), P(None, ("dp", "vocab"))),
        check_vma=False,
    )
```

profile of v0, /device:TPU:1, one launch (start us, length us, event | category | flops | bytes accessed | tf_op | source)
XLA Modules:
  0.0 473.6 jit_solution(16044244641711408158)
XLA Ops:
  7.2 0.7 all-gather.5.cloned.1.call-update
  7.9 0.7 all-gather.3.cloned.1.call-update
  9.9 1.3 dynamic-slice
  11.9 0.8 dynamic-update-slice
  12.6 0.8 dynamic-update-slice.1
  13.4 0.8 dynamic-update-slice.2
  14.2 14.7 %all-reduce.3 = (s32[32]{0:T(128)S(1)}, s32[32]{0:T(128)S(1)}, s32[768]{0:T(1024)S(1)}) all-reduce(s32[32]{0:T(128)S(1)} %dynamic-update-slice, s32[32]{0:T(128)S(1)} %dynamic-update-slice.1, s32[768]{0:T(1024)S(1)} %dynamic-update-slice.2), channel_id=1, replica_groups=mesh['dp'=32,'vocab'=8] {'dp'}, use_global_device_ids=true, to_apply=%add | all-reduce | flops 832 | bytes 6656
  29.3 38.4 %all-gather.5.cloned.1.call-done = bf16[768,3584]{1,0:T(8,128)(2,1)} async-done(((bf16[24,3584]{1,0:T(8,128)(2,1)}), bf16[768,3584]{1,0:T(8,128)(2,1)}) %all-gather.5.cloned.1.call-update) | async-done | bytes 5505040 | tf_op jit(solution)/shard_map/all_gather | solution.py:31
  67.7 7.9 %fusion.4 = (f32[768]{0:T(1024)S(1)}, f32[768,512]{0,1:T(8,128)}) fusion(bf16[768,3584]{1,0:T(8,128)(2,1)} %all-gather.5.cloned.1.call-done, bf16[3584,512]{1,0:T(8,128)(2,1)} %param.9), kind=kOutput, calls=%fused_computation.17 | convolution fusion | flops 2818964736 | bytes 10750976 | tf_op jit(solution)/shard_map/dot_general | solution.py:33
  75.6 49.5 %all-gather.3.cloned.1.call-done = bf16[768,4608]{1,0:T(8,128)(2,1)} async-done(((bf16[24,4608]{1,0:T(8,128)(2,1)}), bf16[768,4608]{1,0:T(8,128)(2,1)}) %all-gather.3.cloned.1.call-update) | async-done | bytes 7077904 | tf_op jit(solution)/shard_map/all_gather | solution.py:35
  125.1 9.3 %fusion.5 = f32[768,512]{1,0:T(8,128)} fusion(bf16[768,4608]{1,0:T(8,128)(2,1)} %all-gather.3.cloned.1.call-done, bf16[4608,512]{1,0:T(8,128)(2,1)} %param.10), kind=kOutput, calls=%fused_computation.18 | convolution fusion | flops 3623878656 | bytes 13369344 | tf_op jit(solution)/shard_map/dot_general | solution.py:34
  134.4 6.6 %scatter_custom_fusion = f32[768,512]{1,0:T(8,128)S(1)} fusion(s32[768]{0:T(1024)S(1)} %compare_select_fusion, f32[768,512]{1,0:T(8,128)} %fusion.5, f32[]{:T(128)} %constant.12.clone.1), kind=kCustom, calls=%fused_computation.8 | custom fusion | bytes 1573376 | tf_op jit(solution)/shard_map/scatter | solution.py:41
  141.0 0.5 copy.12
  141.5 0.2 reduce_max.18
  141.6 75.6 %all-reduce.6 = (f32[768]{0:T(1024)S(1)}, f32[768]{0:T(1024)S(1)}) all-reduce(f32[768]{0:T(1024)S(1)} %get-tuple-element.21, f32[768]{0:T(1024)S(1)} %reduce_max.18), channel_id=1, replica_groups=mesh['dp'=32,'vocab'=8] {'dp','vocab'}, use_global_device_ids=true, to_apply=%region_8.9 | all-reduce | flops 1536 | bytes 12288 | tf_op jit(solution)/shard_map/pmax | solution.py:43
  217.3 2.1 multiply_reduce_fusion
  219.4 74.5 %all-reduce.5 = (f32[768]{0:T(1024)S(1)}, f32[768]{0:T(1024)S(1)}) all-reduce(f32[768]{0:T(1024)S(1)} %get-tuple-element.11, f32[768]{0:T(1024)S(1)} %get-tuple-element.10), channel_id=1, replica_groups=mesh['dp'=32,'vocab'=8] {'dp','vocab'}, use_global_device_ids=true, to_apply=%region_10.11 | all-reduce | flops 1536 | bytes 12288 | tf_op jit(solution)/shard_map/psum | solution.py:47
  293.9 0.5 select_convert_fusion
  294.4 8.2 %fusion.6 = f32[768,3584]{1,0:T(8,128)} fusion(bf16[768,512]{0,1:T(8,128)(2,1)S(1)} %select_convert_fusion, bf16[3584,512]{1,0:T(8,128)(2,1)} %param.9), kind=kOutput, calls=%fused_computation.19 | convolution fusion | flops 2818572288 | bytes 15466496 | tf_op jit(solution)/shard_map/dot_general | solution.py:68
  302.6 4.5 fusion
  307.1 5.9 %copy.15 = bf16[3584,512]{1,0:T(8,128)(2,1)} copy(bf16[3584,512]{0,1:T(8,128)(2,1)} %fusion) | data formatting | bytes 7340032
  313.0 149.9 %all-reduce.8 = (f32[768]{0:T(1024)S(1)}, bf16[768,3584]{1,0:T(8,128)(2,1)}) all-reduce(f32[768]{0:T(1024)S(1)} %get-tuple-element.9, f32[768,3584]{1,0:T(8,128)} %fusion.6), channel_id=1, replica_groups=mesh['dp'=32,'vocab'=8] {'dp','vocab'}, use_global_device_ids=true, to_apply=%region_4.5 | all-reduce | flops 2753280 | bytes 16521216 | tf_op jit(solution)/shard_map/psum | solution.py:47
  462.9 0.6 select_reduce_fusion
  464.2 1.5 dynamic_slice.5
  (18 shorter events, 0.5 us)
Async XLA Ops:
  7.2 60.5 %all-gather.5.cloned.1.call-start = ((), (), s32[]{:S(2)}) async-start(), calls=%async_computation.1 | async-start | bytes 5677056 | tf_op jit(solution)/shard_map/all_gather | solution.py:31
  7.9 117.2 %all-gather.3.cloned.1.call-start = ((), (), s32[]{:S(2)}) async-start(), calls=%async_computation | async-start | bytes 7299072 | tf_op jit(solution)/shard_map/all_gather | solution.py:35
  217.3 76.6 %copy-start = (f32[768,512]{0,1:T(8,128)S(1)}, f32[768,512]{0,1:T(8,128)}, u32[]{:S(2)}) copy-start(f32[768,512]{0,1:T(8,128)} %get-tuple-element.22) | copy-start | bytes 4718596
  293.9 8.7 %slice-start = ((s8[5505024]{0:T(1024)(128)(4,1)}), s8[4194304]{0:T(1024)(128)(4,1)S(1)}, s32[]{:S(2)}) async-start(s8[5505024]{0:T(1024)(128)(4,1)} %bitcast.13), calls=%async_computation.2 | async-start | bytes 8388608
  294.4 8.2 %slice-start.1 = ((s8[5505024]{0:T(1024)(128)(4,1)}), s8[1310720]{0:T(1024)(128)(4,1)S(1)}, s32[]{:S(2)}) async-start(s8[5505024]{0:T(1024)(128)(4,1)} %bitcast.13), calls=%async_computation.3 | async-start | bytes 2621440
Sparse Core Ops, SparseCore 0:
  10.5 57.1 all-gather.4
  70.2 54.7 all-gather.2
where the time goes:
time: 474 us
  blocking collectives  315 us (66%)
  waiting for transfers between devices  89.3 us (19%)
  matrix products  29.9 us (6%)
  local copies, waits for them, and re-layouts  18.2 us (4%)
  between operations  17.9 us (4%)
    psum x2, blocking collectives, per_device(): lax.psum((jnp.sum(teacher_weights, axis=1), jnp.sum(jnp.exp(student_logit...  224 us
    pmax x1, blocking collectives, per_device(): lax.pmax((jnp.max(teacher_logits, axis=1), jnp.max(student_logits, axis=1...  75.6 us
    all_gather x1, waiting for transfers between devices, per_device(): lax.all_gather(teacher_hidden, 'dp', axis=0, tiled=True)  49.5 us
    all_gather x1, waiting for transfers between devices, per_device(): gathered = lax.all_gather(student_hidden, 'dp', axis=0, tiled=True)  38.4 us
    unnamed x1, blocking collectives  14.7 us
    unnamed x14, local copies, waits for them, and re-layouts  9.54 us
  transfers between devices with their start and end apart: 2, of which 2 were waited for; matrix products, arithmetic and copies ran while one was open for 2% of the time, Pallas kernels for 0%

commit v1 on v0

v1 whole, which is shorter than its diff:
```python
import functools

import jax
import jax.numpy as jnp
from jax import lax
from jax.experimental import pallas as pl
from jax.experimental.pallas import tpu as pltpu
from jax.sharding import PartitionSpec as P

loss_scale = 65536.0
MIB = 1 << 20
bf16 = jnp.bfloat16
f32 = jnp.float32


def params(mib=40):
    return pltpu.CompilerParams(
        vmem_limit_bytes=mib * MIB, dimension_semantics=("arbitrary",)
    )


def student_kernel(h_ref, w_ref, s_ref, lse_ref):
    k = pl.program_id(0)
    part = jnp.dot(h_ref[...], w_ref[...], preferred_element_type=f32)

    @pl.when(k == 0)
    def _():
        s_ref[...] = part

    @pl.when(k > 0)
    def _():
        s_ref[...] += part

    @pl.when(k == pl.num_programs(0) - 1)
    def _():
        s = s_ref[...]
        top = jnp.max(s, axis=1, keepdims=True)
        lse = top + jnp.log(jnp.sum(jnp.exp(s - top), axis=1, keepdims=True))
        lse_ref[...] = jnp.broadcast_to(lse, lse_ref.shape)


def student_logits(h, w, chunks):
    rows = h.shape[0]
    depth, cols = w.shape
    kb = depth // chunks
    return pl.pallas_call(
        student_kernel,
        grid=(chunks,),
        in_specs=[
            pl.BlockSpec((rows, kb), lambda k: (0, k)),
            pl.BlockSpec((kb, cols), lambda k: (k, 0)),
        ],
        out_specs=[
            pl.BlockSpec((rows, cols), lambda k: (0, 0)),
            pl.BlockSpec((rows, 128), lambda k: (0, 0)),
        ],
        out_shape=[
            jax.ShapeDtypeStruct((rows, cols), f32),
            jax.ShapeDtypeStruct((rows, 128), f32),
        ],
        compiler_params=params(),
        name="student_logits",
    )(h, w)


def teacher_kernel(h_ref, w_ref, target_ref, s_ref, lse_ref, t_ref, stat_ref, acc):
    k = pl.program_id(0)
    part = jnp.dot(h_ref[...], w_ref[...], preferred_element_type=f32)

    @pl.when(k == 0)
    def _():
        acc[...] = part

    @pl.when(k > 0)
    def _():
        acc[...] += part

    @pl.when(k == pl.num_programs(0) - 1)
    def _():
        rows, cols = acc.shape
        token = lax.broadcasted_iota(jnp.int32, (rows, rows), 0)
        pick = (token == target_ref[...]).astype(f32).astype(bf16)
        value = acc[...]
        high = value.astype(bf16)
        rest = value - high.astype(f32)
        mid = rest.astype(bf16)
        low = (rest - mid.astype(f32)).astype(bf16)
        t = jnp.dot(pick, high, preferred_element_type=f32)
        t += jnp.dot(pick, mid, preferred_element_type=f32)
        t += jnp.dot(pick, low, preferred_element_type=f32)
        t_ref[...] = t
        top = jnp.max(t, axis=1, keepdims=True)
        weight = jnp.exp(t - top)
        total = jnp.sum(weight, axis=1, keepdims=True)
        cross = jnp.sum(weight * (t - s_ref[...]), axis=1, keepdims=True) / total
        lse = top + jnp.log(total)
        lane = lax.broadcasted_iota(jnp.int32, (rows, 128), 1)
        stats = jnp.where(lane == 0, lse_ref[...], jnp.where(lane == 1, lse, cross))
        flat = jnp.transpose(stats)
        for i in range(3):
            for j in range(rows // 128):
                stat_ref[i * (rows // 128) + j, :] = flat[i, j * 128 : (j + 1) * 128]
        used = 3 * (rows // 128)
        stat_ref[used:, :] = jnp.zeros((stat_ref.shape[0] - used, 128), f32)


def teacher_logits(h, w, target, s, lse, kb):
    rows = h.shape[0]
    depth, cols = w.shape
    chunks = depth // kb
    first = (h.shape[1] - depth) // kb
    stat_rows = -(-3 * (rows // 128) // 8) * 8
    whole = lambda shape: pl.BlockSpec(shape, lambda k: (0, 0))
    return pl.pallas_call(
        teacher_kernel,
        grid=(chunks,),
        in_specs=[
            pl.BlockSpec((rows, kb), lambda k: (0, first + k)),
            pl.BlockSpec((kb, cols), lambda k: (k, 0)),
            whole((1, rows)),
            whole((rows, cols)),
            whole((rows, 128)),
        ],
        out_specs=[whole((rows, cols)), whole((stat_rows, 128))],
        out_shape=[
            jax.ShapeDtypeStruct((rows, cols), f32),
            jax.ShapeDtypeStruct((stat_rows, 128), f32),
        ],
        scratch_shapes=[pltpu.VMEM((rows, cols), f32)],
        compiler_params=params(),
        name="teacher_logits",
    )(h, w, target, s, lse)


def merged(x, n):
    student, teacher, cross = x[:, 0:n], x[:, n : 2 * n], x[:, 2 * n : 3 * n]
    s_top = jnp.max(student, axis=0)
    s_norm = s_top + jnp.log(jnp.sum(jnp.exp(student - s_top[None]), axis=0))
    t_top = jnp.max(teacher, axis=0)
    weight = jnp.exp(teacher - t_top[None])
    total = jnp.sum(weight, axis=0)
    return s_norm, t_top + jnp.log(total), jnp.sum(weight * cross, axis=0) / total


def merge_kernel(n, x_ref, out_ref):
    s_norm, t_norm, cross = merged(x_ref[...], n)
    out_ref[:, 0:n] = jnp.broadcast_to(s_norm[None], (out_ref.shape[0],) + s_norm.shape)
    out_ref[:, n : 2 * n] = jnp.broadcast_to(t_norm[None], (out_ref.shape[0],) + s_norm.shape)
    out_ref[:, 2 * n : 3 * n] = jnp.broadcast_to(cross[None], (out_ref.shape[0],) + s_norm.shape)
    rest = out_ref.shape[1] - 3 * n
    out_ref[:, 3 * n :] = jnp.zeros((out_ref.shape[0], rest, 128), f32)


def merge(x, n, copies):
    return pl.pallas_call(
        functools.partial(merge_kernel, n),
        out_shape=jax.ShapeDtypeStruct((copies,) + x.shape[1:], f32),
        compiler_params=pltpu.CompilerParams(vmem_limit_bytes=24 * MIB),
        name="merge_stats",
    )(x)


def norm_kernel(n, live_total, x_ref, live_ref, norm_ref, loss_ref):
    s_norm, t_norm, cross = merged(x_ref[...], n)
    live = live_ref[...] > 0
    term = jnp.where(live, cross - t_norm + s_norm, 0.0)
    loss_ref[...] = jnp.sum(term, keepdims=True) / live_total
    norm_ref[0:n, :] = jnp.where(live, s_norm, jnp.inf)
    norm_ref[n : 2 * n, :] = jnp.where(live, t_norm, jnp.inf)


def norms(x, live, n, live_total):
    return pl.pallas_call(
        functools.partial(norm_kernel, n, live_total),
        out_shape=[
            jax.ShapeDtypeStruct((2 * n, 128), f32),
            jax.ShapeDtypeStruct((1, 1), f32),
        ],
        compiler_params=pltpu.CompilerParams(vmem_limit_bytes=24 * MIB),
        name="norms",
    )(x, live)


def column(norm_ref, first, n):
    return jnp.concatenate(
        [
            jnp.transpose(jnp.broadcast_to(norm_ref[first + j : first + j + 1, :], (128, 128)))[:, 0:1]
            for j in range(n)
        ],
        axis=0,
    )


def send_kernel(grad_scale, tok, core_ref, s_ref, t_ref, norm_ref, w_ref, g_ref, out_ref, full, mine):
    k = pl.program_id(0)
    rows = s_ref.shape[0]
    n = rows // 128

    @pl.when(k == 0)
    def _():
        gap = jnp.exp(s_ref[...] - column(norm_ref, 0, n)) - jnp.exp(
            t_ref[...] - column(norm_ref, n, n)
        )
        full[...] = gap * grad_scale
        g_ref[...] = full[...].astype(bf16)
        core = core_ref[0]
        for j in range(rows // (2 * tok)):
            start = pl.multiple_of(2 * tok * j + tok * (1 - core), 8)
            mine[pl.ds(tok * j, tok), :] = full[pl.ds(start, tok), :]

    out_ref[...] = lax.dot_general(
        mine[...].astype(bf16), w_ref[...], (((1,), (1,)), ((), ())), preferred_element_type=f32
    ).astype(bf16)


def grad_send(core, s, t, norm, w, grad_scale, tok, chunks):
    rows, cols = s.shape
    depth = w.shape[0]
    kb = depth // chunks
    whole = lambda shape: pl.BlockSpec(shape, lambda k: (0, 0))
    return pl.pallas_call(
        functools.partial(send_kernel, grad_scale, tok),
        grid=(chunks,),
        in_specs=[
            pl.BlockSpec(memory_space=pltpu.SMEM),
            whole((rows, cols)),
            whole((rows, cols)),
            whole(norm.shape),
            pl.BlockSpec((kb, cols), lambda k: (k, 0)),
        ],
        out_specs=[whole((rows, cols)), pl.BlockSpec((rows // 2, kb), lambda k: (0, k))],
        out_shape=[
            jax.ShapeDtypeStruct((rows, cols), bf16),
            jax.ShapeDtypeStruct((rows // 2, depth), bf16),
        ],
        scratch_shapes=[pltpu.VMEM((rows, cols), f32), pltpu.VMEM((rows // 2, cols), f32)],
        compiler_params=params(),
        name="grad_send",
    )(core, s, t, norm, w)


def keep_kernel(tok, core_ref, g_ref, w_ref, got_ref, out_ref, full, mine):
    rows = g_ref.shape[0]

    @pl.when(pl.program_id(0) == 0)
    def _():
        full[...] = g_ref[...].astype(f32)
        core = core_ref[0]
        for j in range(rows // (2 * tok)):
            start = pl.multiple_of(2 * tok * j + tok * core, 8)
            mine[pl.ds(tok * j, tok), :] = full[pl.ds(start, tok), :]

    part = lax.dot_general(
        mine[...].astype(bf16), w_ref[...], (((1,), (1,)), ((), ())), preferred_element_type=f32
    )
    out_ref[...] = (part + got_ref[...].astype(f32)).astype(bf16)


def grad_keep(core, g, w, got, tok, chunks):
    rows, cols = g.shape
    depth = w.shape[0]
    kb = depth // chunks
    return pl.pallas_call(
        functools.partial(keep_kernel, tok),
        grid=(chunks,),
        in_specs=[
            pl.BlockSpec(memory_space=pltpu.SMEM),
            pl.BlockSpec((rows, cols), lambda k: (0, 0)),
            pl.BlockSpec((kb, cols), lambda k: (k, 0)),
            pl.BlockSpec((rows // 2, kb), lambda k: (0, k)),
        ],
        out_specs=pl.BlockSpec((rows // 2, kb), lambda k: (0, k)),
        out_shape=jax.ShapeDtypeStruct((rows // 2, depth), bf16),
        scratch_shapes=[pltpu.VMEM((rows, cols), f32), pltpu.VMEM((rows // 2, cols), f32)],
        compiler_params=params(),
        name="grad_keep",
    )(core, g, w, got)


def head_kernel(h_ref, g_ref, out_ref):
    out_ref[...] = lax.dot_general(
        h_ref[...], g_ref[...], (((0,), (0,)), ((), ())), preferred_element_type=f32
    ).astype(bf16)


def grad_head_of(h, g, depth, chunks):
    rows, cols = g.shape
    kb = depth // chunks
    return pl.pallas_call(
        head_kernel,
        grid=(chunks,),
        in_specs=[
            pl.BlockSpec((rows, kb), lambda k: (0, k)),
            pl.BlockSpec((rows, cols), lambda k: (0, 0)),
        ],
        out_specs=pl.BlockSpec((kb, cols), lambda k: (k, 0)),
        out_shape=jax.ShapeDtypeStruct((depth, cols), bf16),
        compiler_params=params(),
        name="grad_head",
    )(h, g)


def per_device(
    student_hidden,
    teacher_hidden,
    student_head,
    teacher_head,
    live_count,
    teacher_count,
    teacher_dest,
):
    tok, depth = student_hidden.shape
    shards, slices = lax.axis_size("dp"), lax.axis_size("vocab")
    rows = tok * shards
    live_total = rows // 2
    n = rows // 128
    core = (lax.axis_index("dp") % 2).astype(jnp.int32).reshape(1)
    swap = [(i, i ^ 1) for i in range(shards)]
    same_core = [list(range(c, shards, 2)) for c in range(2)]

    packed = jnp.concatenate([student_hidden, teacher_hidden], axis=1)
    gathered = lax.all_gather(packed, "dp", axis=0, tiled=True)

    own = jnp.concatenate([teacher_dest, live_count, teacher_count])
    table = lax.all_to_all(
        jnp.broadcast_to(own[None], (shards, tok + 2)), "dp", 0, 0, tiled=True
    )
    position = lax.broadcasted_iota(jnp.int32, (shards, tok), 1)
    live = (position < table[:, tok : tok + 1]).astype(f32).reshape(n, 128)
    filled = position < table[:, tok + 1 : tok + 2]
    target = jnp.where(filled, table[:, :tok], rows).reshape(1, rows)

    s, s_lse = student_logits(gathered, student_head, 4)
    t, stats = teacher_logits(gathered, teacher_head, target, s, s_lse, 512)

    stats = lax.all_to_all(
        jnp.broadcast_to(stats[None], (shards,) + stats.shape), "dp", 0, 0
    )
    stats = lax.all_to_all(merge(stats, n, slices), "vocab", 0, 0)
    norm, loss = norms(stats, live, n, live_total)

    g, other = grad_send(core, s, t, norm, student_head, loss_scale / live_total, tok, 7)
    got = lax.ppermute(other, "dp", swap)
    grad_head = grad_head_of(gathered, g, depth, 7)
    mine = grad_keep(core, g, student_head, got, tok, 7)
    parts = lax.all_to_all(
        mine.reshape(shards // 2, tok, depth), "dp", 0, 0, axis_index_groups=same_core
    )
    part = jnp.sum(parts.astype(f32), axis=0).astype(bf16)
    part = part.reshape(tok, slices, depth // slices).transpose(1, 0, 2)
    parts = lax.all_to_all(part, "vocab", 0, 0)
    grad_hidden = jnp.sum(parts.astype(f32), axis=0).astype(bf16)
    return (loss[0, 0], grad_hidden, grad_head)


def solution(mesh):
    return jax.shard_map(
        per_device,
        mesh=mesh,
        in_specs=(
            P("dp", None),
            P("dp", None),
            P(None, ("dp", "vocab")),
            P(None, ("dp", "vocab")),
            P("dp"),
            P("dp"),
            P("dp"),
        ),
        out_specs=(P(), P("dp", "vocab"), P(None, ("dp", "vocab"))),
        check_vma=False,
    )
```

time: 474 us -> 218 us (0.46)
  blocking collectives: 315 us -> 53.4 us
  Pallas kernels: 0 us -> 33.3 us
  matrix products: 29.9 us -> 0 us
  starting transfers between devices: 0.08 us -> 17 us
  waiting for transfers between devices: 89.3 us -> 79.3 us
  local copies, waits for them, and re-layouts: 18.2 us -> 13.3 us
    psum x2 -> x0, blocking collectives: 224 us -> none  [per_device(): lax.psum((jnp.sum(teacher_weights, axis=1), jnp.sum(jnp.exp(student_logit...]
    pmax x1 -> x0, blocking collectives: 75.6 us -> none  [per_device(): lax.pmax((jnp.max(teacher_logits, axis=1), jnp.max(student_logits, axis=1...]
    all_to_all x0 -> x2, blocking collectives: none -> 53.4 us  [the longest x1 38.1 us: per_device(): lax.all_to_all(mine.reshape(shards // 2, tok, depth), 'dp', 0, 0, axis_in...]
    pallas_call x0 -> x7, Pallas kernels: none -> 33.3 us  [the longest x1 12.1 us: teacher_logits(): pl.pallas_call(teacher_kernel, grid=(chunks,), in_specs=[pl.BlockSpec((ro...]
    all_gather x2 -> x1, waiting for transfers between devices: 87.9 us -> 56.5 us  [per_device(): gathered = lax.all_gather(packed, 'dp', axis=0, tiled=True)]
    dot_general x4 -> x0, matrix products: 29.9 us -> none  [the longest x1 9.34 us: per_device(): jnp.dot(lax.all_gather(teacher_hidden, 'dp', axis=0, tiled=True), teacher...]
    all_to_all x0 -> x3, waiting for transfers between devices: none -> 18.1 us  [the longest x1 10.3 us: per_device(): lax.all_to_all(jnp.broadcast_to(stats[None], (shards,) + stats.shape), 'd...]
    all_to_all x0 -> x3, starting transfers between devices: none -> 15.5 us  [the longest x1 6.73 us: per_device(): stats = lax.all_to_all(merge(stats, n, slices), 'vocab', 0, 0)]
  transfers between devices with their start and end apart: 2 -> 5, of which waited for: 2 -> 4; matrix products, arithmetic and copies ran while one was open for 2% -> 1% of each run, Pallas kernels for 0% -> 3%
where the time goes in v1:
time: 218 us; the launch traced here: 217 us
  waiting for transfers between devices  79.3 us (36%)
  blocking collectives  53.4 us (24%)
  Pallas kernels  33.3 us (15%)
  starting transfers between devices  17 us (8%)
  between operations  15.4 us (7%)
  local copies, waits for them, and re-layouts  13.3 us (6%)
  other arithmetic  5.5 us (3%)
    all_gather x1, waiting for transfers between devices, per_device(): gathered = lax.all_gather(packed, 'dp', axis=0, tiled=True)  56.5 us
    all_to_all x1, blocking collectives, per_device(): lax.all_to_all(mine.reshape(shards // 2, tok, depth), 'dp', 0, 0, axis_in...  38.1 us
    all_to_all x1, blocking collectives, per_device(): lax.all_to_all(jnp.broadcast_to(own[None], (shards, tok + 2)), 'dp', 0, 0...  15.3 us
    pallas_call x1, Pallas kernels, teacher_logits(): pl.pallas_call(teacher_kernel, grid=(chunks,), in_specs=[pl.BlockSpec((ro...  12.1 us
    unnamed x12, local copies, waits for them, and re-layouts  11.2 us
    all_to_all x1, waiting for transfers between devices, per_device(): lax.all_to_all(jnp.broadcast_to(stats[None], (shards,) + stats.shape), 'd...  10.3 us
    all_to_all x1, waiting for transfers between devices, per_device(): stats = lax.all_to_all(merge(stats, n, slices), 'vocab', 0, 0)  7.79 us
    all_to_all x1, starting transfers between devices, per_device(): stats = lax.all_to_all(merge(stats, n, slices), 'vocab', 0, 0)  6.73 us
  transfers between devices with their start and end apart: 5, of which 4 were waited for; matrix products, arithmetic and copies ran while one was open for 1% of the time, Pallas kernels for 3%

profile of v1, /device:TPU:1, one launch (start us, length us, event | category | flops | bytes accessed | tf_op | source)
XLA Modules:
  0.0 217.4 jit_solution(12210600050598004272)
XLA Ops:
  7.2 1.8 pad_maximum_fusion
  11.1 15.3 %all_to_all.29 = s32[32,1,26]{2,1,0:T(1,128)S(1)} all-to-all(s32[32,1,26]{2,1,0:T(1,128)S(1)} %broadcast_in_dim.8), channel_id=1, replica_groups=mesh['dp'=32,'vocab'=8] {'dp'}, dimensions={0} | all-to-all | bytes 6656 | tf_op jit(solution)/shard_map/all_to_all | solution.py:325
  26.8 56.5 %all-gather.2.cloned.1.call-done.h_ref = bf16[768,8192]{1,0:T(8,128)(2,1)} async-done(((bf16[24,8192]{1,0:T(8,128)(2,1)}), bf16[768,8192]{1,0:T(8,128)(2,1)}) %all-gather.2.cloned.1.call-update) | async-done | bytes 12582928 | tf_op jit(solution)/shard_map/all_gather | solution.py:322
  83.3 2.0 copy-done.1
  85.3 6.6 %student_logits.1 = (f32[768,512]{1,0:T(8,128)S(1)}, f32[768,128]{1,0:T(8,128)S(1)}) custom-call(bf16[768,8192]{1,0:T(8,128)(2,1)} %all-gather.2.cloned.1.call-done.h_ref, bf16[3584,512]{1,0:T(8,128)(2,1)S(1)} %copy-done.1), custom_call_target="tpu_custom_call" | custom-call | tf_op jit(solution)/shard_map/student_logits/pallas_call | solution.py:46
  91.9 12.1 %teacher_logits.1 = (f32[768,512]{1,0:T(8,128)S(1)}, f32[24,128]{1,0:T(8,128)S(1)}) custom-call(bf16[768,8192]{1,0:T(8,128)(2,1)} %all-gather.2.cloned.1.call-done.h_ref, bf16[4608,512]{1,0:T(8,128)(2,1)S(1)} %copy-done.3, s32[1,768]{1,0:T(1,128)S(1)} %reshape.31.target_ref, f32[768,512]{1,0:T(8,128)S(1)} %get-tuple-element.11.s_ref, ...), custom_call_target="tpu_custom_call" | custom-call | tf_op jit(solution)/shard_map/teacher_logits/pallas_call | solution.py:114
  104.0 1.1 copy-done.4
  105.2 0.8 broadcast_in_dim.18
  106.0 5.4 %all-to-all-start.1 = ((f32[32,24,128]{2,1,0:T(8,128)}), f32[32,24,128]{2,1,0:T(8,128)S(1)}, u32[]{:S(2)}, u32[]{:S(2)}) async-start(f32[32,24,128]{2,1,0:T(8,128)} %broadcast_in_dim.18), calls=%async_computation.1 | async-start | bytes 786432 | tf_op jit(solution)/shard_map/all_to_all | solution.py:336
  111.4 10.3 %all-to-all-done.1.x_ref = f32[32,24,128]{2,1,0:T(8,128)S(1)} async-done(((f32[32,24,128]{2,1,0:T(8,128)}), f32[32,24,128]{2,1,0:T(8,128)S(1)}, u32[]{:S(2)}, u32[]{:S(2)}) %all-to-all-start.1) | async-done | bytes 393248 | tf_op jit(solution)/shard_map/all_to_all | solution.py:336
  121.7 0.8 merge_stats.1
  122.5 6.7 %all-to-all-start.2 = ((f32[8,24,128]{2,1,0:T(8,128)}), f32[8,24,128]{2,1,0:T(8,128)S(1)}, u32[]{:S(2)}, u32[]{:S(2)}) async-start(f32[8,24,128]{2,1,0:T(8,128)} %merge_stats.1), calls=%async_computation.2 | async-start | bytes 196608 | tf_op jit(solution)/shard_map/all_to_all | solution.py:339
  129.4 7.8 %all-to-all-done.2.x_ref = f32[8,24,128]{2,1,0:T(8,128)S(1)} async-done(((f32[8,24,128]{2,1,0:T(8,128)}), f32[8,24,128]{2,1,0:T(8,128)S(1)}, u32[]{:S(2)}, u32[]{:S(2)}) %all-to-all-start.2) | async-done | bytes 98336 | tf_op jit(solution)/shard_map/all_to_all | solution.py:339
  137.8 2.0 copy-done.2
  139.9 1.4 copy-done.5
  141.3 3.9 %grad_send.1 = (bf16[768,512]{1,0:T(8,128)(2,1)S(1)}, bf16[384,3584]{1,0:T(8,128)(2,1)S(1)}) custom-call(s32[1]{0:T(128)} %bitcast.2.core_ref, f32[768,512]{1,0:T(8,128)S(1)} %get-tuple-element.11.s_ref, f32[768,512]{1,0:T(8,128)S(1)} %copy-done.5, f32[12,128]{1,0:T(8,128)S(1)} %get-tuple-element.16.norm_ref, bf16[3584,512]{1,0:T(8,128)(2,1)S(1)} %copy-done.2), custom_call_target="tpu_custom_call" | custom-call | tf_op jit(solution)/shard_map/grad_send/pallas_call | solution.py:221
  145.1 1.5 collective-permute-start
  146.6 4.7 %collective-permute-done.got_ref = bf16[384,3584]{1,0:T(8,128)(2,1)S(1)} collective-permute-done((bf16[384,3584]{1,0:T(8,128)(2,1)S(1)}, bf16[384,3584]{1,0:T(8,128)(2,1)S(1)}, u32[]{:S(2)}, u32[]{:S(2)}) %collective-permute-start) | collective-permute-done | bytes 2752544 | tf_op jit(solution)/shard_map/ppermute | solution.py:343
  151.3 3.5 %grad_keep.1 = bf16[384,3584]{1,0:T(8,128)(2,1)S(1)} custom-call(s32[1]{0:T(128)} %bitcast.2.core_ref, bf16[768,512]{1,0:T(8,128)(2,1)S(1)} %get-tuple-element.17.g_ref, bf16[3584,512]{1,0:T(8,128)(2,1)S(1)} %copy-done.2, bf16[384,3584]{1,0:T(8,128)(2,1)S(1)} %collective-permute-done.got_ref), custom_call_target="tpu_custom_call" | custom-call | tf_op jit(solution)/shard_map/grad_keep/pallas_call | solution.py:263
  154.8 38.1 %all_to_all.30 = bf16[16,24,3584]{2,1,0:T(8,128)(2,1)} all-to-all(bf16[16,24,3584]{2,1,0:T(8,128)(2,1)S(1)} %bitcast.5), channel_id=1, replica_groups={{0,16,32,48,64,80,96,112,128,144,160,176,192,208,224,240},{8,24,40,56,7..., dimensions={0} | all-to-all | bytes 5505024 | tf_op jit(solution)/shard_map/all_to_all | solution.py:346
  192.9 2.2 %reduce_sum.24 = bf16[24,3584]{1,0:T(8,128)(2,1)S(1)} reduce(bf16[16,24,3584]{2,1,0:T(8,128)(2,1)} %all_to_all.30, bf16[]{:T(256)} %constant.24.clone.1), dimensions={0}, to_apply=%region_0.1 | reduce | flops 1290240 | bytes 2924546 | tf_op jit(solution)/shard_map/reduce_sum | solution.py:349
  196.0 3.4 %all-to-all-start.4 = ((bf16[8,24,448]{2,1,0:T(8,128)(2,1)}), bf16[8,24,448]{2,1,0:T(8,128)(2,1)S(1)}, u32[]{:S(2)}, u32[]{:S(2)}) async-start(bf16[8,24,448]{2,1,0:T(8,128)(2,1)} %copy.12), calls=%async_computation.4 | async-start | bytes 393216 | tf_op jit(solution)/shard_map/all_to_all | solution.py:351
  199.5 4.6 %copy-done = bf16[768,8192]{1,0:T(8,128)(2,1)S(1)} copy-done((bf16[768,8192]{1,0:T(8,128)(2,1)S(1)}, bf16[768,8192]{1,0:T(8,128)(2,1)}, u32[]{:S(2)}) %copy-start) | copy-done | bytes 12582936
  204.0 5.8 %grad_head.1 = bf16[3584,512]{1,0:T(8,128)(2,1)} custom-call(bf16[768,8192]{1,0:T(8,128)(2,1)S(1)} %copy-done, bf16[768,512]{1,0:T(8,128)(2,1)S(1)} %get-tuple-element.17.g_ref), custom_call_target="tpu_custom_call" | custom-call | tf_op jit(solution)/shard_map/grad_head/pallas_call | solution.py:289
  (21 shorter events, 3.6 us)
Async XLA Ops:
  7.2 76.1 %all-gather.2.cloned.1.call-start = ((), (), s32[]{:S(2)}) async-start(), calls=%async_computation.5 | async-start | bytes 12976128 | tf_op jit(solution)/shard_map/all_gather | solution.py:322
  83.3 2.0 copy-start.1
  85.3 6.6 %copy-start.3 = (bf16[4608,512]{1,0:T(8,128)(2,1)S(1)}, bf16[4608,512]{1,0:T(8,128)(2,1)}, u32[]{:S(2)}) copy-start(bf16[4608,512]{1,0:T(8,128)(2,1)} %w_ref.5) | copy-start | bytes 14155780
  104.0 1.1 copy-start.4
  106.0 15.7 %all-to-all-start.1 = ((f32[32,24,128]{2,1,0:T(8,128)}), f32[32,24,128]{2,1,0:T(8,128)S(1)}, u32[]{:S(2)}, u32[]{:S(2)}) async-start(f32[32,24,128]{2,1,0:T(8,128)} %broadcast_in_dim.18), calls=%async_computation.1 | async-start | bytes 786432 | tf_op jit(solution)/shard_map/all_to_all | solution.py:336
  122.5 14.7 %all-to-all-start.2 = ((f32[8,24,128]{2,1,0:T(8,128)}), f32[8,24,128]{2,1,0:T(8,128)S(1)}, u32[]{:S(2)}, u32[]{:S(2)}) async-start(f32[8,24,128]{2,1,0:T(8,128)} %merge_stats.1), calls=%async_computation.2 | async-start | bytes 196608 | tf_op jit(solution)/shard_map/all_to_all | solution.py:339
  137.8 2.0 copy-start.2
  139.9 1.4 copy-start.5
  145.1 6.2 %collective-permute-start = (bf16[384,3584]{1,0:T(8,128)(2,1)S(1)}, bf16[384,3584]{1,0:T(8,128)(2,1)S(1)}, u32[]{:S(2)}, u32[]{:S(2)}) collective-permute-start(bf16[384,3584]{1,0:T(8,128)(2,1)S(1)} %get-tuple-element.18), channel_id=1, source_target_pairs={{0,8},{8,0},{16,24},{24,16},{32,40},{40,32},{48,56},{56,48},{64,72... | collective-permute-start | bytes 8257544 | tf_op jit(solution)/shard_map/ppermute | solution.py:343
  196.0 13.8 %all-to-all-start.4 = ((bf16[8,24,448]{2,1,0:T(8,128)(2,1)}), bf16[8,24,448]{2,1,0:T(8,128)(2,1)S(1)}, u32[]{:S(2)}, u32[]{:S(2)}) async-start(bf16[8,24,448]{2,1,0:T(8,128)(2,1)} %copy.12), calls=%async_computation.4 | async-start | bytes 393216 | tf_op jit(solution)/shard_map/all_to_all | solution.py:351
  199.4 4.6 %copy-start = (bf16[768,8192]{1,0:T(8,128)(2,1)S(1)}, bf16[768,8192]{1,0:T(8,128)(2,1)}, u32[]{:S(2)}) copy-start(bf16[768,8192]{1,0:T(8,128)(2,1)} %all-gather.2.cloned.1.call-done.h_ref) | copy-start | bytes 37748740
Sparse Core Ops, SparseCore 0:
  11.1 72.1 all-gather.1

commit v2 on v0

v2 whole, which is shorter than its diff:
```python
import functools

import jax
import jax.numpy as jnp
from jax import lax
from jax.experimental import pallas as pl
from jax.experimental.pallas import tpu as pltpu
from jax.sharding import PartitionSpec as P

loss_scale = 65536.0
MIB = 1 << 20
bf16 = jnp.bfloat16
f32 = jnp.float32


def params(mib=40):
    return pltpu.CompilerParams(
        vmem_limit_bytes=mib * MIB, dimension_semantics=("arbitrary",)
    )


OFFSETS = (0, 3, 1, 2)
SIDE = 4


def shifted(axis, step, shards):
    def to(i):
        x, y, c = i // (2 * SIDE), i // 2 % SIDE, i % 2
        if axis == 0:
            x = (x + step) % SIDE
        else:
            y = (y + step) % SIDE
        return (x * SIDE + y) * 2 + c

    return [(i, to(i)) for i in range(shards)]


def both_ways(block, axis, shards, cut):
    up, down = shifted(axis, 1, shards), shifted(axis, -1, shards)
    before = lax.ppermute(block, "dp", up)
    after = lax.ppermute(block, "dp", down)
    far_left = lax.ppermute(before[:, :cut], "dp", up)
    far_right = lax.ppermute(after[:, cut:], "dp", down)
    return block, before, after, far_left, far_right


def joined(parts):
    block, before, after, far_left, far_right = parts
    return jnp.concatenate([block, before, after, jnp.concatenate([far_left, far_right], axis=1)], axis=0)


def block_start(pos_ref, i, j, first_axis, size):
    x, y = pos_ref[0], pos_ref[1]
    dx, dy = (OFFSETS[j], OFFSETS[i]) if first_axis == 0 else (OFFSETS[i], OFFSETS[j])
    return pl.multiple_of((((x + dx) % SIDE) * SIDE + (y + dy) % SIDE) * size, 16)


def pack_kernel(tok, meta, pos_ref, counts_ref, dest_ref, s_ref, t_ref, keep_ref, send_ref):
    rows, s_half, t_half = s_ref.shape[0], s_ref.shape[1] // 2, t_ref.shape[1] // 2
    core = pos_ref[2]
    lane = lax.broadcasted_iota(jnp.int32, (rows, meta), 1)
    row = lax.broadcasted_iota(jnp.int32, (rows, meta), 0)
    live = jnp.where(row < counts_ref[0], 1, 0)
    dest = jnp.transpose(jnp.broadcast_to(dest_ref[...], (meta, meta)))[:rows, :]
    none = tok * 2 * SIDE * SIDE
    target = jnp.where(row < counts_ref[1], dest, none)
    notes = jnp.where(lane == 0, live, jnp.where(lane == 1, target // 32, target % 32))
    notes = notes.astype(f32).astype(bf16)
    first = core == 0
    for ref, low in ((keep_ref, first), (send_ref, jnp.logical_not(first))):
        ref[:, :s_half] = jnp.where(low, s_ref[:, :s_half], s_ref[:, s_half:])
        ref[:, s_half : s_half + meta] = notes
        ref[:, s_half + meta :] = jnp.where(low, t_ref[:, :t_half], t_ref[:, t_half:])


SMEM = pl.BlockSpec(memory_space=pltpu.SMEM)


def pack(pos, counts, dest, s, t, meta):
    tok = s.shape[0]
    width = s.shape[1] // 2 + meta + t.shape[1] // 2
    vmem = pl.BlockSpec(memory_space=pltpu.VMEM)
    return pl.pallas_call(
        functools.partial(pack_kernel, tok, meta),
        in_specs=[SMEM, SMEM, vmem, vmem, vmem],
        out_shape=[jax.ShapeDtypeStruct((tok, width), bf16)] * 2,
        compiler_params=pltpu.CompilerParams(vmem_limit_bytes=24 * MIB),
        name="pack",
    )(pos, counts, dest, s, t)


def pair_kernel(tok, width, pos_ref, own_ref, got_ref, a_ref, b_ref):
    first = pos_ref[2] == 0
    own, got = own_ref[...].astype(f32), got_ref[...].astype(f32)
    low = jnp.where(first, own, got)
    high = jnp.where(first, got, own)
    both = jnp.concatenate([low, high], axis=0).astype(bf16)
    a_ref[...] = both[:, :width]
    b_ref[...] = both[:, width:]


def pair(pos, own, got, width):
    tok, total = own.shape
    vmem = pl.BlockSpec(memory_space=pltpu.VMEM)
    return pl.pallas_call(
        functools.partial(pair_kernel, tok, width),
        in_specs=[SMEM, vmem, vmem],
        out_shape=[
            jax.ShapeDtypeStruct((2 * tok, width), bf16),
            jax.ShapeDtypeStruct((2 * tok, total - width), bf16),
        ],
        compiler_params=pltpu.CompilerParams(vmem_limit_bytes=24 * MIB),
        name="pair",
    )(pos, own, got)


def near_kernel(depth, pos_ref, p0, p1, p2, own_w, other_w, own_ref, other_ref, rows):
    n = p0.shape[0]
    for i, p in enumerate((p0, p1, p2)):
        rows[i * n : (i + 1) * n, :] = p[:, :depth]
    other_ref[...] = jnp.dot(rows[...], other_w[...], preferred_element_type=f32)
    own_ref[...] = jnp.dot(rows[...], own_w[...], preferred_element_type=f32)


def far_kernel(depth, pos_ref, left, right, own_w, other_w, own_ref, other_ref, rows):
    cut = left.shape[1]
    rows[:, :cut] = left[...]
    rows[:, cut:] = right[:, : depth - cut]
    other_ref[...] = jnp.dot(rows[...], other_w[...], preferred_element_type=f32)
    own_ref[...] = jnp.dot(rows[...], own_w[...], preferred_element_type=f32)


def partial_logits(kernel, name, pos, pieces, own_w, other_w):
    n = pieces[0].shape[0] * (3 if len(pieces) == 3 else 1)
    depth, cols = own_w.shape[0] // 2, own_w.shape[1]
    half = pl.BlockSpec((depth, cols), lambda k, pos: (pos[2], 0))
    whole = lambda shape: pl.BlockSpec(shape, lambda k, pos: (0, 0))
    return pl.pallas_call(
        functools.partial(kernel, depth),
        grid_spec=pltpu.PrefetchScalarGridSpec(
            num_scalar_prefetch=1,
            grid=(1,),
            in_specs=[whole(p.shape) for p in pieces] + [half, half],
            out_specs=[whole((n, cols))] * 2,
            scratch_shapes=[pltpu.VMEM((n, depth), bf16)],
        ),
        out_shape=[jax.ShapeDtypeStruct((n, cols), f32)] * 2,
        compiler_params=params(),
        name=name,
    )(pos, *pieces, own_w, other_w)


def place(out_ref, pos_ref, near, far, first_axis):
    size = near.shape[0] // (3 * SIDE)
    for i in range(SIDE):
        source = near if i < 3 else far
        for j in range(SIDE):
            at = ((i if i < 3 else 0) * SIDE + j) * size
            out_ref[pl.ds(block_start(pos_ref, i, j, first_axis, size), size), :] = source[at : at + size, :]


def student_kernel(pos_ref, near, far, near_got, far_got, m0, m1, m2, m3, s_ref, lse_ref, target_ref, live_ref, notes):
    place(s_ref, pos_ref, near[...] + near_got[...], far[...] + far_got[...], 0)
    size = m0.shape[0] // SIDE
    for i, m in enumerate((m0, m1, m2, m3)):
        note = m[...].astype(f32)
        for j in range(SIDE):
            notes[pl.ds(block_start(pos_ref, i, j, 0, size), size), :] = note[j * size : (j + 1) * size, :]
    flat = jnp.transpose(notes[...])
    target_ref[...] = (flat[1:2, :] * 32.0 + flat[2:3, :]).astype(jnp.int32)
    for j in range(live_ref.shape[0]):
        live_ref[j : j + 1, :] = flat[0:1, j * 128 : (j + 1) * 128]
    s = s_ref[...]
    top = jnp.max(s, axis=1, keepdims=True)
    lse = top + jnp.log(jnp.sum(jnp.exp(s - top), axis=1, keepdims=True))
    lse_ref[...] = jnp.broadcast_to(lse, lse_ref.shape)


def student_logits(pos, near, far, near_got, far_got, pieces, depth, meta):
    cols = near.shape[1]
    rows = near.shape[0] + far.shape[0]
    block, before, after, far_left, far_right = pieces
    at = depth // meta
    size = block.shape[0]
    whole = lambda shape: pl.BlockSpec(shape, lambda k, pos: (0, 0))
    note = pl.BlockSpec((size, meta), lambda k, pos: (0, at))
    last = pl.BlockSpec((size, meta), lambda k, pos: (0, at - far_left.shape[1] // meta))
    return pl.pallas_call(
        student_kernel,
        grid_spec=pltpu.PrefetchScalarGridSpec(
            num_scalar_prefetch=1,
            grid=(1,),
            in_specs=[whole(near.shape), whole(far.shape)] * 2 + [note, note, note, last],
            out_specs=[whole((rows, cols)), whole((rows, 128)), whole((1, rows)), whole((rows // 128, 128))],
            scratch_shapes=[pltpu.VMEM((rows, meta), f32)],
        ),
        out_shape=[
            jax.ShapeDtypeStruct((rows, cols), f32),
            jax.ShapeDtypeStruct((rows, 128), f32),
            jax.ShapeDtypeStruct((1, rows), jnp.int32),
            jax.ShapeDtypeStruct((rows // 128, 128), f32),
        ],
        compiler_params=params(),
        name="student_logits",
    )(pos, near, far, near_got, far_got, block, before, after, far_right)


def teacher_kernel(pos_ref, near, far, near_got, far_got, target_ref, s_ref, lse_ref, t_ref, stat_ref, slots):
    rows, cols = slots.shape
    place(slots, pos_ref, near[...] + near_got[...], far[...] + far_got[...], 1)
    token = lax.broadcasted_iota(jnp.int32, (rows, rows), 0)
    pick = (token == target_ref[...]).astype(f32).astype(bf16)
    value = slots[...]
    high = value.astype(bf16)
    rest = value - high.astype(f32)
    mid = rest.astype(bf16)
    low = (rest - mid.astype(f32)).astype(bf16)
    t = jnp.dot(pick, high, preferred_element_type=f32)
    t += jnp.dot(pick, mid, preferred_element_type=f32)
    t += jnp.dot(pick, low, preferred_element_type=f32)
    t_ref[...] = t
    top = jnp.max(t, axis=1, keepdims=True)
    weight = jnp.exp(t - top)
    total = jnp.sum(weight, axis=1, keepdims=True)
    cross = jnp.sum(weight * (t - s_ref[...]), axis=1, keepdims=True) / total
    lse = top + jnp.log(total)
    lane = lax.broadcasted_iota(jnp.int32, (rows, 128), 1)
    stats = jnp.where(lane == 0, lse_ref[...], jnp.where(lane == 1, lse, cross))
    flat = jnp.transpose(stats)
    n = rows // 128
    copies, used = stat_ref.shape[0], 3 * n
    for i in range(3):
        for j in range(n):
            line = flat[i : i + 1, j * 128 : (j + 1) * 128]
            stat_ref[:, i * n + j, :] = jnp.broadcast_to(line, (copies, 128))
    stat_ref[:, used:, :] = jnp.zeros((copies, stat_ref.shape[1] - used, 128), f32)


def teacher_logits(pos, near, far, near_got, far_got, target, s, lse, copies):
    rows, cols = s.shape
    stat_rows = -(-3 * (rows // 128) // 8) * 8
    whole = lambda shape: pl.BlockSpec(shape, lambda k, pos: (0,) * len(shape))
    return pl.pallas_call(
        teacher_kernel,
        grid_spec=pltpu.PrefetchScalarGridSpec(
            num_scalar_prefetch=1,
            grid=(1,),
            in_specs=[whole(near.shape), whole(far.shape)] * 2
            + [whole((1, rows)), whole((rows, cols)), whole((rows, 128))],
            out_specs=[whole((rows, cols)), whole((copies, stat_rows, 128))],
            scratch_shapes=[pltpu.VMEM((rows, cols), f32)],
        ),
        out_shape=[
            jax.ShapeDtypeStruct((rows, cols), f32),
            jax.ShapeDtypeStruct((copies, stat_rows, 128), f32),
        ],
        compiler_params=params(),
        name="teacher_logits",
    )(pos, near, far, near_got, far_got, target, s, lse)


def merged(x, n):
    student, teacher, cross = x[:, 0:n], x[:, n : 2 * n], x[:, 2 * n : 3 * n]
    s_top = jnp.max(student, axis=0)
    s_norm = s_top + jnp.log(jnp.sum(jnp.exp(student - s_top[None]), axis=0))
    t_top = jnp.max(teacher, axis=0)
    weight = jnp.exp(teacher - t_top[None])
    total = jnp.sum(weight, axis=0)
    return s_norm, t_top + jnp.log(total), jnp.sum(weight * cross, axis=0) / total


def merge_kernel(n, x_ref, out_ref):
    s_norm, t_norm, cross = merged(x_ref[...], n)
    out_ref[:, 0:n] = jnp.broadcast_to(s_norm[None], (out_ref.shape[0],) + s_norm.shape)
    out_ref[:, n : 2 * n] = jnp.broadcast_to(t_norm[None], (out_ref.shape[0],) + s_norm.shape)
    out_ref[:, 2 * n : 3 * n] = jnp.broadcast_to(cross[None], (out_ref.shape[0],) + s_norm.shape)
    rest = out_ref.shape[1] - 3 * n
    out_ref[:, 3 * n :] = jnp.zeros((out_ref.shape[0], rest, 128), f32)


def merge(x, n, copies):
    return pl.pallas_call(
        functools.partial(merge_kernel, n),
        out_shape=jax.ShapeDtypeStruct((copies,) + x.shape[1:], f32),
        compiler_params=pltpu.CompilerParams(vmem_limit_bytes=24 * MIB),
        name="merge_stats",
    )(x)


def norm_kernel(n, live_total, x_ref, live_ref, norm_ref, loss_ref):
    s_norm, t_norm, cross = merged(x_ref[...], n)
    live = live_ref[...] > 0
    term = jnp.where(live, cross - t_norm + s_norm, 0.0)
    loss_ref[...] = jnp.sum(term, keepdims=True) / live_total
    norm_ref[0:n, :] = jnp.where(live, s_norm, jnp.inf)
    norm_ref[n : 2 * n, :] = jnp.where(live, t_norm, jnp.inf)


def norms(x, live, n, live_total):
    return pl.pallas_call(
        functools.partial(norm_kernel, n, live_total),
        out_shape=[
            jax.ShapeDtypeStruct((2 * n, 128), f32),
            jax.ShapeDtypeStruct((1, 1), f32),
        ],
        compiler_params=pltpu.CompilerParams(vmem_limit_bytes=24 * MIB),
        name="norms",
    )(x, live)


def column(norm_ref, first, n):
    return jnp.concatenate(
        [
            jnp.transpose(jnp.broadcast_to(norm_ref[first + j : first + j + 1, :], (128, 128)))[:, 0:1]
            for j in range(n)
        ],
        axis=0,
    )


def gap_kernel(grad_scale, tok, pos_ref, s_ref, t_ref, norm_ref, send_ref, keep_ref, piece_ref, full, part):
    rows = s_ref.shape[0]
    n = rows // 128
    gap = jnp.exp(s_ref[...] - column(norm_ref, 0, n)) - jnp.exp(t_ref[...] - column(norm_ref, n, n))
    full[...] = gap * grad_scale
    core = pos_ref[2]
    for ref, c in ((send_ref, 1 - core), (keep_ref, core)):
        for j in range(rows // (2 * tok)):
            start = pl.multiple_of(2 * tok * j + tok * c, 8)
            part[tok * j : tok * (j + 1), :] = full[pl.ds(start, tok), :]
        ref[...] = part[...].astype(bf16)
    size = 2 * tok
    for i in range(SIDE):
        for j in range(SIDE):
            at = (i * SIDE + j) * size
            piece_ref[at : at + size, :] = full[
                pl.ds(block_start(pos_ref, i, j, 0, size), size), :
            ].astype(bf16)


def logit_gap(pos, s, t, norm, grad_scale, tok):
    rows, cols = s.shape
    vmem = pl.BlockSpec(memory_space=pltpu.VMEM)
    return pl.pallas_call(
        functools.partial(gap_kernel, grad_scale, tok),
        in_specs=[SMEM, vmem, vmem, vmem],
        out_shape=[
            jax.ShapeDtypeStruct((rows // 2, cols), bf16),
            jax.ShapeDtypeStruct((rows // 2, cols), bf16),
            jax.ShapeDtypeStruct((rows, cols), bf16),
        ],
        scratch_shapes=[pltpu.VMEM((rows, cols), f32), pltpu.VMEM((rows // 2, cols), f32)],
        compiler_params=pltpu.CompilerParams(vmem_limit_bytes=40 * MIB),
        name="logit_gap",
    )(pos, s, t, norm)


def hidden_kernel(keep_ref, got_ref, own_w, other_w, out_ref):
    turned = (((1,), (1,)), ((), ()))
    out_ref[...] = (
        lax.dot_general(keep_ref[...], own_w[...], turned, preferred_element_type=f32)
        + lax.dot_general(got_ref[...], other_w[...], turned, preferred_element_type=f32)
    ).astype(bf16)


def grad_hidden_of(keep, got, own_w, other_w, chunks):
    rows, cols = keep.shape
    depth = own_w.shape[0]
    kb = depth // chunks
    whole = pl.BlockSpec((rows, cols), lambda k: (0, 0))
    head = pl.BlockSpec((kb, cols), lambda k: (k, 0))
    return pl.pallas_call(
        hidden_kernel,
        grid=(chunks,),
        in_specs=[whole, whole, head, head],
        out_specs=pl.BlockSpec((rows, kb), lambda k: (0, k)),
        out_shape=jax.ShapeDtypeStruct((rows, depth), bf16),
        compiler_params=params(),
        name="grad_hidden",
    )(keep, got, own_w, other_w)


def head_kernel(pos_ref, a0, a1, a2, a3, a4, b0, b1, b2, b3, b4, g_ref, out_ref, rows):
    depth, size = rows.shape[1], a0.shape[0]
    low = (pl.program_id(0) == pos_ref[2]).astype(jnp.int32)

    def fill(pieces):
        block, before, after, left, right = pieces
        cut = left.shape[1]
        for i, p in enumerate((block, before, after)):
            rows[i * size : (i + 1) * size, :] = p[:, :depth]
        rows[3 * size :, :cut] = left[...]
        rows[3 * size :, cut:] = right[:, : depth - cut]

    @pl.when(low == 1)
    def _():
        fill((a0, a1, a2, a3, a4))

    @pl.when(low == 0)
    def _():
        fill((b0, b1, b2, b3, b4))

    out_ref[...] = lax.dot_general(
        rows[...], g_ref[...], (((0,), (0,)), ((), ())), preferred_element_type=f32
    ).astype(bf16)


def grad_head_of(pos, own, other, g, depth):
    rows, cols = g.shape
    whole = lambda shape: pl.BlockSpec(shape, lambda k, pos: (0, 0))
    return pl.pallas_call(
        head_kernel,
        grid_spec=pltpu.PrefetchScalarGridSpec(
            num_scalar_prefetch=1,
            grid=(2,),
            in_specs=[whole(p.shape) for p in own + other] + [whole((rows, cols))],
            out_specs=pl.BlockSpec((depth, cols), lambda k, pos: (k, 0)),
            scratch_shapes=[pltpu.VMEM((rows, depth), bf16)],
        ),
        out_shape=jax.ShapeDtypeStruct((2 * depth, cols), bf16),
        compiler_params=params(),
        name="grad_head",
    )(pos, *own, *other, g)


def per_device(
    student_hidden,
    teacher_hidden,
    student_head,
    teacher_head,
    live_count,
    teacher_count,
    teacher_dest,
):
    tok, depth = student_hidden.shape
    shards, slices = lax.axis_size("dp"), lax.axis_size("vocab")
    rows = tok * shards
    live_total = rows // 2
    n = rows // 128
    meta = 128
    s_half = depth // 2
    s_width, t_width = s_half + meta, teacher_hidden.shape[1] // 2
    index = lax.axis_index("dp").astype(jnp.int32)
    pos = jnp.stack([index // (2 * SIDE), index // 2 % SIDE, index % 2])
    swap = [(i, i ^ 1) for i in range(shards)]
    other = lambda v: lax.ppermute(v, "dp", swap)
    same_core = [list(range(c, shards, 2)) for c in range(2)]

    counts = jnp.concatenate([live_count, teacher_count])
    dest = jnp.pad(teacher_dest, (0, 128 - tok)).reshape(1, 128)
    keep, send = pack(pos, counts, dest, student_hidden, teacher_hidden, meta)
    a, b = pair(pos, keep, other(send), s_width)
    student_other, teacher_other = other(student_head), other(teacher_head)
    a = both_ways(a, 0, shards, s_width // 256 * 128 + 128)
    b = both_ways(b, 1, shards, t_width // 2)
    a = both_ways(joined(a), 1, shards, s_width // 256 * 128 + 128)
    b = both_ways(joined(b), 0, shards, t_width // 2)

    s_near, s_send = partial_logits(near_kernel, "student_near", pos, a[:3], student_head, student_other)
    t_near, t_send = partial_logits(near_kernel, "teacher_near", pos, b[:3], teacher_head, teacher_other)
    s_near_got, t_near_got = other(s_send), other(t_send)
    s_far, s_send = partial_logits(far_kernel, "student_far", pos, a[3:], student_head, student_other)
    s_far_got = other(s_send)
    s, s_lse, target, live = student_logits(
        pos, s_near, s_far, s_near_got, s_far_got, a, s_half, meta
    )
    t_far, t_send = partial_logits(far_kernel, "teacher_far", pos, b[3:], teacher_head, teacher_other)
    t_far_got = other(t_send)
    t, stats = teacher_logits(pos, t_near, t_far, t_near_got, t_far_got, target, s, s_lse, shards)

    stats = lax.all_to_all(stats, "dp", 0, 0)
    stats = lax.all_to_all(merge(stats, n, slices), "vocab", 0, 0)
    norm, loss = norms(stats, live, n, live_total)

    send, keep, piece = logit_gap(pos, s, t, norm, loss_scale / live_total, tok)
    mine = grad_hidden_of(keep, other(send), student_head, student_other, 7)
    parts = lax.all_to_all(
        mine.reshape(shards // 2, tok, depth), "dp", 0, 0, axis_index_groups=same_core
    )
    a_other = tuple(other(p) for p in a)
    grad_head = grad_head_of(pos, a, a_other, piece, s_half)
    part = jnp.sum(parts.astype(f32), axis=0).astype(bf16)
    part = part.reshape(tok, slices, depth // slices).transpose(1, 0, 2)
    parts = lax.all_to_all(part, "vocab", 0, 0)
    grad_hidden = jnp.sum(parts.astype(f32), axis=0).astype(bf16)
    return (loss[0, 0], grad_hidden, grad_head)


def solution(mesh):
    return jax.shard_map(
        per_device,
        mesh=mesh,
        in_specs=(
            P("dp", None),
            P("dp", None),
            P(None, ("dp", "vocab")),
            P(None, ("dp", "vocab")),
            P("dp"),
            P("dp"),
            P("dp"),
        ),
        out_specs=(P(), P("dp", "vocab"), P(None, ("dp", "vocab"))),
        check_vma=False,
    )
```

time: 474 us -> 223 us (0.47)
  the two profiles are of different devices: /device:TPU:1 before, /device:TPU:28 now
where the time goes in v2:
time: 223 us
  waiting for transfers between devices  106 us (48%)
  Pallas kernels  41.7 us (19%)
  starting transfers between devices  31.3 us (14%)
  blocking collectives  30.6 us (14%)
  local copies, waits for them, and re-layouts  6.63 us (3%)
  other arithmetic  3.79 us (2%)
  between operations  2.26 us (1%)
    all_to_all x1, waiting for transfers between devices, per_device(): lax.all_to_all(mine.reshape(shards // 2, tok, depth), 'dp', 0, 0, axis_in...  39.1 us
    ppermute x4, waiting for transfers between devices, both_ways(): far_left = lax.ppermute(before[:, :cut], 'dp', up)  22.1 us
    ppermute x4, waiting for transfers between devices, both_ways(): after = lax.ppermute(block, 'dp', down)  17.4 us
    all_to_all x1, blocking collectives, per_device(): stats = lax.all_to_all(merge(stats, n, slices), 'vocab', 0, 0)  16.8 us
    pallas_call x4, Pallas kernels, partial_logits(): pl.pallas_call(functools.partial(kernel, depth), grid_spec=pltpu.Prefetch...  15.7 us
    all_to_all x1, blocking collectives, per_device(): stats = lax.all_to_all(stats, 'dp', 0, 0)  13.8 us
    ppermute x4, waiting for transfers between devices, both_ways(): far_right = lax.ppermute(after[:, cut:], 'dp', down)  11.8 us
    ppermute x4, waiting for transfers between devices, both_ways(): before = lax.ppermute(block, 'dp', up)  9.12 us
  transfers between devices with their start and end apart: 31, of which 12 were waited for; matrix products, arithmetic and copies ran while one was open for 3% of the time, Pallas kernels for 12%

profile of v2, /device:TPU:28, one launch (start us, length us, event | category | flops | bytes accessed | tf_op | source)
XLA Modules:
  0.0 222.6 jit_solution(5666324566228390783)
XLA Ops:
  6.0 3.2 %collective-permute-done.got_ref = bf16[24,4224]{1,0:T(8,128)(2,1)S(1)} collective-permute-done((bf16[24,4224]{1,0:T(8,128)(2,1)S(1)}, bf16[24,4224]{1,0:T(8,128)(2,1)S(1)}, u32[]{:S(2)}, u32[]{:S(2)}) %collective-permute-start) | collective-permute-done | bytes 202784 | tf_op jit(solution)/shard_map/ppermute | solution.py:446
  12.0 4.7 %collective-permute-done.12 = bf16[48,1920]{1,0:T(8,128)(2,1)S(1)} collective-permute-done((bf16[48,1920]{1,0:T(8,128)(2,1)S(1)}, bf16[48,1920]{1,0:T(8,128)(2,1)S(1)}, u32[]{:S(2)}, u32[]{:S(2)}) %collective-permute-start.12) | collective-permute-done | bytes 184352 | tf_op jit(solution)/shard_map/ppermute | solution.py:40
  19.6 2.9 %collective-permute-done.15 = bf16[48,896]{1,0:T(8,128)(2,1)S(1)} collective-permute-done((bf16[48,896]{1,0:T(8,128)(2,1)S(1)}, bf16[48,896]{1,0:T(8,128)(2,1)S(1)}, u32[]{:S(2)}, u32[]{:S(2)}) %collective-permute-start.15) | collective-permute-done | bytes 86048 | tf_op jit(solution)/shard_map/ppermute | solution.py:43
  26.4 4.5 %collective-permute-done.1 = bf16[48,2304]{1,0:T(8,128)(2,1)S(1)} collective-permute-done((bf16[48,2304]{1,0:T(8,128)(2,1)S(1)}, bf16[48,2304]{1,0:T(8,128)(2,1)S(1)}, u32[]{:S(2)}, u32[]{:S(2)}) %collective-permute-start.1) | collective-permute-done | bytes 221216 | tf_op jit(solution)/shard_map/ppermute | solution.py:40
  30.9 2.9 %collective-permute-start.3 = (bf16[48,1152]{1,0:T(8,128)(2,1)S(1)}, bf16[48,1152]{1,0:T(8,128)(2,1)S(1)}, u32[]{:S(2)}, u32[]{:S(2)}) collective-permute-start(bf16[48,1152]{1,0:T(8,128)(2,1)S(1)} %slice.32), channel_id=1, source_target_pairs={{0,16},{8,24},{16,32},{24,40},{32,48},{40,56},{48,0},{56,8},{64,80... | collective-permute-start | bytes 331784 | tf_op jit(solution)/shard_map/ppermute | solution.py:42
  33.8 12.4 %collective-permute-done.3 = bf16[48,1152]{1,0:T(8,128)(2,1)S(1)} collective-permute-done((bf16[48,1152]{1,0:T(8,128)(2,1)S(1)}, bf16[48,1152]{1,0:T(8,128)(2,1)S(1)}, u32[]{:S(2)}, u32[]{:S(2)}) %collective-permute-start.3) | collective-permute-done | bytes 110624 | tf_op jit(solution)/shard_map/ppermute | solution.py:42
  46.2 2.7 %collective-permute-start.5 = (bf16[192,2304]{1,0:T(8,128)(2,1)S(1)}, bf16[192,2304]{1,0:T(8,128)(2,1)S(1)}, u32[]{:S(2)}, u32[]{:S(2)}) collective-permute-start(bf16[192,2304]{1,0:T(8,128)(2,1)S(1)} %maximum_maximum_fusion.p0), channel_id=1, source_target_pairs={{0,64},{8,72},{16,80},{24,88},{32,96},{40,104},{48,112},{56,120},{... | collective-permute-start | bytes 2654216 | tf_op jit(solution)/shard_map/ppermute | solution.py:40
  49.7 15.8 %collective-permute-done.17.p2.m2.a2 = bf16[192,1920]{1,0:T(8,128)(2,1)S(1)} collective-permute-done((bf16[192,1920]{1,0:T(8,128)(2,1)S(1)}, bf16[192,1920]{1,0:T(8,128)(2,1)S(1)}, u32[]{:S(2)}, u32[]{:S(2)}) %collective-permute-start.17) | collective-permute-done | bytes 737312 | tf_op jit(solution)/shard_map/ppermute | solution.py:41
  65.4 4.3 %student_near.1 = (f32[576,512]{1,0:T(8,128)S(1)}, f32[576,512]{1,0:T(8,128)}) custom-call(s32[3]{0:T(128)S(1)} %pad_add_fusion.pos_ref, bf16[192,1920]{1,0:T(8,128)(2,1)S(1)} %maximum_maximum_fusion.1.p0.m0.a0, bf16[192,1920]{1,0:T(8,128)(2,1)S(1)} %collective-permute-done.16.p1.m1.a1, bf16[192,1920]{1,0:T(8,128)(2,1)S(1)} %collective-permute-done.17.p2.m2.a2, ...), custom_call_target="tpu_custom_call" | custom-call | tf_op jit(solution)/shard_map/student_near/pallas_call | solution.py:138
  69.9 5.1 %teacher_near.1 = (f32[576,512]{1,0:T(8,128)S(1)}, f32[576,512]{1,0:T(8,128)}) custom-call(s32[3]{0:T(128)S(1)} %pad_add_fusion.pos_ref, bf16[192,2304]{1,0:T(8,128)(2,1)S(1)} %maximum_maximum_fusion.p0, bf16[192,2304]{1,0:T(8,128)(2,1)S(1)} %collective-permute-done.5.p1, bf16[192,2304]{1,0:T(8,128)(2,1)S(1)} %collective-permute-done.6.p2, ...), custom_call_target="tpu_custom_call" | custom-call | tf_op jit(solution)/shard_map/teacher_near/pallas_call | solution.py:138
  78.0 8.9 %collective-permute-done.20.right.m3.a4 = bf16[192,896]{1,0:T(8,128)(2,1)S(1)} collective-permute-done((bf16[192,896]{1,0:T(8,128)(2,1)S(1)}, bf16[192,896]{1,0:T(8,128)(2,1)S(1)}, u32[]{:S(2)}, u32[]{:S(2)}) %collective-permute-start.20) | collective-permute-done | bytes 344096 | tf_op jit(solution)/shard_map/ppermute | solution.py:43
  87.5 9.7 %collective-permute-done.19.left.a3 = bf16[192,1024]{1,0:T(8,128)(2,1)S(1)} collective-permute-done((bf16[192,1024]{1,0:T(8,128)(2,1)S(1)}, bf16[192,1024]{1,0:T(8,128)(2,1)S(1)}, u32[]{:S(2)}, u32[]{:S(2)}) %collective-permute-start.19) | collective-permute-done | bytes 393248 | tf_op jit(solution)/shard_map/ppermute | solution.py:42
  97.1 2.9 %student_far.1 = (f32[192,512]{1,0:T(8,128)S(1)}, f32[192,512]{1,0:T(8,128)S(1)}) custom-call(s32[3]{0:T(128)S(1)} %pad_add_fusion.pos_ref, bf16[192,1024]{1,0:T(8,128)(2,1)S(1)} %collective-permute-done.19.left.a3, bf16[192,896]{1,0:T(8,128)(2,1)S(1)} %collective-permute-done.20.right.m3.a4, bf16[3584,512]{1,0:T(8,128)(2,1)S(1)} %copy-done, ...), custom_call_target="tpu_custom_call" | custom-call | tf_op jit(solution)/shard_map/student_far/pallas_call | solution.py:138
  100.2 3.3 %teacher_far.1 = (f32[192,512]{1,0:T(8,128)S(1)}, f32[192,512]{1,0:T(8,128)S(1)}) custom-call(s32[3]{0:T(128)S(1)} %pad_add_fusion.pos_ref, bf16[192,1152]{1,0:T(8,128)(2,1)S(1)} %collective-permute-done.8.left, bf16[192,1152]{1,0:T(8,128)(2,1)S(1)} %collective-permute-done.9.right, bf16[4608,512]{1,0:T(8,128)(2,1)S(1)} %bitcast.9, ...), custom_call_target="tpu_custom_call" | custom-call | tf_op jit(solution)/shard_map/teacher_far/pallas_call | solution.py:138
  104.3 2.5 %student_logits.1 = (f32[768,512]{1,0:T(8,128)S(1)}, f32[768,128]{1,0:T(8,128)S(1)}, s32[1,768]{1,0:T(1,128)S(1)}, f32[6,128]{1,0:T(8,128)S(1)}) custom-call(s32[3]{0:T(128)S(1)} %pad_add_fusion.pos_ref, f32[576,512]{1,0:T(8,128)S(1)} %get-tuple-element.34.near, f32[192,512]{1,0:T(8,128)S(1)} %get-tuple-element.35.far, ...), custom_call_target="tpu_custom_call" | custom-call | tf_op jit(solution)/shard_map/student_logits/pallas_call | solution.py:188
  106.9 5.0 %teacher_logits.1 = (f32[768,512]{1,0:T(8,128)S(1)}, f32[32,24,128]{2,1,0:T(8,128)S(1)}) custom-call(s32[3]{0:T(128)S(1)} %pad_add_fusion.pos_ref, f32[576,512]{1,0:T(8,128)S(1)} %get-tuple-element.29.near, f32[192,512]{1,0:T(8,128)S(1)} %get-tuple-element.30.far, f32[576,512]{1,0:T(8,128)} %collective-permute-done.10.near_got, ...), custom_call_target="tpu_custom_call" | custom-call | tf_op jit(solution)/shard_map/teacher_logits/pallas_call | solution.py:243
  111.9 13.8 %all_to_all.20.x_ref = f32[32,24,128]{2,1,0:T(8,128)S(1)} all-to-all(f32[32,24,128]{2,1,0:T(8,128)S(1)} %get-tuple-element.41), channel_id=1, replica_groups=mesh['dp'=32,'vocab'=8] {'dp'}, dimensions={0} | all-to-all | bytes 786432 | tf_op jit(solution)/shard_map/all_to_all | solution.py:471
  125.9 16.8 %all_to_all.21.x_ref = f32[8,24,128]{2,1,0:T(8,128)S(1)} all-to-all(f32[8,24,128]{2,1,0:T(8,128)S(1)} %merge_stats.1), channel_id=1, replica_groups=mesh['dp'=32,'vocab'=8] {'vocab'}, dimensions={0} | all-to-all | bytes 196608 | tf_op jit(solution)/shard_map/all_to_all | solution.py:472
  147.4 7.8 %grad_hidden.1 = bf16[384,3584]{1,0:T(8,128)(2,1)} custom-call(bf16[384,512]{1,0:T(8,128)(2,1)S(1)} %get-tuple-element.46.keep_ref, bf16[384,512]{1,0:T(8,128)(2,1)S(1)} %collective-permute-done.23.got_ref, bf16[3584,512]{1,0:T(8,128)(2,1)S(1)} %copy-done, bf16[3584,512]{1,0:T(8,128)(2,1)} %collective-permute-done.18.other_w), custom_call_target="tpu_custom_call" | custom-call | tf_op jit(solution)/shard_map/grad_hidden/pallas_call | solution.py:372
  155.2 8.2 %all-to-all-start.2 = ((bf16[16,24,3584]{2,1,0:T(8,128)(2,1)}), bf16[16,24,3584]{2,1,0:T(8,128)(2,1)}, u32[]{:S(2)}, u32[]{:S(2)}) async-start(bf16[16,24,3584]{2,1,0:T(8,128)(2,1)} %bitcast.5), calls=%async_computation.2 | async-start | bytes 5505024 | tf_op jit(solution)/shard_map/all_to_all | solution.py:477
  164.6 39.1 %all-to-all-done.2 = bf16[16,24,3584]{2,1,0:T(8,128)(2,1)} async-done(((bf16[16,24,3584]{2,1,0:T(8,128)(2,1)}), bf16[16,24,3584]{2,1,0:T(8,128)(2,1)}, u32[]{:S(2)}, u32[]{:S(2)}) %all-to-all-start.2) | async-done | bytes 2752544 | tf_op jit(solution)/shard_map/all_to_all | solution.py:477
  203.7 2.9 %reduce_sum.24 = bf16[24,3584]{1,0:T(8,128)(2,1)} reduce(bf16[16,24,3584]{2,1,0:T(8,128)(2,1)} %all-to-all-done.2, bf16[]{:T(256)} %constant.54.clone.1), dimensions={0}, to_apply=%region_0.1 | reduce | flops 1290240 | bytes 2924546 | tf_op jit(solution)/shard_map/reduce_sum | solution.py:482
  208.4 3.4 %all-to-all-start.3 = ((bf16[8,24,448]{2,1,0:T(8,128)(2,1)}), bf16[8,24,448]{2,1,0:T(8,128)(2,1)S(1)}, u32[]{:S(2)}, u32[]{:S(2)}) async-start(bf16[8,24,448]{2,1,0:T(8,128)(2,1)} %copy.10), calls=%async_computation.3 | async-start | bytes 393216 | tf_op jit(solution)/shard_map/all_to_all | solution.py:484
  213.0 7.1 %grad_head.1 = bf16[3584,512]{1,0:T(8,128)(2,1)} custom-call(s32[3]{0:T(128)S(1)} %pad_add_fusion.pos_ref, bf16[192,1920]{1,0:T(8,128)(2,1)S(1)} %maximum_maximum_fusion.1.p0.m0.a0, bf16[192,1920]{1,0:T(8,128)(2,1)S(1)} %collective-permute-done.16.p1.m1.a1, bf16[192,1920]{1,0:T(8,128)(2,1)S(1)} %collective-permute-done.17.p2.m2.a2, ...), custom_call_target="tpu_custom_call" | custom-call | tf_op jit(solution)/shard_map/grad_head/pallas_call | solution.py:411
  (85 shorter events, 30.5 us)
Async XLA Ops:
  0.6 69.3 %collective-permute-start.7 = (bf16[4608,512]{1,0:T(8,128)(2,1)}, bf16[4608,512]{1,0:T(8,128)(2,1)}, u32[]{:S(2)}, u32[]{:S(2)}) collective-permute-start(bf16[4608,512]{1,0:T(8,128)(2,1)} %own_w.6), channel_id=1, source_target_pairs={{0,8},{8,0},{16,24},{24,16},{32,40},{40,32},{48,56},{56,48},{64,72... | collective-permute-start | bytes 14155784 | tf_op jit(solution)/shard_map/ppermute | solution.py:446
  0.7 64.7 %collective-permute-start.18 = (bf16[3584,512]{1,0:T(8,128)(2,1)}, bf16[3584,512]{1,0:T(8,128)(2,1)}, u32[]{:S(2)}, u32[]{:S(2)}) collective-permute-start(bf16[3584,512]{1,0:T(8,128)(2,1)} %own_w.9), channel_id=1, source_target_pairs={{0,8},{8,0},{16,24},{24,16},{32,40},{40,32},{48,56},{56,48},{64,72... | collective-permute-start | bytes 11010056 | tf_op jit(solution)/shard_map/ppermute | solution.py:446
  16.6 7.5 %collective-permute-start.14 = (bf16[48,1024]{1,0:T(8,128)(2,1)S(1)}, bf16[48,1024]{1,0:T(8,128)(2,1)S(1)}, u32[]{:S(2)}, u32[]{:S(2)}) collective-permute-start(bf16[48,1024]{1,0:T(8,128)(2,1)S(1)} %slice.36), channel_id=1, source_target_pairs={{0,64},{8,72},{16,80},{24,88},{32,96},{40,104},{48,112},{56,120},{... | collective-permute-start | bytes 294920 | tf_op jit(solution)/shard_map/ppermute | solution.py:42
  18.8 7.3 %collective-permute-start.2 = (bf16[48,2304]{1,0:T(8,128)(2,1)S(1)}, bf16[48,2304]{1,0:T(8,128)(2,1)S(1)}, u32[]{:S(2)}, u32[]{:S(2)}) collective-permute-start(bf16[48,2304]{1,0:T(8,128)(2,1)S(1)} %get-tuple-element.28), channel_id=1, source_target_pairs={{0,48},{8,56},{16,0},{24,8},{32,16},{40,24},{48,32},{56,40},{64,11... | collective-permute-start | bytes 663560 | tf_op jit(solution)/shard_map/ppermute | solution.py:41
  22.5 8.4 %collective-permute-start.1 = (bf16[48,2304]{1,0:T(8,128)(2,1)S(1)}, bf16[48,2304]{1,0:T(8,128)(2,1)S(1)}, u32[]{:S(2)}, u32[]{:S(2)}) collective-permute-start(bf16[48,2304]{1,0:T(8,128)(2,1)S(1)} %get-tuple-element.28), channel_id=1, source_target_pairs={{0,16},{8,24},{16,32},{24,40},{32,48},{40,56},{48,0},{56,8},{64,80... | collective-permute-start | bytes 663560 | tf_op jit(solution)/shard_map/ppermute | solution.py:40
  24.2 24.7 %collective-permute-start.16 = (bf16[192,1920]{1,0:T(8,128)(2,1)S(1)}, bf16[192,1920]{1,0:T(8,128)(2,1)S(1)}, u32[]{:S(2)}, u32[]{:S(2)}) collective-permute-start(bf16[192,1920]{1,0:T(8,128)(2,1)S(1)} %maximum_maximum_fusion.1.p0.m0.a0), channel_id=1, source_target_pairs={{0,16},{8,24},{16,32},{24,40},{32,48},{40,56},{48,0},{56,8},{64,80... | collective-permute-start | bytes 2211848 | tf_op jit(solution)/shard_map/ppermute | solution.py:40
  26.1 7.6 %collective-permute-start.4 = (bf16[48,1152]{1,0:T(8,128)(2,1)S(1)}, bf16[48,1152]{1,0:T(8,128)(2,1)S(1)}, u32[]{:S(2)}, u32[]{:S(2)}) collective-permute-start(bf16[48,1152]{1,0:T(8,128)(2,1)S(1)} %slice.33), channel_id=1, source_target_pairs={{0,48},{8,56},{16,0},{24,8},{32,16},{40,24},{48,32},{56,40},{64,11... | collective-permute-start | bytes 331784 | tf_op jit(solution)/shard_map/ppermute | solution.py:43
  30.9 15.3 %collective-permute-start.3 = (bf16[48,1152]{1,0:T(8,128)(2,1)S(1)}, bf16[48,1152]{1,0:T(8,128)(2,1)S(1)}, u32[]{:S(2)}, u32[]{:S(2)}) collective-permute-start(bf16[48,1152]{1,0:T(8,128)(2,1)S(1)} %slice.32), channel_id=1, source_target_pairs={{0,16},{8,24},{16,32},{24,40},{32,48},{40,56},{48,0},{56,8},{64,80... | collective-permute-start | bytes 331784 | tf_op jit(solution)/shard_map/ppermute | solution.py:42
  46.2 23.6 %collective-permute-start.5 = (bf16[192,2304]{1,0:T(8,128)(2,1)S(1)}, bf16[192,2304]{1,0:T(8,128)(2,1)S(1)}, u32[]{:S(2)}, u32[]{:S(2)}) collective-permute-start(bf16[192,2304]{1,0:T(8,128)(2,1)S(1)} %maximum_maximum_fusion.p0), channel_id=1, source_target_pairs={{0,64},{8,72},{16,80},{24,88},{32,96},{40,104},{48,112},{56,120},{... | collective-permute-start | bytes 2654216 | tf_op jit(solution)/shard_map/ppermute | solution.py:40
  48.9 21.0 %collective-permute-start.6 = (bf16[192,2304]{1,0:T(8,128)(2,1)S(1)}, bf16[192,2304]{1,0:T(8,128)(2,1)S(1)}, u32[]{:S(2)}, u32[]{:S(2)}) collective-permute-start(bf16[192,2304]{1,0:T(8,128)(2,1)S(1)} %maximum_maximum_fusion.p0), channel_id=1, source_target_pairs={{0,192},{8,200},{16,208},{24,216},{32,224},{40,232},{48,240},{56,2... | collective-permute-start | bytes 2654216 | tf_op jit(solution)/shard_map/ppermute | solution.py:41
  48.9 16.5 %collective-permute-start.17 = (bf16[192,1920]{1,0:T(8,128)(2,1)S(1)}, bf16[192,1920]{1,0:T(8,128)(2,1)S(1)}, u32[]{:S(2)}, u32[]{:S(2)}) collective-permute-start(bf16[192,1920]{1,0:T(8,128)(2,1)S(1)} %maximum_maximum_fusion.1.p0.m0.a0), channel_id=1, source_target_pairs={{0,48},{8,56},{16,0},{24,8},{32,16},{40,24},{48,32},{56,40},{64,11... | collective-permute-start | bytes 2211848 | tf_op jit(solution)/shard_map/ppermute | solution.py:41
  69.8 34.6 %collective-permute-start.21 = (f32[576,512]{1,0:T(8,128)}, f32[576,512]{1,0:T(8,128)}, u32[]{:S(2)}, u32[]{:S(2)}) collective-permute-start(f32[576,512]{1,0:T(8,128)} %get-tuple-element.36), channel_id=1, source_target_pairs={{0,8},{8,0},{16,24},{24,16},{32,40},{40,32},{48,56},{56,48},{64,72... | collective-permute-start | bytes 3538952 | tf_op jit(solution)/shard_map/ppermute | solution.py:446
  75.0 31.8 %collective-permute-start.10 = (f32[576,512]{1,0:T(8,128)}, f32[576,512]{1,0:T(8,128)}, u32[]{:S(2)}, u32[]{:S(2)}) collective-permute-start(f32[576,512]{1,0:T(8,128)} %get-tuple-element.31), channel_id=1, source_target_pairs={{0,8},{8,0},{16,24},{24,16},{32,40},{40,32},{48,56},{56,48},{64,72... | collective-permute-start | bytes 3538952 | tf_op jit(solution)/shard_map/ppermute | solution.py:446
  75.6 11.3 %collective-permute-start.20 = (bf16[192,896]{1,0:T(8,128)(2,1)S(1)}, bf16[192,896]{1,0:T(8,128)(2,1)S(1)}, u32[]{:S(2)}, u32[]{:S(2)}) collective-permute-start(bf16[192,896]{1,0:T(8,128)(2,1)S(1)} %slice.39), channel_id=1, source_target_pairs={{0,48},{8,56},{16,0},{24,8},{32,16},{40,24},{48,32},{56,40},{64,11... | collective-permute-start | bytes 1032200 | tf_op jit(solution)/shard_map/ppermute | solution.py:43
  75.8 24.4 %collective-permute-start.8 = (bf16[192,1152]{1,0:T(8,128)(2,1)S(1)}, bf16[192,1152]{1,0:T(8,128)(2,1)S(1)}, u32[]{:S(2)}, u32[]{:S(2)}) collective-permute-start(bf16[192,1152]{1,0:T(8,128)(2,1)S(1)} %slice.34), channel_id=1, source_target_pairs={{0,64},{8,72},{16,80},{24,88},{32,96},{40,104},{48,112},{56,120},{... | collective-permute-start | bytes 1327112 | tf_op jit(solution)/shard_map/ppermute | solution.py:42
  77.6 22.6 %collective-permute-start.9 = (bf16[192,1152]{1,0:T(8,128)(2,1)S(1)}, bf16[192,1152]{1,0:T(8,128)(2,1)S(1)}, u32[]{:S(2)}, u32[]{:S(2)}) collective-permute-start(bf16[192,1152]{1,0:T(8,128)(2,1)S(1)} %slice.35), channel_id=1, source_target_pairs={{0,192},{8,200},{16,208},{24,216},{32,224},{40,232},{48,240},{56,2... | collective-permute-start | bytes 1327112 | tf_op jit(solution)/shard_map/ppermute | solution.py:43
  86.9 10.2 %collective-permute-start.19 = (bf16[192,1024]{1,0:T(8,128)(2,1)S(1)}, bf16[192,1024]{1,0:T(8,128)(2,1)S(1)}, u32[]{:S(2)}, u32[]{:S(2)}) collective-permute-start(bf16[192,1024]{1,0:T(8,128)(2,1)S(1)} %slice.38), channel_id=1, source_target_pairs={{0,16},{8,24},{16,32},{24,40},{32,48},{40,56},{48,0},{56,8},{64,80... | collective-permute-start | bytes 1179656 | tf_op jit(solution)/shard_map/ppermute | solution.py:42
  155.2 48.4 %all-to-all-start.2 = ((bf16[16,24,3584]{2,1,0:T(8,128)(2,1)}), bf16[16,24,3584]{2,1,0:T(8,128)(2,1)}, u32[]{:S(2)}, u32[]{:S(2)}) async-start(bf16[16,24,3584]{2,1,0:T(8,128)(2,1)} %bitcast.5), calls=%async_computation.2 | async-start | bytes 5505024 | tf_op jit(solution)/shard_map/all_to_all | solution.py:477
  163.5 48.4 %collective-permute-start.24 = (bf16[192,1920]{1,0:T(8,128)(2,1)S(1)}, bf16[192,1920]{1,0:T(8,128)(2,1)}, u32[]{:S(2)}, u32[]{:S(2)}) collective-permute-start(bf16[192,1920]{1,0:T(8,128)(2,1)S(1)} %maximum_maximum_fusion.1.p0.m0.a0), channel_id=1, source_target_pairs={{0,8},{8,0},{16,24},{24,16},{32,40},{40,32},{48,56},{56,48},{64,72... | collective-permute-start | bytes 2211848 | tf_op jit(solution)/shard_map/ppermute | solution.py:446
  163.5 48.4 %collective-permute-start.25 = (bf16[192,1920]{1,0:T(8,128)(2,1)S(1)}, bf16[192,1920]{1,0:T(8,128)(2,1)}, u32[]{:S(2)}, u32[]{:S(2)}) collective-permute-start(bf16[192,1920]{1,0:T(8,128)(2,1)S(1)} %collective-permute-done.16.p1.m1.a1), channel_id=1, source_target_pairs={{0,8},{8,0},{16,24},{24,16},{32,40},{40,32},{48,56},{56,48},{64,72... | collective-permute-start | bytes 2211848 | tf_op jit(solution)/shard_map/ppermute | solution.py:446
  164.0 47.9 %collective-permute-start.26 = (bf16[192,1920]{1,0:T(8,128)(2,1)S(1)}, bf16[192,1920]{1,0:T(8,128)(2,1)}, u32[]{:S(2)}, u32[]{:S(2)}) collective-permute-start(bf16[192,1920]{1,0:T(8,128)(2,1)S(1)} %collective-permute-done.17.p2.m2.a2), channel_id=1, source_target_pairs={{0,8},{8,0},{16,24},{24,16},{32,40},{40,32},{48,56},{56,48},{64,72... | collective-permute-start | bytes 2211848 | tf_op jit(solution)/shard_map/ppermute | solution.py:446
  164.1 47.8 %collective-permute-start.27 = (bf16[192,1024]{1,0:T(8,128)(2,1)S(1)}, bf16[192,1024]{1,0:T(8,128)(2,1)S(1)}, u32[]{:S(2)}, u32[]{:S(2)}) collective-permute-start(bf16[192,1024]{1,0:T(8,128)(2,1)S(1)} %collective-permute-done.19.left.a3), channel_id=1, source_target_pairs={{0,8},{8,0},{16,24},{24,16},{32,40},{40,32},{48,56},{56,48},{64,72... | collective-permute-start | bytes 1179656 | tf_op jit(solution)/shard_map/ppermute | solution.py:446
  164.5 47.4 %collective-permute-start.28 = (bf16[192,896]{1,0:T(8,128)(2,1)S(1)}, bf16[192,896]{1,0:T(8,128)(2,1)}, u32[]{:S(2)}, u32[]{:S(2)}) collective-permute-start(bf16[192,896]{1,0:T(8,128)(2,1)S(1)} %collective-permute-done.20.right.m3.a4), channel_id=1, source_target_pairs={{0,8},{8,0},{16,24},{24,16},{32,40},{40,32},{48,56},{56,48},{64,72... | collective-permute-start | bytes 1032200 | tf_op jit(solution)/shard_map/ppermute | solution.py:446
  208.4 13.5 %all-to-all-start.3 = ((bf16[8,24,448]{2,1,0:T(8,128)(2,1)}), bf16[8,24,448]{2,1,0:T(8,128)(2,1)S(1)}, u32[]{:S(2)}, u32[]{:S(2)}) async-start(bf16[8,24,448]{2,1,0:T(8,128)(2,1)} %copy.10), calls=%async_computation.3 | async-start | bytes 393216 | tf_op jit(solution)/shard_map/all_to_all | solution.py:484
  (14 other events, 128.7 us)

commit v3 on v2

v3 whole, which is shorter than its diff:
```python
import functools

import jax
import jax.numpy as jnp
from jax import lax
from jax.experimental import pallas as pl
from jax.experimental.pallas import tpu as pltpu
from jax.sharding import PartitionSpec as P

loss_scale = 65536.0
MIB = 1 << 20
bf16 = jnp.bfloat16
f32 = jnp.float32


def params(mib=12):
    return pltpu.CompilerParams(
        vmem_limit_bytes=mib * MIB, dimension_semantics=("arbitrary",)
    )


AFTER = pl.BlockSpec(memory_space=pl.ANY)


OFFSETS = (0, 3, 1, 2)
SIDE = 4


def shifted(stage, step, shards):
    def to(i):
        x, y, c = i // (2 * SIDE), i // 2 % SIDE, i % 2
        if c == stage:
            x = (x + step) % SIDE
        else:
            y = (y + step) % SIDE
        return (x * SIDE + y) * 2 + c

    return [(i, to(i)) for i in range(shards)]


def cost(flops, size):
    return pl.CostEstimate(flops=int(flops), bytes_accessed=int(size), transcendentals=0)


def whole(shape):
    return pl.BlockSpec(shape, lambda *_: (0,) * len(shape))


def cut_kernel(before, after, left, right):
    left[...] = before[:, : left.shape[1]]
    right[...] = after[:, left.shape[1] :]


def both_ways(block, stage, shards, cut):
    up, down = shifted(stage, 1, shards), shifted(stage, -1, shards)
    before = lax.ppermute(block, "dp", up)
    after = lax.ppermute(block, "dp", down)
    rows, width = block.shape
    shapes = [(rows, cut), (rows, width - cut)]
    left, right = pl.pallas_call(
        cut_kernel,
        grid=(1,),
        in_specs=[whole(block.shape)] * 2,
        out_specs=[whole(v) for v in shapes],
        out_shape=[jax.ShapeDtypeStruct(v, bf16) for v in shapes],
        compiler_params=params(),
        cost_estimate=cost(0, 4 * rows * width),
        name="cut",
    )(before, after)
    return block, before, after, lax.ppermute(left, "dp", up), lax.ppermute(right, "dp", down)


def join_kernel(*refs):
    block, before, after, left, right = refs[:5]
    out, size, cut = refs[-1], block.shape[0], left.shape[1]
    for i, p in enumerate((block, before, after)):
        out[i * size : (i + 1) * size, :] = p[...]
    out[3 * size :, :cut] = left[...]
    out[3 * size :, cut:] = right[...]


def joined(parts, *waits):
    shape = (SIDE * parts[0].shape[0], parts[0].shape[1])
    return pl.pallas_call(
        join_kernel,
        grid=(1,),
        in_specs=[whole(v.shape) for v in parts] + [AFTER] * len(waits),
        out_specs=whole(shape),
        out_shape=jax.ShapeDtypeStruct(shape, bf16),
        compiler_params=params(),
        cost_estimate=cost(0, 4 * shape[0] * shape[1]),
        name="join",
    )(*parts, *waits)


def half_kernel(pos_ref, w_ref, wait_ref, out_ref):
    out_ref[...] = w_ref[...]


def half_for_other(pos, w, wait, chunks):
    depth, cols = w.shape[0] // 2, w.shape[1]
    kb = depth // chunks
    return pl.pallas_call(
        half_kernel,
        grid_spec=pltpu.PrefetchScalarGridSpec(
            num_scalar_prefetch=1,
            grid=(chunks,),
            in_specs=[pl.BlockSpec((kb, cols), lambda k, pos: ((1 - pos[2]) * chunks + k, 0)), AFTER],
            out_specs=pl.BlockSpec((kb, cols), lambda k, pos: (k, 0)),
        ),
        out_shape=jax.ShapeDtypeStruct((depth, cols), w.dtype),
        compiler_params=params(),
        cost_estimate=cost(0, 4 * depth * cols),
        name="half_head",
    )(pos, w, wait)


def block_start(pos_ref, i, j, core, size):
    dx = jnp.where(core == 0, OFFSETS[j], OFFSETS[i])
    dy = jnp.where(core == 0, OFFSETS[i], OFFSETS[j])
    x, y = lax.rem(pos_ref[0] + dx, SIDE), lax.rem(pos_ref[1] + dy, SIDE)
    return pl.multiple_of((x * SIDE + y) * size, 16)


def pack_kernel(tok, meta, pos_ref, live_ref, filled_ref, dest_ref, s_ref, t_ref, keep_ref, send_ref):
    rows, s_half, t_half = s_ref.shape[0], s_ref.shape[1] // 2, t_ref.shape[1] // 2
    core = pos_ref[2]
    lane = lax.broadcasted_iota(jnp.int32, (rows, meta), 1)
    row = lax.broadcasted_iota(jnp.int32, (rows, meta), 0)
    live = jnp.where(row < live_ref[0], 1, 0)
    target = jnp.full((rows, meta), tok * 2 * SIDE * SIDE, jnp.int32)
    for i in range(tok):
        target = jnp.where(row == i, dest_ref[i], target)
    target = jnp.where(row < filled_ref[0], target, tok * 2 * SIDE * SIDE)
    notes = jnp.where(lane == 0, live, jnp.where(lane == 1, target // 32, target % 32))
    notes = notes.astype(f32).astype(bf16)
    first = core == 0
    for ref, low in ((keep_ref, first), (send_ref, jnp.logical_not(first))):
        ref[:, :s_half] = jnp.where(low, s_ref[:, :s_half], s_ref[:, s_half:])
        ref[:, s_half : s_half + meta] = notes
        ref[:, s_half + meta :] = jnp.where(low, t_ref[:, :t_half], t_ref[:, t_half:])


SMEM = pl.BlockSpec(memory_space=pltpu.SMEM)


def pack(pos, live, filled, dest, s, t, meta):
    tok = s.shape[0]
    width = s.shape[1] // 2 + meta + t.shape[1] // 2
    return pl.pallas_call(
        functools.partial(pack_kernel, tok, meta),
        grid=(1,),
        in_specs=[SMEM, SMEM, SMEM, SMEM, whole(s.shape), whole(t.shape)],
        out_specs=[whole((tok, width))] * 2,
        out_shape=[jax.ShapeDtypeStruct((tok, width), bf16)] * 2,
        compiler_params=params(),
        name="pack",
    )(pos, live, filled, dest, s, t)


def pair_kernel(pos_ref, own_ref, got_ref, out_ref):
    first = pos_ref[2] == 0
    own, got = own_ref[...].astype(f32), got_ref[...].astype(f32)
    low = jnp.where(first, own, got)
    high = jnp.where(first, got, own)
    out_ref[...] = jnp.concatenate([low, high], axis=0).astype(bf16)


def pair(pos, own, got):
    tok, width = own.shape
    return pl.pallas_call(
        pair_kernel,
        grid=(1,),
        in_specs=[SMEM, whole(own.shape), whole(got.shape)],
        out_specs=whole((2 * tok, width)),
        out_shape=jax.ShapeDtypeStruct((2 * tok, width), bf16),
        compiler_params=params(),
        name="pair",
    )(pos, own, got)


def near_kernel(first, pos_ref, p0, p1, p2, own_w, other_w, *refs):
    own_ref, other_ref, rows = refs[-3:]
    n, depth = p0.shape[0], rows.shape[1]
    for i, p in enumerate((p0, p1, p2)):
        rows[i * n : (i + 1) * n, :] = p[:, first : first + depth]
    other_ref[...] = jnp.dot(rows[...], other_w[...], preferred_element_type=f32)
    own_ref[...] = jnp.dot(rows[...], own_w[...], preferred_element_type=f32)


def far_kernel(first, pos_ref, left, right, own_w, other_w, own_ref, other_ref, rows):
    depth = rows.shape[1]
    cut = min(left.shape[1] - first, depth)
    rows[:, :cut] = left[:, first : first + cut]
    if cut < depth:
        rows[:, cut:] = right[:, : depth - cut]
    other_ref[...] = jnp.dot(rows[...], other_w[...], preferred_element_type=f32)
    own_ref[...] = jnp.dot(rows[...], own_w[...], preferred_element_type=f32)


def partial_logits(kernel, name, pos, pieces, first, own_w, other_w, *waits):
    n = pieces[0].shape[0] * (3 if len(pieces) == 3 else 1)
    depth, cols = own_w.shape[0] // 2, own_w.shape[1]
    half = pl.BlockSpec((depth, cols), lambda k, pos: (pos[2], 0))
    other = half if other_w.shape == own_w.shape else whole(other_w.shape)
    return pl.pallas_call(
        functools.partial(kernel, first),
        grid_spec=pltpu.PrefetchScalarGridSpec(
            num_scalar_prefetch=1,
            grid=(1,),
            in_specs=[whole(p.shape) for p in pieces] + [half, other] + [AFTER] * len(waits),
            out_specs=[whole((n, cols)), whole((n, cols)), whole((n, depth))],
        ),
        out_shape=[
            jax.ShapeDtypeStruct((n, cols), f32),
            jax.ShapeDtypeStruct((n, cols), f32),
            jax.ShapeDtypeStruct((n, depth), bf16),
        ],
        compiler_params=params(28),
        cost_estimate=cost(4 * n * depth * cols, 2 * (n + 2 * cols) * depth + 8 * n * cols),
        name=name,
    )(pos, *pieces, own_w, other_w, *waits)


def place(out_ref, pos_ref, near, far, near_got, far_got):
    size = near.shape[0] // (3 * SIDE)
    core = pos_ref[2]
    for i in range(SIDE):
        for j in range(SIDE):
            at = pl.ds(((i if i < 3 else 0) * SIDE + j) * size, size)
            start = block_start(pos_ref, i, j, core, size)
            out_ref[pl.ds(start, size), :] = (near if i < 3 else far)[at, :]
    for i in range(SIDE):
        for j in range(SIDE):
            at = pl.ds(((i if i < 3 else 0) * SIDE + j) * size, size)
            start = block_start(pos_ref, i, j, 1 - core, size)
            out_ref[pl.ds(start, size), :] += (near_got if i < 3 else far_got)[at, :]


def student_kernel(pos_ref, near, far, near_got, far_got, m0, m1, m2, m3, s_ref, lse_ref, target_ref, live_ref, notes):
    place(s_ref, pos_ref, near, far, near_got, far_got)
    size = m0.shape[0] // SIDE
    for i, m in enumerate((m0, m1, m2, m3)):
        note = m[...].astype(f32)
        for j in range(SIDE):
            notes[pl.ds(block_start(pos_ref, i, j, pos_ref[2], size), size), :] = note[j * size : (j + 1) * size, :]
    flat = jnp.transpose(notes[...])
    target_ref[...] = (flat[1:2, :] * 32.0 + flat[2:3, :]).astype(jnp.int32)
    for j in range(live_ref.shape[0]):
        live_ref[j : j + 1, :] = flat[0:1, j * 128 : (j + 1) * 128]
    s = s_ref[...]
    top = jnp.max(s, axis=1, keepdims=True)
    lse = top + jnp.log(jnp.sum(jnp.exp(s - top), axis=1, keepdims=True))
    lse_ref[...] = jnp.broadcast_to(lse, lse_ref.shape)


def student_logits(pos, near, far, near_got, far_got, pieces, depth, meta):
    cols = near.shape[1]
    rows = near.shape[0] + far.shape[0]
    block, before, after, far_left, _ = pieces
    at = depth // meta
    size = block.shape[0]
    note = pl.BlockSpec((size, meta), lambda k, pos: (0, at))
    return pl.pallas_call(
        student_kernel,
        grid_spec=pltpu.PrefetchScalarGridSpec(
            num_scalar_prefetch=1,
            grid=(1,),
            in_specs=[whole(near.shape), whole(far.shape)] * 2 + [note] * 4,
            out_specs=[whole((rows, cols)), whole((rows, 128)), whole((1, rows)), whole((rows // 128, 128))],
            scratch_shapes=[pltpu.VMEM((rows, meta), f32)],
        ),
        out_shape=[
            jax.ShapeDtypeStruct((rows, cols), f32),
            jax.ShapeDtypeStruct((rows, 128), f32),
            jax.ShapeDtypeStruct((1, rows), jnp.int32),
            jax.ShapeDtypeStruct((rows // 128, 128), f32),
        ],
        compiler_params=params(20),
        cost_estimate=cost(8 * rows * cols, 12 * rows * cols),
        name="student_logits",
    )(pos, near, far, near_got, far_got, block, before, after, far_left)


def teacher_kernel(pos_ref, near, far, near_got, far_got, target_ref, s_ref, lse_ref, t_ref, stat_ref, slots):
    rows, cols = slots.shape
    place(slots, pos_ref, near, far, near_got, far_got)
    token = lax.broadcasted_iota(jnp.int32, (rows, rows), 0)
    pick = (token == target_ref[...]).astype(f32).astype(bf16)
    value = slots[...]
    high = value.astype(bf16)
    rest = value - high.astype(f32)
    mid = rest.astype(bf16)
    low = (rest - mid.astype(f32)).astype(bf16)
    t = jnp.dot(pick, high, preferred_element_type=f32)
    t += jnp.dot(pick, mid, preferred_element_type=f32)
    t += jnp.dot(pick, low, preferred_element_type=f32)
    t_ref[...] = t
    top = jnp.max(t, axis=1, keepdims=True)
    weight = jnp.exp(t - top)
    total = jnp.sum(weight, axis=1, keepdims=True)
    cross = jnp.sum(weight * (t - s_ref[...]), axis=1, keepdims=True) / total
    lse = top + jnp.log(total)
    lane = lax.broadcasted_iota(jnp.int32, (rows, 128), 1)
    stats = jnp.where(lane == 0, lse_ref[...], jnp.where(lane == 1, lse, cross))
    flat = jnp.transpose(stats)
    n = rows // 128
    copies, used = stat_ref.shape[0], 3 * n
    for i in range(3):
        for j in range(n):
            line = flat[i : i + 1, j * 128 : (j + 1) * 128]
            stat_ref[:, i * n + j, :] = jnp.broadcast_to(line, (copies, 128))
    stat_ref[:, used:, :] = jnp.zeros((copies, stat_ref.shape[1] - used, 128), f32)


def teacher_logits(pos, near, far, near_got, far_got, target, s, lse, copies):
    rows, cols = s.shape
    stat_rows = -(-3 * (rows // 128) // 8) * 8
    return pl.pallas_call(
        teacher_kernel,
        grid_spec=pltpu.PrefetchScalarGridSpec(
            num_scalar_prefetch=1,
            grid=(1,),
            in_specs=[whole(near.shape), whole(far.shape)] * 2
            + [whole((1, rows)), whole((rows, cols)), whole((rows, 128))],
            out_specs=[whole((rows, cols)), whole((copies, stat_rows, 128))],
            scratch_shapes=[pltpu.VMEM((rows, cols), f32)],
        ),
        out_shape=[
            jax.ShapeDtypeStruct((rows, cols), f32),
            jax.ShapeDtypeStruct((copies, stat_rows, 128), f32),
        ],
        compiler_params=params(28),
        cost_estimate=cost(6 * rows * rows * cols, 16 * rows * cols),
        name="teacher_logits",
    )(pos, near, far, near_got, far_got, target, s, lse)


def merged(x, n):
    student, teacher, cross = x[:, 0:n], x[:, n : 2 * n], x[:, 2 * n : 3 * n]
    s_top = jnp.max(student, axis=0)
    s_norm = s_top + jnp.log(jnp.sum(jnp.exp(student - s_top[None]), axis=0))
    t_top = jnp.max(teacher, axis=0)
    weight = jnp.exp(teacher - t_top[None])
    total = jnp.sum(weight, axis=0)
    return s_norm, t_top + jnp.log(total), jnp.sum(weight * cross, axis=0) / total


def merge_kernel(n, x_ref, out_ref):
    s_norm, t_norm, cross = merged(x_ref[...], n)
    out_ref[:, 0:n] = jnp.broadcast_to(s_norm[None], (out_ref.shape[0],) + s_norm.shape)
    out_ref[:, n : 2 * n] = jnp.broadcast_to(t_norm[None], (out_ref.shape[0],) + s_norm.shape)
    out_ref[:, 2 * n : 3 * n] = jnp.broadcast_to(cross[None], (out_ref.shape[0],) + s_norm.shape)
    rest = out_ref.shape[1] - 3 * n
    out_ref[:, 3 * n :] = jnp.zeros((out_ref.shape[0], rest, 128), f32)


def merge(x, n, copies):
    return pl.pallas_call(
        functools.partial(merge_kernel, n),
        out_shape=jax.ShapeDtypeStruct((copies,) + x.shape[1:], f32),
        compiler_params=pltpu.CompilerParams(vmem_limit_bytes=24 * MIB),
        name="merge_stats",
    )(x)


def norm_kernel(n, live_total, x_ref, live_ref, norm_ref, loss_ref):
    s_norm, t_norm, cross = merged(x_ref[...], n)
    live = live_ref[...] > 0
    term = jnp.where(live, cross - t_norm + s_norm, 0.0)
    loss_ref[...] = jnp.sum(term, keepdims=True) / live_total
    norm_ref[0:n, :] = jnp.where(live, s_norm, jnp.inf)
    norm_ref[n : 2 * n, :] = jnp.where(live, t_norm, jnp.inf)


def norms(x, live, n, live_total):
    return pl.pallas_call(
        functools.partial(norm_kernel, n, live_total),
        out_shape=[
            jax.ShapeDtypeStruct((2 * n, 128), f32),
            jax.ShapeDtypeStruct((1, 1), f32),
        ],
        compiler_params=pltpu.CompilerParams(vmem_limit_bytes=24 * MIB),
        name="norms",
    )(x, live)


def column(norm_ref, first, n):
    return jnp.concatenate(
        [
            jnp.transpose(jnp.broadcast_to(norm_ref[first + j : first + j + 1, :], (128, 128)))[:, 0:1]
            for j in range(n)
        ],
        axis=0,
    )


def gap_kernel(grad_scale, tok, pos_ref, s_ref, t_ref, norm_ref, send_ref, keep_ref, own_ref, other_ref, full, part):
    rows = s_ref.shape[0]
    n = rows // 128
    gap = jnp.exp(s_ref[...] - column(norm_ref, 0, n)) - jnp.exp(t_ref[...] - column(norm_ref, n, n))
    full[...] = gap * grad_scale
    core = pos_ref[2]
    for ref, c in ((send_ref, 1 - core), (keep_ref, core)):
        for j in range(rows // (2 * tok)):
            start = pl.multiple_of(2 * tok * j + tok * c, 8)
            part[tok * j : tok * (j + 1), :] = full[pl.ds(start, tok), :]
        ref[...] = part[...].astype(bf16)
    size = 2 * tok
    for ref, c in ((own_ref, core), (other_ref, 1 - core)):
        for i in range(SIDE):
            for j in range(SIDE):
                at = (i * SIDE + j) * size
                start = block_start(pos_ref, i, j, c, size)
                ref[at : at + size, :] = full[pl.ds(start, size), :].astype(bf16)


def logit_gap(pos, s, t, norm, grad_scale, tok):
    rows, cols = s.shape
    half = (rows // 2, cols)
    return pl.pallas_call(
        functools.partial(gap_kernel, grad_scale, tok),
        grid=(1,),
        in_specs=[SMEM, whole((rows, cols)), whole((rows, cols)), whole(norm.shape)],
        out_specs=[whole(half), whole(half), whole((rows, cols)), whole((rows, cols))],
        out_shape=[
            jax.ShapeDtypeStruct((rows // 2, cols), bf16),
            jax.ShapeDtypeStruct((rows // 2, cols), bf16),
            jax.ShapeDtypeStruct((rows, cols), bf16),
            jax.ShapeDtypeStruct((rows, cols), bf16),
        ],
        scratch_shapes=[pltpu.VMEM((rows, cols), f32), pltpu.VMEM((rows // 2, cols), f32)],
        compiler_params=params(20),
        name="logit_gap",
    )(pos, s, t, norm)


def turn_kernel(own_ref, other_ref, own_out, other_out):
    own_out[...] = jnp.transpose(own_ref[...])
    other_out[...] = jnp.transpose(other_ref[...])


def turned(own, other, chunks):
    depth, cols = own.shape
    kb = depth // chunks
    return pl.pallas_call(
        turn_kernel,
        grid=(chunks,),
        in_specs=[pl.BlockSpec((kb, cols), lambda k: (k, 0))] * 2,
        out_specs=[pl.BlockSpec((cols, kb), lambda k: (0, k))] * 2,
        out_shape=[jax.ShapeDtypeStruct((cols, depth), bf16)] * 2,
        compiler_params=params(),
        cost_estimate=cost(0, 16 * depth * cols),
        name="turn",
    )(own, other)


def hidden_kernel(keep_ref, got_ref, own_w, other_w, out_ref):
    out_ref[...] = (
        jnp.dot(keep_ref[...], own_w[...], preferred_element_type=f32)
        + jnp.dot(got_ref[...], other_w[...], preferred_element_type=f32)
    ).astype(bf16)


def grad_hidden_of(keep, got, own_w, other_w, chunks):
    rows, cols = keep.shape
    depth = own_w.shape[1]
    kb = depth // chunks
    head = pl.BlockSpec((cols, kb), lambda k: (0, k))
    return pl.pallas_call(
        hidden_kernel,
        grid=(chunks,),
        in_specs=[whole((rows, cols)), whole((rows, cols)), head, head],
        out_specs=pl.BlockSpec((rows, kb), lambda k: (0, k)),
        out_shape=jax.ShapeDtypeStruct((rows, depth), bf16),
        compiler_params=params(),
        cost_estimate=cost(4 * rows * depth * cols, 2 * depth * (2 * cols + rows)),
        name="grad_hidden",
    )(keep, got, own_w, other_w)


def sum_kernel(slices, x_ref, wait_ref, out_ref):
    total = jnp.sum(x_ref[...].astype(f32), axis=0)
    width = total.shape[1] // slices
    for z in range(slices):
        out_ref[z, :, :] = total[:, z * width : (z + 1) * width].astype(bf16)


def summed(parts, slices, wait):
    n, tok, depth = parts.shape
    out = (slices, tok, depth // slices)
    return pl.pallas_call(
        functools.partial(sum_kernel, slices),
        grid=(1,),
        in_specs=[whole(parts.shape), AFTER],
        out_specs=whole(out),
        out_shape=jax.ShapeDtypeStruct(out, bf16),
        compiler_params=params(),
        name="sum_parts",
    )(parts, wait)


def head_kernel(pos_ref, near, far, near_got, far_got, own_g, other_g, out_ref):
    own = pl.program_id(0) == pos_ref[2]

    def write(near, far, g):
        n = near.shape[0]
        down = (((0,), (0,)), ((), ()))
        out_ref[...] = (
            lax.dot_general(near[...], g[:n, :], down, preferred_element_type=f32)
            + lax.dot_general(far[...], g[n:, :], down, preferred_element_type=f32)
        ).astype(bf16)

    @pl.when(own)
    def _():
        write(near, far, own_g)

    @pl.when(jnp.logical_not(own))
    def _():
        write(near_got, far_got, other_g)


def grad_head_of(pos, near, far, near_got, far_got, own_g, other_g):
    rows, cols = own_g.shape
    depth = near.shape[1]
    args = (near, far, near_got, far_got, own_g, other_g)
    return pl.pallas_call(
        head_kernel,
        grid_spec=pltpu.PrefetchScalarGridSpec(
            num_scalar_prefetch=1,
            grid=(2,),
            in_specs=[whole(v.shape) for v in args],
            out_specs=pl.BlockSpec((depth, cols), lambda k, pos: (k, 0)),
        ),
        out_shape=jax.ShapeDtypeStruct((2 * depth, cols), bf16),
        compiler_params=params(32),
        cost_estimate=cost(4 * rows * depth * cols, 4 * depth * (rows + cols)),
        name="grad_head",
    )(pos, *args)


def per_device(
    student_hidden,
    teacher_hidden,
    student_head,
    teacher_head,
    live_count,
    teacher_count,
    teacher_dest,
):
    tok, depth = student_hidden.shape
    shards, slices = lax.axis_size("dp"), lax.axis_size("vocab")
    rows = tok * shards
    live_total = rows // 2
    n = rows // 128
    meta = 128
    s_half = depth // 2
    first = s_half + meta
    index = lax.axis_index("dp").astype(jnp.int32)
    pos = jnp.stack([index // (2 * SIDE), index // 2 % SIDE, index % 2])
    swap = [(i, i ^ 1) for i in range(shards)]
    other = lambda v: lax.ppermute(v, "dp", swap)
    same_core = [list(range(c, shards, 2)) for c in range(2)]

    keep, send = pack(pos, live_count, teacher_count, teacher_dest, student_hidden, teacher_hidden, meta)
    rows_own = pair(pos, keep, other(send))
    student_other = other(student_head)
    cut = rows_own.shape[1] // 256 * 128
    line = joined(both_ways(rows_own, 0, shards, cut), student_other)
    teacher_other = other(half_for_other(pos, teacher_head, line, 3))
    pieces = both_ways(line, 1, shards, cut)
    heads = turned(student_head, student_other, 7)

    s_near, s_send, near = partial_logits(
        near_kernel, "student_near", pos, pieces[:3], 0, student_head, student_other, *heads
    )
    t_near, t_send, _ = partial_logits(
        near_kernel, "teacher_near", pos, pieces[:3], first, teacher_head, teacher_other
    )
    s_near_got, t_near_got = other(s_send), other(t_send)
    s_far, s_send, far = partial_logits(
        far_kernel, "student_far", pos, pieces[3:], 0, student_head, student_other
    )
    t_far, t_send, _ = partial_logits(
        far_kernel, "teacher_far", pos, pieces[3:], first, teacher_head, teacher_other
    )
    s_far_got, t_far_got = other(s_send), other(t_send)
    s, s_lse, target, live = student_logits(
        pos, s_near, s_far, s_near_got, s_far_got, pieces, s_half, meta
    )
    t, stats = teacher_logits(pos, t_near, t_far, t_near_got, t_far_got, target, s, s_lse, shards)

    stats = lax.all_to_all(stats, "dp", 0, 0)
    stats = lax.all_to_all(merge(stats, n, slices), "vocab", 0, 0)
    norm, loss = norms(stats, live, n, live_total)

    send, keep, own_g, other_g = logit_gap(pos, s, t, norm, loss_scale / live_total, tok)
    mine = grad_hidden_of(keep, other(send), *heads, 7)
    parts = lax.all_to_all(
        mine.reshape(shards // 2, tok, depth), "dp", 0, 0, axis_index_groups=same_core
    )
    grad_head = grad_head_of(pos, near, far, other(near), other(far), own_g, other_g)
    parts = lax.all_to_all(summed(parts, slices, grad_head), "vocab", 0, 0)
    grad_hidden = jnp.sum(parts.astype(f32), axis=0).astype(bf16)
    return (loss[0, 0], grad_hidden, grad_head)


def solution(mesh):
    return jax.shard_map(
        per_device,
        mesh=mesh,
        in_specs=(
            P("dp", None),
            P("dp", None),
            P(None, ("dp", "vocab")),
            P(None, ("dp", "vocab")),
            P("dp"),
            P("dp"),
            P("dp"),
        ),
        out_specs=(P(), P("dp", "vocab"), P(None, ("dp", "vocab"))),
        check_vma=False,
    )
```

time: 223 us -> 181 us (0.81)
  waiting for transfers between devices: 106 us -> 61.9 us
  blocking collectives: 30.6 us -> 44.8 us
  starting transfers between devices: 31.3 us -> 19.7 us
  local copies, waits for them, and re-layouts: 6.63 us -> 10.8 us
  other arithmetic: 3.79 us -> 0.72 us
    ppermute x8 -> x4, waiting for transfers between devices: 33.9 us -> 6.29 us  [the longest x2 5.62 us: both_ways(): lax.ppermute(left, 'dp', up)]
    all_to_all x1, waiting for transfers between devices: 39.1 us -> 24.9 us  [per_device(): lax.all_to_all(mine.reshape(shards // 2, tok, depth), 'dp', 0, 0, axis_in...]
    ppermute x4 -> x2, waiting for transfers between devices: 17.4 us -> 3.6 us  [both_ways(): after = lax.ppermute(block, 'dp', down)]
    all_to_all x0 -> x1, blocking collectives: none -> 12.6 us  [per_device(): parts = lax.all_to_all(summed(parts, slices, grad_head), 'vocab', 0, 0)]
    ppermute x4 -> x2, waiting for transfers between devices: 9.12 us -> 19 us  [both_ways(): before = lax.ppermute(block, 'dp', up)]
    unnamed x14 -> x34, local copies, waits for them, and re-layouts: 3.89 us -> 10.8 us
    all_to_all x1 -> x0, starting transfers between devices: 3.39 us -> none  [per_device(): parts = lax.all_to_all(part, 'vocab', 0, 0)]
    ppermute x4 -> x2, starting transfers between devices: 5.83 us -> 2.54 us  [both_ways(): before = lax.ppermute(block, 'dp', up)]
  transfers between devices with their start and end apart: 31 -> 19, of which waited for: 12 -> 11; matrix products, arithmetic and copies ran while one was open for 3% -> 0% of each run, Pallas kernels for 12% -> 16%
where the time goes in v3:
time: 181 us
  waiting for transfers between devices  61.9 us (34%)
  blocking collectives  44.8 us (25%)
  Pallas kernels  40.5 us (22%)
  starting transfers between devices  19.7 us (11%)
  local copies, waits for them, and re-layouts  10.8 us (6%)
  between operations  2.23 us (1%)
    all_to_all x1, waiting for transfers between devices, per_device(): lax.all_to_all(mine.reshape(shards // 2, tok, depth), 'dp', 0, 0, axis_in...  24.9 us
    ppermute x2, waiting for transfers between devices, both_ways(): before = lax.ppermute(block, 'dp', up)  19 us
    all_to_all x1, blocking collectives, per_device(): stats = lax.all_to_all(stats, 'dp', 0, 0)  16.7 us
    all_to_all x1, blocking collectives, per_device(): stats = lax.all_to_all(merge(stats, n, slices), 'vocab', 0, 0)  15.5 us
    pallas_call x4, Pallas kernels, partial_logits(): pl.pallas_call(functools.partial(kernel, first), grid_spec=pltpu.Prefetch...  13 us
    all_to_all x1, blocking collectives, per_device(): parts = lax.all_to_all(summed(parts, slices, grad_head), 'vocab', 0, 0)  12.6 us
    unnamed x34, local copies, waits for them, and re-layouts  10.8 us
    ppermute x10, waiting for transfers between devices, per_device(): other = lambda v: lax.ppermute(v, 'dp', swap)  8.13 us
  transfers between devices with their start and end apart: 19, of which 11 were waited for; matrix products, arithmetic and copies ran while one was open for 0% of the time, Pallas kernels for 16%

profile of v3, /device:TPU:28, one launch (start us, length us, event | category | flops | bytes accessed | tf_op | source)
XLA Modules:
  0.0 180.8 jit_solution(13294484077073097172)
XLA Ops:
  5.8 1.6 collective-permute-done.got_ref
  10.2 5.9 %collective-permute-done.1.before.refs_1_ = bf16[48,4224]{1,0:T(8,128)(2,1)S(1)} collective-permute-done((bf16[48,4224]{1,0:T(8,128)(2,1)S(1)}, bf16[48,4224]{1,0:T(8,128)(2,1)S(1)}, u32[]{:S(2)}, u32[]{:S(2)}) %collective-permute-start.1) | collective-permute-done | bytes 405536 | tf_op jit(solution)/shard_map/ppermute | solution.py:56
  19.4 4.5 %collective-permute-done.3.refs_3_ = bf16[48,2048]{1,0:T(8,128)(2,1)S(1)} collective-permute-done((bf16[48,2048]{1,0:T(8,128)(2,1)S(1)}, bf16[48,2048]{1,0:T(8,128)(2,1)S(1)}, u32[]{:S(2)}, u32[]{:S(2)}) %collective-permute-start.3) | collective-permute-done | bytes 196640 | tf_op jit(solution)/shard_map/ppermute | solution.py:70
  27.0 5.8 %turn.1 = (bf16[512,3584]{1,0:T(8,128)(2,1)S(1)}, bf16[512,3584]{1,0:T(8,128)(2,1)S(1)}) custom-call(bf16[3584,512]{1,0:T(8,128)(2,1)S(1)} %copy-done.1, bf16[3584,512]{1,0:T(8,128)(2,1)} %collective-permute-done.5.refs_5_.other_ref.other_w), custom_call_target="tpu_custom_call" | custom-call | bytes 29360128 | tf_op jit(solution)/shard_map/turn/pallas_call | solution.py:446
  32.8 13.1 %collective-permute-done.6.p1.before.m1 = bf16[192,4224]{1,0:T(8,128)(2,1)S(1)} collective-permute-done((bf16[192,4224]{1,0:T(8,128)(2,1)S(1)}, bf16[192,4224]{1,0:T(8,128)(2,1)S(1)}, u32[]{:S(2)}, u32[]{:S(2)}) %collective-permute-start.6) | collective-permute-done | bytes 1622048 | tf_op jit(solution)/shard_map/ppermute | solution.py:56
  45.9 2.4 %collective-permute-done.7.p2.after.m2 = bf16[192,4224]{1,0:T(8,128)(2,1)S(1)} collective-permute-done((bf16[192,4224]{1,0:T(8,128)(2,1)S(1)}, bf16[192,4224]{1,0:T(8,128)(2,1)S(1)}, u32[]{:S(2)}, u32[]{:S(2)}) %collective-permute-start.7) | collective-permute-done | bytes 1622048 | tf_op jit(solution)/shard_map/ppermute | solution.py:57
  49.4 3.2 %collective-permute-start.9 = (bf16[192,2048]{1,0:T(8,128)(2,1)}, bf16[192,2048]{1,0:T(8,128)(2,1)S(1)}, u32[]{:S(2)}, u32[]{:S(2)}) collective-permute-start(bf16[192,2048]{1,0:T(8,128)(2,1)} %get-tuple-element.38), channel_id=1, source_target_pairs={{0,16},{8,72},{16,32},{24,88},{32,48},{40,104},{48,0},{56,120},{64... | collective-permute-start | bytes 2359304 | tf_op jit(solution)/shard_map/ppermute | solution.py:70
  52.6 4.3 %student_near.1 = (f32[576,512]{1,0:T(8,128)S(1)}, f32[576,512]{1,0:T(8,128)S(1)}, bf16[576,1792]{1,0:T(8,128)(2,1)S(1)}) custom-call(s32[3]{0:T(128)S(1)} %pad_add_fusion.pos_ref, bf16[192,4224]{1,0:T(8,128)(2,1)S(1)} %join.1.wait_ref.p0.m0, bf16[192,4224]{1,0:T(8,128)(2,1)S(1)} %collective-permute-done.6.p1.before.m1, ...), custom_call_target="tpu_custom_call" | custom-call | flops 2113929216 | bytes 8093696 | tf_op jit(solution)/shard_map/student_near/pallas_call | solution.py:206
  57.1 3.4 %teacher_near.1 = (f32[576,512]{1,0:T(8,128)S(1)}, f32[576,512]{1,0:T(8,128)S(1)}, bf16[576,2304]{1,0:T(8,128)(2,1)}) custom-call(s32[3]{0:T(128)S(1)} %pad_add_fusion.pos_ref, bf16[192,4224]{1,0:T(8,128)(2,1)S(1)} %join.1.wait_ref.p0.m0, bf16[192,4224]{1,0:T(8,128)(2,1)S(1)} %collective-permute-done.6.p1.before.m1, ...), custom_call_target="tpu_custom_call" | custom-call | flops 2717908992 | bytes 9732096 | tf_op jit(solution)/shard_map/teacher_near/pallas_call | solution.py:206
  63.1 2.9 %student_far.1 = (f32[192,512]{1,0:T(8,128)S(1)}, f32[192,512]{1,0:T(8,128)S(1)}, bf16[192,1792]{1,0:T(8,128)(2,1)S(1)}) custom-call(s32[3]{0:T(128)S(1)} %pad_add_fusion.pos_ref, bf16[192,2048]{1,0:T(8,128)(2,1)S(1)} %collective-permute-done.9.left.m3, bf16[192,2176]{1,0:T(8,128)(2,1)S(1)} %collective-permute-done.10.right, ...), custom_call_target="tpu_custom_call" | custom-call | flops 704643072 | bytes 5144576 | tf_op jit(solution)/shard_map/student_far/pallas_call | solution.py:206
  66.9 2.3 %teacher_far.1 = (f32[192,512]{1,0:T(8,128)S(1)}, f32[192,512]{1,0:T(8,128)S(1)}, bf16[192,2304]{1,0:T(8,128)(2,1)}) custom-call(s32[3]{0:T(128)S(1)} %pad_add_fusion.pos_ref, bf16[192,2048]{1,0:T(8,128)(2,1)S(1)} %collective-permute-done.9.left.m3, bf16[192,2176]{1,0:T(8,128)(2,1)S(1)} %collective-permute-done.10.right, bf16[4608,512]{1,0:T(8,128)(2,1)S(1)} %copy-done, ...), custom_call_target="tpu_custom_call" | custom-call | flops 905969664 | bytes 6389760 | tf_op jit(solution)/shard_map/teacher_far/pallas_call | solution.py:206
  71.1 3.7 %teacher_logits.1 = (f32[768,512]{1,0:T(8,128)S(1)}, f32[32,24,128]{2,1,0:T(8,128)S(1)}) custom-call(s32[3]{0:T(128)S(1)} %pad_add_fusion.pos_ref, f32[576,512]{1,0:T(8,128)S(1)} %get-tuple-element.37.near, f32[192,512]{1,0:T(8,128)S(1)} %get-tuple-element.40.far, f32[576,512]{1,0:T(8,128)S(1)} %collective-permute-done.11.near_got, ...), custom_call_target="tpu_custom_call" | custom-call | flops 1811939328 | bytes 6291456 | tf_op jit(solution)/shard_map/teacher_logits/pallas_call | solution.py:319
  74.8 16.7 %all_to_all.20.x_ref = f32[32,24,128]{2,1,0:T(8,128)S(1)} all-to-all(f32[32,24,128]{2,1,0:T(8,128)S(1)} %get-tuple-element.52), channel_id=1, replica_groups=mesh['dp'=32,'vocab'=8] {'dp'}, dimensions={0} | all-to-all | bytes 786432 | tf_op jit(solution)/shard_map/all_to_all | solution.py:593
  91.7 15.5 %all_to_all.21.x_ref = f32[8,24,128]{2,1,0:T(8,128)S(1)} all-to-all(f32[8,24,128]{2,1,0:T(8,128)S(1)} %merge_stats.1), channel_id=1, replica_groups=mesh['dp'=32,'vocab'=8] {'vocab'}, dimensions={0} | all-to-all | bytes 196608 | tf_op jit(solution)/shard_map/all_to_all | solution.py:594
  107.9 1.5 logit_gap.1
  109.5 1.7 collective-permute-done.15.got_ref
  111.3 4.7 %grad_hidden.1 = bf16[384,3584]{1,0:T(8,128)(2,1)S(1)} custom-call(bf16[384,512]{1,0:T(8,128)(2,1)S(1)} %get-tuple-element.57.keep_ref, bf16[384,512]{1,0:T(8,128)(2,1)S(1)} %collective-permute-done.15.got_ref, bf16[512,3584]{1,0:T(8,128)(2,1)S(1)} %copy-done.3, bf16[512,3584]{1,0:T(8,128)(2,1)S(1)} %copy-done.5), custom_call_target="tpu_custom_call" | custom-call | flops 2818572288 | bytes 10092544 | tf_op jit(solution)/shard_map/grad_hidden/pallas_call | solution.py:470
  117.5 7.5 %all-to-all-start.2 = ((bf16[16,24,3584]{2,1,0:T(8,128)(2,1)}), bf16[16,24,3584]{2,1,0:T(8,128)(2,1)S(1)}, u32[]{:S(2)}, u32[]{:S(2)}) async-start(bf16[16,24,3584]{2,1,0:T(8,128)(2,1)} %bitcast.5), calls=%async_computation.2 | async-start | bytes 5505024 | tf_op jit(solution)/shard_map/all_to_all | solution.py:599
  125.5 4.8 %collective-permute-done.17.far_got = bf16[192,1792]{1,0:T(8,128)(2,1)S(1)} collective-permute-done((bf16[192,1792]{1,0:T(8,128)(2,1)}, bf16[192,1792]{1,0:T(8,128)(2,1)S(1)}, u32[]{:S(2)}, u32[]{:S(2)}) %collective-permute-start.17) | collective-permute-done | bytes 688160 | tf_op jit(solution)/shard_map/ppermute | solution.py:562
  130.3 1.6 copy-done.9
  134.1 6.1 %grad_head.1.wait_ref = bf16[3584,512]{1,0:T(8,128)(2,1)} custom-call(s32[3]{0:T(128)S(1)} %pad_add_fusion.pos_ref, bf16[576,1792]{1,0:T(8,128)(2,1)S(1)} %copy-done.9, bf16[192,1792]{1,0:T(8,128)(2,1)S(1)} %copy-done.13, bf16[576,1792]{1,0:T(8,128)(2,1)S(1)} %collective-permute-done.16.near_got, bf16[192,1792]{1,0:T(8,128)(2,1)S(1)} %collective-permute-done.17.far_got, ...), custom_call_target="tpu_custom_call" | custom-call | flops 2818572288 | bytes 9175040 | tf_op jit(solution)/shard_map/grad_head/pallas_call | solution.py:527
  140.1 24.9 %all-to-all-done.2.x_ref = bf16[16,24,3584]{2,1,0:T(8,128)(2,1)S(1)} async-done(((bf16[16,24,3584]{2,1,0:T(8,128)(2,1)}), bf16[16,24,3584]{2,1,0:T(8,128)(2,1)S(1)}, u32[]{:S(2)}, u32[]{:S(2)}) %all-to-all-start.2) | async-done | bytes 2752544 | tf_op jit(solution)/shard_map/all_to_all | solution.py:599
  165.0 2.0 %copy-done.6 = bf16[3584,512]{1,0:T(8,128)(2,1)S(1)} copy-done((bf16[3584,512]{1,0:T(8,128)(2,1)S(1)}, bf16[3584,512]{1,0:T(8,128)(2,1)}, u32[]{:S(2)}) %copy-start.6) | copy-done | bytes 3670040
  167.5 12.6 %all_to_all.22 = bf16[8,24,448]{2,1,0:T(8,128)(2,1)S(1)} all-to-all(bf16[8,24,448]{2,1,0:T(8,128)(2,1)S(1)} %sum_parts.1), channel_id=1, replica_groups=mesh['dp'=32,'vocab'=8] {'vocab'}, dimensions={0} | all-to-all | bytes 344064 | tf_op jit(solution)/shard_map/all_to_all | solution.py:603
  (72 shorter events, 25.7 us)
Async XLA Ops:
  0.6 23.2 %collective-permute-start.5 = (bf16[3584,512]{1,0:T(8,128)(2,1)}, bf16[3584,512]{1,0:T(8,128)(2,1)}, u32[]{:S(2)}, u32[]{:S(2)}) collective-permute-start(bf16[3584,512]{1,0:T(8,128)(2,1)} %own_w.7), channel_id=1, source_target_pairs={{0,8},{8,0},{16,24},{24,16},{32,40},{40,32},{48,56},{56,48},{64,72... | collective-permute-start | bytes 11010056 | tf_op jit(solution)/shard_map/ppermute | solution.py:562
  5.3 2.2 %collective-permute-start = (bf16[24,4224]{1,0:T(8,128)(2,1)S(1)}, bf16[24,4224]{1,0:T(8,128)(2,1)S(1)}, u32[]{:S(2)}, u32[]{:S(2)}) collective-permute-start(bf16[24,4224]{1,0:T(8,128)(2,1)S(1)} %get-tuple-element.34), channel_id=1, source_target_pairs={{0,8},{8,0},{16,24},{24,16},{32,40},{40,32},{48,56},{56,48},{64,72... | collective-permute-start | bytes 608264 | tf_op jit(solution)/shard_map/ppermute | solution.py:562
  8.1 8.0 %collective-permute-start.1 = (bf16[48,4224]{1,0:T(8,128)(2,1)S(1)}, bf16[48,4224]{1,0:T(8,128)(2,1)S(1)}, u32[]{:S(2)}, u32[]{:S(2)}) collective-permute-start(bf16[48,4224]{1,0:T(8,128)(2,1)S(1)} %pair.1.refs_0_), channel_id=1, source_target_pairs={{0,64},{8,24},{16,80},{24,40},{32,96},{40,56},{48,112},{56,8},{64,... | collective-permute-start | bytes 1216520 | tf_op jit(solution)/shard_map/ppermute | solution.py:56
  9.3 7.9 %collective-permute-start.2 = (bf16[48,4224]{1,0:T(8,128)(2,1)S(1)}, bf16[48,4224]{1,0:T(8,128)(2,1)S(1)}, u32[]{:S(2)}, u32[]{:S(2)}) collective-permute-start(bf16[48,4224]{1,0:T(8,128)(2,1)S(1)} %pair.1.refs_0_), channel_id=1, source_target_pairs={{0,192},{8,56},{16,208},{24,8},{32,224},{40,24},{48,240},{56,40},{... | collective-permute-start | bytes 1216520 | tf_op jit(solution)/shard_map/ppermute | solution.py:57
  17.3 6.6 %collective-permute-start.4 = (bf16[48,2176]{1,0:T(8,128)(2,1)S(1)}, bf16[48,2176]{1,0:T(8,128)(2,1)S(1)}, u32[]{:S(2)}, u32[]{:S(2)}) collective-permute-start(bf16[48,2176]{1,0:T(8,128)(2,1)S(1)} %get-tuple-element.36), channel_id=1, source_target_pairs={{0,192},{8,56},{16,208},{24,8},{32,224},{40,24},{48,240},{56,40},{... | collective-permute-start | bytes 626696 | tf_op jit(solution)/shard_map/ppermute | solution.py:70
  18.2 5.7 %collective-permute-start.3 = (bf16[48,2048]{1,0:T(8,128)(2,1)S(1)}, bf16[48,2048]{1,0:T(8,128)(2,1)S(1)}, u32[]{:S(2)}, u32[]{:S(2)}) collective-permute-start(bf16[48,2048]{1,0:T(8,128)(2,1)S(1)} %get-tuple-element.35), channel_id=1, source_target_pairs={{0,64},{8,24},{16,80},{24,40},{32,96},{40,56},{48,112},{56,8},{64,... | collective-permute-start | bytes 589832 | tf_op jit(solution)/shard_map/ppermute | solution.py:70
  24.8 32.3 %collective-permute-start.8 = (bf16[2304,512]{1,0:T(8,128)(2,1)S(1)}, bf16[2304,512]{1,0:T(8,128)(2,1)S(1)}, u32[]{:S(2)}, u32[]{:S(2)}) collective-permute-start(bf16[2304,512]{1,0:T(8,128)(2,1)S(1)} %half_head.1), channel_id=1, source_target_pairs={{0,8},{8,0},{16,24},{24,16},{32,40},{40,32},{48,56},{56,48},{64,72... | collective-permute-start | bytes 7077896 | tf_op jit(solution)/shard_map/ppermute | solution.py:562
  24.9 21.0 %collective-permute-start.6 = (bf16[192,4224]{1,0:T(8,128)(2,1)S(1)}, bf16[192,4224]{1,0:T(8,128)(2,1)S(1)}, u32[]{:S(2)}, u32[]{:S(2)}) collective-permute-start(bf16[192,4224]{1,0:T(8,128)(2,1)S(1)} %join.1.wait_ref.p0.m0), channel_id=1, source_target_pairs={{0,16},{8,72},{16,32},{24,88},{32,48},{40,104},{48,0},{56,120},{64... | collective-permute-start | bytes 4866056 | tf_op jit(solution)/shard_map/ppermute | solution.py:56
  26.1 22.2 %collective-permute-start.7 = (bf16[192,4224]{1,0:T(8,128)(2,1)S(1)}, bf16[192,4224]{1,0:T(8,128)(2,1)S(1)}, u32[]{:S(2)}, u32[]{:S(2)}) collective-permute-start(bf16[192,4224]{1,0:T(8,128)(2,1)S(1)} %join.1.wait_ref.p0.m0), channel_id=1, source_target_pairs={{0,48},{8,200},{16,0},{24,216},{32,16},{40,232},{48,32},{56,248},{... | collective-permute-start | bytes 4866056 | tf_op jit(solution)/shard_map/ppermute | solution.py:57
  32.8 24.2 %copy-start.2 = (bf16[512,3584]{1,0:T(8,128)(2,1)}, bf16[512,3584]{1,0:T(8,128)(2,1)S(1)}, u32[]{:S(2)}) copy-start(bf16[512,3584]{1,0:T(8,128)(2,1)S(1)} %get-tuple-element.43.refs_0_.own_w) | copy-start | bytes 11010052
  32.8 24.2 %copy-start.4 = (bf16[512,3584]{1,0:T(8,128)(2,1)}, bf16[512,3584]{1,0:T(8,128)(2,1)S(1)}, u32[]{:S(2)}) copy-start(bf16[512,3584]{1,0:T(8,128)(2,1)S(1)} %get-tuple-element.44.refs_1_.other_w) | copy-start | bytes 11010052
  49.4 13.7 %collective-permute-start.10 = (bf16[192,2176]{1,0:T(8,128)(2,1)S(1)}, bf16[192,2176]{1,0:T(8,128)(2,1)S(1)}, u32[]{:S(2)}, u32[]{:S(2)}) collective-permute-start(bf16[192,2176]{1,0:T(8,128)(2,1)S(1)} %get-tuple-element.39), channel_id=1, source_target_pairs={{0,48},{8,200},{16,0},{24,216},{32,16},{40,232},{48,32},{56,248},{... | collective-permute-start | bytes 2506760 | tf_op jit(solution)/shard_map/ppermute | solution.py:70
  49.4 13.1 %collective-permute-start.9 = (bf16[192,2048]{1,0:T(8,128)(2,1)}, bf16[192,2048]{1,0:T(8,128)(2,1)S(1)}, u32[]{:S(2)}, u32[]{:S(2)}) collective-permute-start(bf16[192,2048]{1,0:T(8,128)(2,1)} %get-tuple-element.38), channel_id=1, source_target_pairs={{0,16},{8,72},{16,32},{24,88},{32,48},{40,104},{48,0},{56,120},{64... | collective-permute-start | bytes 2359304 | tf_op jit(solution)/shard_map/ppermute | solution.py:70
  57.0 12.8 %collective-permute-start.13 = (f32[576,512]{1,0:T(8,128)S(1)}, f32[576,512]{1,0:T(8,128)S(1)}, u32[]{:S(2)}, u32[]{:S(2)}) collective-permute-start(f32[576,512]{1,0:T(8,128)S(1)} %get-tuple-element.47), channel_id=1, source_target_pairs={{0,8},{8,0},{16,24},{24,16},{32,40},{40,32},{48,56},{56,48},{64,72... | collective-permute-start | bytes 3538952 | tf_op jit(solution)/shard_map/ppermute | solution.py:562
  60.5 10.6 %collective-permute-start.11 = (f32[576,512]{1,0:T(8,128)S(1)}, f32[576,512]{1,0:T(8,128)S(1)}, u32[]{:S(2)}, u32[]{:S(2)}) collective-permute-start(f32[576,512]{1,0:T(8,128)S(1)} %get-tuple-element.41), channel_id=1, source_target_pairs={{0,8},{8,0},{16,24},{24,16},{32,40},{40,32},{48,56},{56,48},{64,72... | collective-permute-start | bytes 3538952 | tf_op jit(solution)/shard_map/ppermute | solution.py:562
  66.9 2.9 %collective-permute-start.14 = (f32[192,512]{1,0:T(8,128)S(1)}, f32[192,512]{1,0:T(8,128)S(1)}, u32[]{:S(2)}, u32[]{:S(2)}) collective-permute-start(f32[192,512]{1,0:T(8,128)S(1)} %get-tuple-element.48), channel_id=1, source_target_pairs={{0,8},{8,0},{16,24},{24,16},{32,40},{40,32},{48,56},{56,48},{64,72... | collective-permute-start | bytes 1179656 | tf_op jit(solution)/shard_map/ppermute | solution.py:562
  69.3 1.9 %collective-permute-start.12 = (f32[192,512]{1,0:T(8,128)S(1)}, f32[192,512]{1,0:T(8,128)S(1)}, u32[]{:S(2)}, u32[]{:S(2)}) collective-permute-start(f32[192,512]{1,0:T(8,128)S(1)} %get-tuple-element.42), channel_id=1, source_target_pairs={{0,8},{8,0},{16,24},{24,16},{32,40},{40,32},{48,56},{56,48},{64,72... | collective-permute-start | bytes 1179656 | tf_op jit(solution)/shard_map/ppermute | solution.py:562
  71.1 40.1 %copy-start.5 = (bf16[512,3584]{1,0:T(8,128)(2,1)S(1)}, bf16[512,3584]{1,0:T(8,128)(2,1)}, u32[]{:S(2)}) copy-start(bf16[512,3584]{1,0:T(8,128)(2,1)} %copy-done.4) | copy-start | bytes 11010052
  91.6 19.7 %copy-start.3 = (bf16[512,3584]{1,0:T(8,128)(2,1)S(1)}, bf16[512,3584]{1,0:T(8,128)(2,1)}, u32[]{:S(2)}) copy-start(bf16[512,3584]{1,0:T(8,128)(2,1)} %copy-done.2) | copy-start | bytes 11010052
  109.4 6.5 %copy-start.10 = (bf16[768,512]{1,0:T(8,128)(2,1)}, bf16[768,512]{1,0:T(8,128)(2,1)S(1)}, u32[]{:S(2)}) copy-start(bf16[768,512]{1,0:T(8,128)(2,1)S(1)} %get-tuple-element.62.other_g) | copy-start | bytes 2359300
  109.4 1.8 %collective-permute-start.15 = (bf16[384,512]{1,0:T(8,128)(2,1)S(1)}, bf16[384,512]{1,0:T(8,128)(2,1)S(1)}, u32[]{:S(2)}, u32[]{:S(2)}) collective-permute-start(bf16[384,512]{1,0:T(8,128)(2,1)S(1)} %get-tuple-element.58), channel_id=1, source_target_pairs={{0,8},{8,0},{16,24},{24,16},{32,40},{40,32},{48,56},{56,48},{64,72... | collective-permute-start | bytes 1179656 | tf_op jit(solution)/shard_map/ppermute | solution.py:562
  117.5 47.6 %all-to-all-start.2 = ((bf16[16,24,3584]{2,1,0:T(8,128)(2,1)}), bf16[16,24,3584]{2,1,0:T(8,128)(2,1)S(1)}, u32[]{:S(2)}, u32[]{:S(2)}) async-start(bf16[16,24,3584]{2,1,0:T(8,128)(2,1)} %bitcast.5), calls=%async_computation.2 | async-start | bytes 5505024 | tf_op jit(solution)/shard_map/all_to_all | solution.py:599
  125.0 5.3 %collective-permute-start.16 = (bf16[576,1792]{1,0:T(8,128)(2,1)}, bf16[576,1792]{1,0:T(8,128)(2,1)S(1)}, u32[]{:S(2)}, u32[]{:S(2)}) collective-permute-start(bf16[576,1792]{1,0:T(8,128)(2,1)} %copy-done.8), channel_id=1, source_target_pairs={{0,8},{8,0},{16,24},{24,16},{32,40},{40,32},{48,56},{56,48},{64,72... | collective-permute-start | bytes 6193160 | tf_op jit(solution)/shard_map/ppermute | solution.py:562
  125.0 5.3 %collective-permute-start.17 = (bf16[192,1792]{1,0:T(8,128)(2,1)}, bf16[192,1792]{1,0:T(8,128)(2,1)S(1)}, u32[]{:S(2)}, u32[]{:S(2)}) collective-permute-start(bf16[192,1792]{1,0:T(8,128)(2,1)} %copy-done.12), channel_id=1, source_target_pairs={{0,8},{8,0},{16,24},{24,16},{32,40},{40,32},{48,56},{56,48},{64,72... | collective-permute-start | bytes 2064392 | tf_op jit(solution)/shard_map/ppermute | solution.py:562
  (12 other events, 23.1 us)

commit v4 on v3

v4 whole, which is shorter than its diff:
```python
import functools

import jax
import jax.numpy as jnp
from jax import lax
from jax.experimental import pallas as pl
from jax.experimental.pallas import tpu as pltpu
from jax.sharding import PartitionSpec as P

loss_scale = 65536.0
MIB = 1 << 20
bf16 = jnp.bfloat16
f32 = jnp.float32


def params(mib=12):
    return pltpu.CompilerParams(
        vmem_limit_bytes=mib * MIB, dimension_semantics=("arbitrary",)
    )


AFTER = pl.BlockSpec(memory_space=pl.ANY)


OFFSETS = (0, 3, 1, 2)
SIDE = 4


def shifted(stage, step, shards):
    def to(i):
        x, y, c = i // (2 * SIDE), i // 2 % SIDE, i % 2
        if c == stage:
            x = (x + step) % SIDE
        else:
            y = (y + step) % SIDE
        return (x * SIDE + y) * 2 + c

    return [(i, to(i)) for i in range(shards)]


def lines(stage):
    out = []
    for c in range(2):
        for a in range(SIDE):
            places = [(b, a) if c == stage else (a, b) for b in range(SIDE)]
            out.append([(x * SIDE + y) * 2 + c for x, y in places])
    return out


def cost(flops, size):
    return pl.CostEstimate(flops=int(flops), bytes_accessed=int(size), transcendentals=0)


def whole(shape):
    return pl.BlockSpec(shape, lambda *_: (0,) * len(shape))


def call(kernel, name, ins, shapes, *waits):
    return pl.pallas_call(
        kernel,
        grid=(1,),
        in_specs=[whole(v.shape) for v in ins] + [AFTER] * len(waits),
        out_specs=[whole(v) for v in shapes],
        out_shape=[jax.ShapeDtypeStruct(v, bf16) for v in shapes],
        compiler_params=params(),
        cost_estimate=cost(0, 0),
        name=name,
    )(*ins, *waits)


def cut_kernel(before, after, *refs):
    left, right = refs[-2:]
    left[...] = before[:, : left.shape[1]]
    right[...] = after[:, left.shape[1] :]


def cut_halves(before, after, cut, *waits):
    rows, width = before.shape
    return call(cut_kernel, "cut", [before, after], [(rows, cut), (rows, width - cut)], *waits)


def join_kernel(block, before, after, left, right, *refs):
    out, size, cut = refs[-1], block.shape[0], left.shape[1]
    for i, p in enumerate((block, before, after)):
        out[i * size : (i + 1) * size, :] = p[...]
    out[3 * size :, :cut] = left[...]
    out[3 * size :, cut:] = right[...]


def joined(parts, *waits):
    shape = (SIDE * parts[0].shape[0], parts[0].shape[1])
    return call(join_kernel, "join", parts, [shape], *waits)[0]


def gathered(s, t, pos, student_head, teacher_head, other, shards):
    def ways(stage):
        up, down = shifted(stage, 1, shards), shifted(stage, -1, shards)
        return lambda a, b: [lax.ppermute(a, "dp", up), lax.ppermute(b, "dp", down)]

    s_cut, t_cut = s.shape[1] // 256 * 128 + 128, t.shape[1] // 2
    one, two = ways(0), ways(1)
    student_other = other(student_head)
    s_near, t_near = one(s, s), one(t, t)
    s_half = cut_halves(*s_near, s_cut, student_other)
    t_half = cut_halves(*t_near, t_cut, s_half[1])
    s_far, t_far = one(*s_half), one(*t_half)
    s_line = joined([s, *s_near, *s_far], t_half[1])
    t_line = joined([t, *t_near, *t_far], s_line)
    s_near, t_near = two(s_line, s_line), two(t_line, t_line)
    teacher_other = other(half_for_other(pos, teacher_head, t_line, 3))
    s_half = cut_halves(*s_near, s_cut, t_line)
    s_far = two(*s_half)
    t_half = cut_halves(*t_near, t_cut, teacher_other, *s_far)
    s_pieces, t_pieces = [s_line, *s_near, *s_far], [t_line, *t_near, *two(*t_half)]
    return s_pieces, t_pieces, s_half[1], t_half[1], student_other, teacher_other


def half_kernel(pos_ref, w_ref, wait_ref, out_ref):
    out_ref[...] = w_ref[...]


def half_for_other(pos, w, wait, chunks):
    depth, cols = w.shape[0] // 2, w.shape[1]
    kb = depth // chunks
    return pl.pallas_call(
        half_kernel,
        grid_spec=pltpu.PrefetchScalarGridSpec(
            num_scalar_prefetch=1,
            grid=(chunks,),
            in_specs=[pl.BlockSpec((kb, cols), lambda k, pos: ((1 - pos[2]) * chunks + k, 0)), AFTER],
            out_specs=pl.BlockSpec((kb, cols), lambda k, pos: (k, 0)),
        ),
        out_shape=jax.ShapeDtypeStruct((depth, cols), w.dtype),
        compiler_params=params(),
        cost_estimate=cost(0, 0),
        name="half_head",
    )(pos, w, wait)


def block_start(pos_ref, i, j, core, size):
    dx = jnp.where(core == 0, OFFSETS[j], OFFSETS[i])
    dy = jnp.where(core == 0, OFFSETS[i], OFFSETS[j])
    x, y = lax.rem(pos_ref[0] + dx, SIDE), lax.rem(pos_ref[1] + dy, SIDE)
    return pl.multiple_of((x * SIDE + y) * size, 16)


def pack_kernel(tok, meta, ints_ref, s_hbm, t_hbm, keep_ref, send_ref, s_ref, t_ref, sem):
    loads = [pltpu.make_async_copy(s_hbm, s_ref, sem.at[0]), pltpu.make_async_copy(t_hbm, t_ref, sem.at[1])]
    for load in loads:
        load.start()
    rows, s_half, t_half = s_ref.shape[0], s_ref.shape[1] // 2, t_ref.shape[1] // 2
    core, live_count, filled, dest = ints_ref[2], ints_ref[3], ints_ref[4], 5
    lane = lax.broadcasted_iota(jnp.int32, (rows, meta), 1)
    row = lax.broadcasted_iota(jnp.int32, (rows, meta), 0)
    live = jnp.where(row < live_count, 1, 0)
    none = tok * 2 * SIDE * SIDE
    target = jnp.full((rows, meta), none, jnp.int32)
    for i in range(tok):
        target = jnp.where(row == i, ints_ref[dest + i], target)
    target = jnp.where(row < filled, target, none)
    notes = jnp.where(lane == 0, live, jnp.where(lane == 1, target // 32, target % 32))
    notes = notes.astype(f32).astype(bf16)
    first = core == 0
    for load in loads:
        load.wait()
    for ref, low in ((keep_ref, first), (send_ref, jnp.logical_not(first))):
        ref[:, :s_half] = jnp.where(low, s_ref[:, :s_half], s_ref[:, s_half:])
        ref[:, s_half : s_half + meta] = notes
        ref[:, s_half + meta :] = jnp.where(low, t_ref[:, :t_half], t_ref[:, t_half:])


SMEM = pl.BlockSpec(memory_space=pltpu.SMEM)
HBM = pl.BlockSpec(memory_space=pltpu.HBM)


def pack(ints, s, t, meta):
    tok = s.shape[0]
    width = s.shape[1] // 2 + meta + t.shape[1] // 2
    return pl.pallas_call(
        functools.partial(pack_kernel, tok, meta),
        grid=(1,),
        in_specs=[SMEM, HBM, HBM],
        out_specs=[whole((tok, width))] * 2,
        out_shape=[jax.ShapeDtypeStruct((tok, width), bf16)] * 2,
        scratch_shapes=[pltpu.VMEM(s.shape, bf16), pltpu.VMEM(t.shape, bf16), pltpu.SemaphoreType.DMA((2,))],
        compiler_params=params(),
        name="pack",
    )(ints, s, t)


def pair_kernel(pos_ref, own_ref, got_ref, a_ref, b_ref):
    first = pos_ref[2] == 0
    own, got = own_ref[...].astype(f32), got_ref[...].astype(f32)
    low = jnp.where(first, own, got)
    high = jnp.where(first, got, own)
    both = jnp.concatenate([low, high], axis=0).astype(bf16)
    a_ref[...] = both[:, : a_ref.shape[1]]
    b_ref[...] = both[:, a_ref.shape[1] :]


def pair(pos, own, got, cut):
    tok, width = own.shape
    return pl.pallas_call(
        pair_kernel,
        grid=(1,),
        in_specs=[SMEM, whole(own.shape), whole(got.shape)],
        out_specs=[whole((2 * tok, cut)), whole((2 * tok, width - cut))],
        out_shape=[
            jax.ShapeDtypeStruct((2 * tok, cut), bf16),
            jax.ShapeDtypeStruct((2 * tok, width - cut), bf16),
        ],
        compiler_params=params(),
        name="pair",
    )(pos, own, got)


def near_kernel(p0, p1, p2, rows):
    at = 0
    for p in (p0, p1, p2):
        n = p.shape[0]
        rows[at : at + n, :] = p[...]
        at += n


def far_kernel(left, right, rows):
    cut = left.shape[1]
    rows[:, :cut] = left[...]
    rows[:, cut:] = right[...]


def logits_kernel(fill, count, pos_ref, *refs):
    own_w, other_w = refs[count : count + 2]
    own_ref, other_ref, rows = refs[-3:]
    fill(*refs[:count], rows)
    depth = own_w.shape[0]
    other_ref[...] = jnp.dot(rows[:, :depth], other_w[...], preferred_element_type=f32)
    own_ref[...] = jnp.dot(rows[:, :depth], own_w[...], preferred_element_type=f32)


def partial_logits(kernel, name, pos, pieces, notes, own_w, other_w, *waits):
    n = pieces[0].shape[0] if len(pieces) == 2 else sum(p.shape[0] for p in pieces)
    depth, cols = own_w.shape[0] // 2, own_w.shape[1]
    half = pl.BlockSpec((depth, cols), lambda k, pos: (pos[2], 0))
    other = half if other_w.shape == own_w.shape else whole(other_w.shape)
    return pl.pallas_call(
        functools.partial(logits_kernel, kernel, len(pieces)),
        grid_spec=pltpu.PrefetchScalarGridSpec(
            num_scalar_prefetch=1,
            grid=(1,),
            in_specs=[whole(p.shape) for p in pieces] + [half, other] + [AFTER] * len(waits),
            out_specs=[whole((n, cols)), whole((n, cols)), whole((n, depth + notes))],
        ),
        out_shape=[
            jax.ShapeDtypeStruct((n, cols), f32),
            jax.ShapeDtypeStruct((n, cols), f32),
            jax.ShapeDtypeStruct((n, depth + notes), bf16),
        ],
        compiler_params=params(28),
        cost_estimate=cost(4 * n * depth * cols, 0),
        name=name,
    )(pos, *pieces, own_w, other_w, *waits)


def place(out_ref, pos_ref, near, far, near_got, far_got):
    size = near.shape[0] // (3 * SIDE)
    core = pos_ref[2]
    for i in range(SIDE):
        for j in range(SIDE):
            at = pl.ds(((i if i < 3 else 0) * SIDE + j) * size, size)
            start = block_start(pos_ref, i, j, core, size)
            out_ref[pl.ds(start, size), :] = (near if i < 3 else far)[at, :]
    for i in range(SIDE):
        for j in range(SIDE):
            at = pl.ds(((i if i < 3 else 0) * SIDE + j) * size, size)
            start = block_start(pos_ref, i, j, 1 - core, size)
            out_ref[pl.ds(start, size), :] += (near_got if i < 3 else far_got)[at, :]


def student_kernel(pos_ref, near, far, near_got, far_got, near_note, far_note, s_ref, lse_ref, target_ref, rank_ref, notes):
    place(s_ref, pos_ref, near, far, near_got, far_got)
    size = far_note.shape[0] // SIDE
    for i in range(SIDE):
        note = far_note[...] if i == 3 else near_note[i * SIDE * size : (i + 1) * SIDE * size, :]
        note = note.astype(f32)
        for j in range(SIDE):
            start = block_start(pos_ref, i, j, pos_ref[2], size)
            notes[pl.ds(start, size), :] = note[j * size : (j + 1) * size, :]
    flat = jnp.transpose(notes[...])
    target_ref[...] = (flat[1:2, :] * 32.0 + flat[2:3, :]).astype(jnp.int32)
    rows = notes.shape[0]
    earlier = lax.broadcasted_iota(jnp.int32, (rows, rows), 0) < lax.broadcasted_iota(jnp.int32, (rows, rows), 1)
    live = jnp.broadcast_to(flat[0:1, :], (16, rows))
    rank = jnp.dot(live.astype(bf16), earlier.astype(f32).astype(bf16), preferred_element_type=f32)
    rank_ref[...] = jnp.where(live > 0, rank, float(rows)).astype(jnp.int32)[0:1, :]
    s = s_ref[...]
    top = jnp.max(s, axis=1, keepdims=True)
    lse = top + jnp.log(jnp.sum(jnp.exp(s - top), axis=1, keepdims=True))
    lse_ref[...] = jnp.broadcast_to(lse, lse_ref.shape)


def student_logits(pos, near, far, near_got, far_got, near_rows, far_rows, depth, meta):
    cols = near.shape[1]
    rows = near.shape[0] + far.shape[0]
    at = depth // meta
    notes = [pl.BlockSpec((v.shape[0], meta), lambda k, pos: (0, at)) for v in (near_rows, far_rows)]
    return pl.pallas_call(
        student_kernel,
        grid_spec=pltpu.PrefetchScalarGridSpec(
            num_scalar_prefetch=1,
            grid=(1,),
            in_specs=[whole(near.shape), whole(far.shape)] * 2 + notes,
            out_specs=[whole((rows, cols)), whole((rows, 128)), whole((1, rows)), whole((1, rows))],
            scratch_shapes=[pltpu.VMEM((rows, meta), f32)],
        ),
        out_shape=[
            jax.ShapeDtypeStruct((rows, cols), f32),
            jax.ShapeDtypeStruct((rows, 128), f32),
            jax.ShapeDtypeStruct((1, rows), jnp.int32),
            jax.ShapeDtypeStruct((1, rows), jnp.int32),
        ],
        compiler_params=params(20),
        cost_estimate=cost(1e11, 0),
        name="student_logits",
    )(pos, near, far, near_got, far_got, near_rows, far_rows)


def picked(pick, value):
    high = value.astype(bf16)
    rest = value - high.astype(f32)
    mid = rest.astype(bf16)
    low = (rest - mid.astype(f32)).astype(bf16)
    out = jnp.dot(pick, high, preferred_element_type=f32)
    out += jnp.dot(pick, mid, preferred_element_type=f32)
    out += jnp.dot(pick, low, preferred_element_type=f32)
    return out


def teacher_kernel(pos_ref, near, far, near_got, far_got, target_ref, rank_ref, s_ref, lse_ref, t_ref, stat_ref, slots):
    rows, cols = slots.shape
    place(slots, pos_ref, near, far, near_got, far_got)
    token = lax.broadcasted_iota(jnp.int32, (rows, rows), 0)
    pick = (token == target_ref[...]).astype(f32).astype(bf16)
    t = picked(pick, slots[...])
    t_ref[...] = t
    top = jnp.max(t, axis=1, keepdims=True)
    weight = jnp.exp(t - top)
    total = jnp.sum(weight, axis=1, keepdims=True)
    cross = jnp.sum(weight * (t - s_ref[...]), axis=1, keepdims=True) / total
    lse = top + jnp.log(total)
    lane = lax.broadcasted_iota(jnp.int32, (rows, 128), 1)
    stats = jnp.where(lane == 0, lse_ref[...], jnp.where(lane == 1, lse, cross))
    live = stat_ref.shape[2] // 3
    chosen = (lax.broadcasted_iota(jnp.int32, (live, rows), 0) == rank_ref[...]).astype(f32).astype(bf16)
    flat = jnp.transpose(picked(chosen, stats))
    line = jnp.concatenate([flat[i : i + 1, :] for i in range(3)], axis=1)
    for i in range(stat_ref.shape[0]):
        stat_ref[i] = line


def teacher_logits(pos, near, far, near_got, far_got, target, rank, s, lse, copies):
    rows, cols = s.shape
    sent = (copies, 1, 3 * (rows // 2))
    return pl.pallas_call(
        teacher_kernel,
        grid_spec=pltpu.PrefetchScalarGridSpec(
            num_scalar_prefetch=1,
            grid=(1,),
            in_specs=[whole(near.shape), whole(far.shape)] * 2
            + [whole((1, rows)), whole((1, rows)), whole((rows, cols)), whole((rows, 128))],
            out_specs=[whole((rows, cols)), whole(sent)],
            scratch_shapes=[pltpu.VMEM((rows, cols), f32)],
        ),
        out_shape=[
            jax.ShapeDtypeStruct((rows, cols), f32),
            jax.ShapeDtypeStruct(sent, f32),
        ],
        compiler_params=params(28),
        cost_estimate=cost(0, 0),
        name="teacher_logits",
    )(pos, near, far, near_got, far_got, target, rank, s, lse)


def merged(x):
    n = x.shape[2] // 3
    student, teacher, cross = x[:, :, 0:n], x[:, :, n : 2 * n], x[:, :, 2 * n :]
    s_top = jnp.max(student, axis=0)
    s_norm = s_top + jnp.log(jnp.sum(jnp.exp(student - s_top[None]), axis=0))
    t_top = jnp.max(teacher, axis=0)
    weight = jnp.exp(teacher - t_top[None])
    total = jnp.sum(weight, axis=0)
    return s_norm, t_top + jnp.log(total), jnp.sum(weight * cross, axis=0) / total


def merge_kernel(x_ref, out_ref):
    line = jnp.concatenate(merged(x_ref[...]), axis=1)
    for i in range(out_ref.shape[0]):
        out_ref[i] = line


def merge(x, copies):
    out = (copies,) + x.shape[1:]
    return pl.pallas_call(
        merge_kernel,
        grid=(1,),
        in_specs=[whole(x.shape)],
        out_specs=whole(out),
        out_shape=jax.ShapeDtypeStruct(out, f32),
        compiler_params=params(),
        name="merge_stats",
    )(x)


def norm_kernel(x_ref, norm_ref, loss_ref):
    s_norm, t_norm, cross = merged(x_ref[...])
    loss_ref[...] = jnp.sum(cross - t_norm + s_norm, keepdims=True) / s_norm.shape[1]
    norm_ref[...] = jnp.concatenate([s_norm, t_norm], axis=1)


def norms(x):
    n = x.shape[2] // 3
    return pl.pallas_call(
        norm_kernel,
        grid=(1,),
        in_specs=[whole(x.shape)],
        out_specs=[whole((1, 2 * n)), whole((1, 1))],
        out_shape=[jax.ShapeDtypeStruct((1, 2 * n), f32), jax.ShapeDtypeStruct((1, 1), f32)],
        compiler_params=params(),
        name="norms",
    )(x)


def column(line):
    return jnp.concatenate(
        [
            jnp.transpose(jnp.broadcast_to(line[:, j : j + 128], (128, 128)))[:, 0:1]
            for j in range(0, line.shape[1], 128)
        ],
        axis=0,
    )


def gap_kernel(grad_scale, tok, pos_ref, s_ref, t_ref, norm_ref, rank_ref, send_ref, keep_ref, own_ref, other_ref, full, part):
    rows = s_ref.shape[0]
    live = norm_ref.shape[1] // 2
    rank = column(rank_ref[...].astype(f32))
    place = lax.broadcasted_iota(jnp.int32, (rows, live), 1).astype(f32)
    lane = lax.broadcasted_iota(jnp.int32, (live, 128), 1)
    norm = norm_ref[...]
    pair = jnp.where(lane == 0, column(norm[:, :live]), column(norm[:, live:]))
    norm = jnp.where(rank < live, picked((place == rank).astype(f32).astype(bf16), pair), jnp.inf)
    gap = jnp.exp(s_ref[...] - norm[:, 0:1]) - jnp.exp(t_ref[...] - norm[:, 1:2])
    full[...] = gap * grad_scale
    core = pos_ref[2]
    for ref, c in ((send_ref, 1 - core), (keep_ref, core)):
        for j in range(rows // (2 * tok)):
            first, second = j // SIDE, j % SIDE
            block = jnp.where(c == 0, first * SIDE + second, second * SIDE + first)
            start = pl.multiple_of(2 * tok * block + tok * c, 8)
            part[tok * j : tok * (j + 1), :] = full[pl.ds(start, tok), :]
        ref[...] = part[...].astype(bf16)
    size = 2 * tok
    for ref, c in ((own_ref, core), (other_ref, 1 - core)):
        for i in range(SIDE):
            for j in range(SIDE):
                at = (i * SIDE + j) * size
                start = block_start(pos_ref, i, j, c, size)
                ref[at : at + size, :] = full[pl.ds(start, size), :].astype(bf16)


def logit_gap(pos, s, t, norm, rank, grad_scale, tok):
    rows, cols = s.shape
    half = (rows // 2, cols)
    return pl.pallas_call(
        functools.partial(gap_kernel, grad_scale, tok),
        grid=(1,),
        in_specs=[SMEM, whole((rows, cols)), whole((rows, cols)), whole(norm.shape), whole(rank.shape)],
        out_specs=[whole(half), whole(half), whole((rows, cols)), whole((rows, cols))],
        out_shape=[
            jax.ShapeDtypeStruct((rows // 2, cols), bf16),
            jax.ShapeDtypeStruct((rows // 2, cols), bf16),
            jax.ShapeDtypeStruct((rows, cols), bf16),
            jax.ShapeDtypeStruct((rows, cols), bf16),
        ],
        scratch_shapes=[pltpu.VMEM((rows, cols), f32), pltpu.VMEM((rows // 2, cols), f32)],
        compiler_params=params(20),
        name="logit_gap",
    )(pos, s, t, norm, rank)


def turn_kernel(own_ref, other_ref, own_out, other_out, done_ref):
    done_ref[...] = jnp.zeros_like(done_ref)
    own_out[...] = jnp.transpose(own_ref[...])
    other_out[...] = jnp.transpose(other_ref[...])


def turned(own, other, chunks):
    depth, cols = own.shape
    kb = depth // chunks
    return pl.pallas_call(
        turn_kernel,
        grid=(chunks,),
        in_specs=[pl.BlockSpec((kb, cols), lambda k: (k, 0))] * 2,
        out_specs=[pl.BlockSpec((cols, kb), lambda k: (0, k))] * 2 + [whole((8, 128))],
        out_shape=[jax.ShapeDtypeStruct((cols, depth), bf16)] * 2 + [jax.ShapeDtypeStruct((8, 128), f32)],
        compiler_params=params(),
        cost_estimate=cost(0, 16 * depth * cols),
        name="turn",
    )(own, other)


def hidden_kernel(keep_ref, got_ref, own_w, other_w, out_hbm, done, sem):
    k = pl.program_id(0)
    kb = own_w.shape[1]

    def store(i):
        return pltpu.make_async_copy(done.at[i], out_hbm.at[:, pl.ds(pl.multiple_of(i * kb, kb), kb)], sem.at[i])

    done[k] = (
        jnp.dot(keep_ref[...], own_w[...], preferred_element_type=f32)
        + jnp.dot(got_ref[...], other_w[...], preferred_element_type=f32)
    ).astype(bf16)
    store(k).start()

    @pl.when(k == pl.num_programs(0) - 1)
    def _():
        for i in range(done.shape[0]):
            store(i).wait()


def grad_hidden_of(keep, got, own_w, other_w, chunks):
    rows, cols = keep.shape
    depth = own_w.shape[1]
    kb = depth // chunks
    head = pl.BlockSpec((cols, kb), lambda k: (0, k))
    return pl.pallas_call(
        hidden_kernel,
        grid=(chunks,),
        in_specs=[whole((rows, cols)), whole((rows, cols)), head, head],
        out_specs=HBM,
        out_shape=pltpu.HBM((rows, depth), bf16),
        scratch_shapes=[pltpu.VMEM((chunks, rows, kb), bf16), pltpu.SemaphoreType.DMA((chunks,))],
        compiler_params=params(),
        cost_estimate=cost(0, 0),
        name="grad_hidden",
    )(keep, got, own_w, other_w)


def sum_kernel(x_ref, wait_ref, out_ref):
    total = jnp.sum(x_ref[...].astype(f32), axis=0)
    n, tok, width = out_ref.shape
    slices = total.shape[1] // width
    for i in range(n):
        j, z = i // slices, i % slices
        out_ref[i] = total[j * tok : (j + 1) * tok, z * width : (z + 1) * width].astype(bf16)


def summed(parts, slices, wait):
    n, rows, depth = parts.shape
    out = (n * slices, rows // n, depth // slices)
    return pl.pallas_call(
        sum_kernel,
        grid=(1,),
        in_specs=[whole(parts.shape), AFTER],
        out_specs=whole(out),
        out_shape=jax.ShapeDtypeStruct(out, bf16),
        compiler_params=params(20),
        name="sum_parts",
    )(parts, wait)


def head_kernel(pos_ref, near, far, near_got, far_got, own_g, other_g, out_ref, done_ref):
    done_ref[...] = jnp.zeros_like(done_ref)
    own = pl.program_id(0) == pos_ref[2]
    depth = out_ref.shape[0]

    def write(near, far, g):
        n = near.shape[0]
        down = (((0,), (0,)), ((), ()))
        out_ref[...] = (
            lax.dot_general(near[:, :depth], g[:n, :], down, preferred_element_type=f32)
            + lax.dot_general(far[:, :depth], g[n:, :], down, preferred_element_type=f32)
        ).astype(bf16)

    @pl.when(own)
    def _():
        write(near, far, own_g)

    @pl.when(jnp.logical_not(own))
    def _():
        write(near_got, far_got, other_g)


def grad_head_of(pos, near, far, near_got, far_got, own_g, other_g, depth):
    rows, cols = own_g.shape
    args = (near, far, near_got, far_got, own_g, other_g)
    return pl.pallas_call(
        head_kernel,
        grid_spec=pltpu.PrefetchScalarGridSpec(
            num_scalar_prefetch=1,
            grid=(2,),
            in_specs=[whole(v.shape) for v in args],
            out_specs=[pl.BlockSpec((depth, cols), lambda k, pos: (k, 0)), whole((8, 128))],
        ),
        out_shape=[jax.ShapeDtypeStruct((2 * depth, cols), bf16), jax.ShapeDtypeStruct((8, 128), f32)],
        compiler_params=params(32),
        cost_estimate=cost(0, 0),
        name="grad_head",
    )(pos, *args)


def per_device(
    student_hidden,
    teacher_hidden,
    student_head,
    teacher_head,
    live_count,
    teacher_count,
    teacher_dest,
):
    tok, depth = student_hidden.shape
    shards, slices = lax.axis_size("dp"), lax.axis_size("vocab")
    rows = tok * shards
    live_total = rows // 2
    meta = 128
    s_half = depth // 2
    first = s_half + meta
    index = lax.axis_index("dp").astype(jnp.int32)
    pos = jnp.stack([index // (2 * SIDE), index // 2 % SIDE, index % 2])
    swap = [(i, i ^ 1) for i in range(shards)]
    other = lambda v: lax.ppermute(v, "dp", swap)

    ints = jnp.concatenate([pos, live_count, teacher_count, teacher_dest])
    keep, send = pack(ints, student_hidden, teacher_hidden, meta)
    a, b = pair(pos, keep, other(send), first)
    s_pieces, t_pieces, s_last_half, t_last_half, student_other, teacher_other = gathered(
        a, b, pos, student_head, teacher_head, other, shards
    )
    *heads, turned_done = turned(student_head, student_other, 7)

    s_near, s_send, near = partial_logits(
        near_kernel, "student_near", pos, s_pieces[:3], meta, student_head, student_other, turned_done, s_last_half
    )
    s_near_got = other(s_send)
    t_near, t_send, _ = partial_logits(
        near_kernel, "teacher_near", pos, t_pieces[:3], 0, teacher_head, teacher_other, t_last_half
    )
    t_near_got = other(t_send)
    s_far, s_send, far = partial_logits(far_kernel, "student_far", pos, s_pieces[3:], meta, student_head, student_other)
    t_far, t_send, _ = partial_logits(far_kernel, "teacher_far", pos, t_pieces[3:], 0, teacher_head, teacher_other)
    s_far_got, t_far_got = other(s_send), other(t_send)
    s, s_lse, target, rank = student_logits(
        pos, s_near, s_far, s_near_got, s_far_got, near, far, s_half, meta
    )
    t, stats = teacher_logits(pos, t_near, t_far, t_near_got, t_far_got, target, rank, s, s_lse, shards)

    stats = lax.all_to_all(stats, "dp", 0, 0)
    stats = lax.all_to_all(merge(stats, slices), "vocab", 0, 0)
    norm, loss = norms(stats)

    send, keep, own_g, other_g = logit_gap(pos, s, t, norm, rank, loss_scale / live_total, tok)
    mine = grad_hidden_of(keep, other(send), *heads, 7)
    parts = lax.all_to_all(
        mine.reshape(SIDE, SIDE * tok, depth), "dp", 0, 0, axis_index_groups=lines(0)
    )
    grad_head, done = grad_head_of(pos, near, far, other(near), other(far), own_g, other_g, s_half)
    groups = [[i * slices + z for i in line for z in range(slices)] for line in lines(1)]
    parts = lax.all_to_all(summed(parts, slices, done), ("dp", "vocab"), 0, 0, axis_index_groups=groups)
    grad_hidden = jnp.sum(parts.astype(f32), axis=0).astype(bf16)
    return (loss[0, 0], grad_hidden, grad_head)


def solution(mesh):
    return jax.shard_map(
        per_device,
        mesh=mesh,
        in_specs=(
            P("dp", None),
            P("dp", None),
            P(None, ("dp", "vocab")),
            P(None, ("dp", "vocab")),
            P("dp"),
            P("dp"),
            P("dp"),
        ),
        out_specs=(P(), P("dp", "vocab"), P(None, ("dp", "vocab"))),
        check_vma=False,
    )
```

time: 181 us -> 171 us (0.945)
  the two profiles are of different devices: /device:TPU:28 before, /device:TPU:1 now
where the time goes in v4:
time: 171 us; the launch traced here: 170 us
  blocking collectives  53.2 us (31%)
  Pallas kernels  47.3 us (28%)
  starting transfers between devices  37.5 us (22%)
  waiting for transfers between devices  24.1 us (14%)
  local copies, waits for them, and re-layouts  4.86 us (3%)
  between operations  2.22 us (1%)
    all_to_all x1, blocking collectives, per_device(): lax.all_to_all(summed(parts, slices, done), ('dp', 'vocab'), 0, 0, axis_i...  25.8 us
    ppermute x16, starting transfers between devices, ways(): return lambda a, b: [lax.ppermute(a, 'dp', up), lax.ppermute(b, 'dp', down)]  20.6 us
    pallas_call x4, Pallas kernels, partial_logits(): pl.pallas_call(functools.partial(logits_kernel, kernel, len(pieces)), gri...  14.4 us
    all_to_all x1, blocking collectives, per_device(): stats = lax.all_to_all(stats, 'dp', 0, 0)  14.1 us
    ppermute x16, waiting for transfers between devices, ways(): return lambda a, b: [lax.ppermute(a, 'dp', up), lax.ppermute(b, 'dp', down)]  13.7 us
    all_to_all x1, blocking collectives, per_device(): stats = lax.all_to_all(merge(stats, slices), 'vocab', 0, 0)  13.3 us
    ppermute x10, starting transfers between devices, per_device(): other = lambda v: lax.ppermute(v, 'dp', swap)  13.2 us
    pallas_call x1, Pallas kernels, grad_head_of(): pl.pallas_call(head_kernel, grid_spec=pltpu.PrefetchScalarGridSpec(num_sc...  8.34 us
  transfers between devices with their start and end apart: 27, of which 10 were waited for; matrix products, arithmetic and copies ran while one was open for 0% of the time, Pallas kernels for 22%

profile of v4, /device:TPU:1, one launch (start us, length us, event | category | flops | bytes accessed | tf_op | source)
XLA Modules:
  0.0 170.1 jit_solution(5049171399673192877)
XLA Ops:
  0.6 3.3 %collective-permute-start.5 = (bf16[3584,512]{1,0:T(8,128)(2,1)}, bf16[3584,512]{1,0:T(8,128)(2,1)}, u32[]{:S(2)}, u32[]{:S(2)}) collective-permute-start(bf16[3584,512]{1,0:T(8,128)(2,1)} %refs_2_.3), channel_id=1, source_target_pairs={{0,8},{8,0},{16,24},{24,16},{32,40},{40,32},{48,56},{56,48},{64,72... | collective-permute-start | bytes 11010056 | tf_op jit(solution)/shard_map/ppermute | solution.py:630
  11.3 2.7 %collective-permute-start.2 = (bf16[48,2304]{1,0:T(8,128)(2,1)S(1)}, bf16[48,2304]{1,0:T(8,128)(2,1)S(1)}, u32[]{:S(2)}, u32[]{:S(2)}) collective-permute-start(bf16[48,2304]{1,0:T(8,128)(2,1)S(1)} %get-tuple-element.44.block), channel_id=1, source_target_pairs={{0,192},{8,56},{16,208},{24,8},{32,224},{40,24},{48,240},{56,40},{... | collective-permute-start | bytes 663560 | tf_op jit(solution)/shard_map/ppermute | solution.py:98
  13.9 2.7 %collective-permute-start.4 = (bf16[48,1920]{1,0:T(8,128)(2,1)S(1)}, bf16[48,1920]{1,0:T(8,128)(2,1)S(1)}, u32[]{:S(2)}, u32[]{:S(2)}) collective-permute-start(bf16[48,1920]{1,0:T(8,128)(2,1)S(1)} %get-tuple-element.45.block), channel_id=1, source_target_pairs={{0,192},{8,56},{16,208},{24,8},{32,224},{40,24},{48,240},{56,40},{... | collective-permute-start | bytes 552968 | tf_op jit(solution)/shard_map/ppermute | solution.py:98
  16.6 3.2 %collective-permute-done.3.before = bf16[48,1920]{1,0:T(8,128)(2,1)S(1)} collective-permute-done((bf16[48,1920]{1,0:T(8,128)(2,1)S(1)}, bf16[48,1920]{1,0:T(8,128)(2,1)S(1)}, u32[]{:S(2)}, u32[]{:S(2)}) %collective-permute-start.3) | collective-permute-done | bytes 184352 | tf_op jit(solution)/shard_map/ppermute | solution.py:98
  20.0 2.7 %collective-permute-start.7 = (bf16[48,1152]{1,0:T(8,128)(2,1)S(1)}, bf16[48,1152]{1,0:T(8,128)(2,1)S(1)}, u32[]{:S(2)}, u32[]{:S(2)}) collective-permute-start(bf16[48,1152]{1,0:T(8,128)(2,1)S(1)} %get-tuple-element.48.refs_0_), channel_id=1, source_target_pairs={{0,192},{8,56},{16,208},{24,8},{32,224},{40,24},{48,240},{56,40},{... | collective-permute-start | bytes 331784 | tf_op jit(solution)/shard_map/ppermute | solution.py:98
  22.6 2.7 %collective-permute-start.9 = (bf16[48,896]{1,0:T(8,128)(2,1)S(1)}, bf16[48,896]{1,0:T(8,128)(2,1)S(1)}, u32[]{:S(2)}, u32[]{:S(2)}) collective-permute-start(bf16[48,896]{1,0:T(8,128)(2,1)S(1)} %get-tuple-element.46.refs_0_), channel_id=1, source_target_pairs={{0,192},{8,56},{16,208},{24,8},{32,224},{40,24},{48,240},{56,40},{... | collective-permute-start | bytes 258056 | tf_op jit(solution)/shard_map/ppermute | solution.py:98
  28.3 3.4 %collective-permute-start.12 = (bf16[2304,512]{1,0:T(8,128)(2,1)S(1)}, bf16[2304,512]{1,0:T(8,128)(2,1)S(1)}, u32[]{:S(2)}, u32[]{:S(2)}) collective-permute-start(bf16[2304,512]{1,0:T(8,128)(2,1)S(1)} %half_head.1), channel_id=1, source_target_pairs={{0,8},{8,0},{16,24},{24,16},{32,40},{40,32},{48,56},{56,48},{64,72... | collective-permute-start | bytes 7077896 | tf_op jit(solution)/shard_map/ppermute | solution.py:630
  31.7 2.8 %collective-permute-start.14 = (bf16[192,1920]{1,0:T(8,128)(2,1)S(1)}, bf16[192,1920]{1,0:T(8,128)(2,1)S(1)}, u32[]{:S(2)}, u32[]{:S(2)}) collective-permute-start(bf16[192,1920]{1,0:T(8,128)(2,1)S(1)} %join.2.refs_0_), channel_id=1, source_target_pairs={{0,48},{8,200},{16,0},{24,216},{32,16},{40,232},{48,32},{56,248},{... | collective-permute-start | bytes 2211848 | tf_op jit(solution)/shard_map/ppermute | solution.py:98
  34.6 2.7 %collective-permute-start.11 = (bf16[192,2304]{1,0:T(8,128)(2,1)S(1)}, bf16[192,2304]{1,0:T(8,128)(2,1)S(1)}, u32[]{:S(2)}, u32[]{:S(2)}) collective-permute-start(bf16[192,2304]{1,0:T(8,128)(2,1)S(1)} %join.3.wait_ref.refs_0_), channel_id=1, source_target_pairs={{0,48},{8,200},{16,0},{24,216},{32,16},{40,232},{48,32},{56,248},{... | collective-permute-start | bytes 2654216 | tf_op jit(solution)/shard_map/ppermute | solution.py:98
  37.2 5.8 %turn.1 = (bf16[512,3584]{1,0:T(8,128)(2,1)S(1)}, bf16[512,3584]{1,0:T(8,128)(2,1)S(1)}, f32[8,128]{1,0:T(8,128)S(1)}) custom-call(bf16[3584,512]{1,0:T(8,128)(2,1)S(1)} %copy-done, bf16[3584,512]{1,0:T(8,128)(2,1)} %collective-permute-done.5.refs_0_.other_ref.refs_4_.refs_3_), custom_call_target="tpu_custom_call" | custom-call | bytes 29360128 | tf_op jit(solution)/shard_map/turn/pallas_call | solution.py:499
  43.8 5.7 %student_near.1 = (f32[576,512]{1,0:T(8,128)S(1)}, f32[576,512]{1,0:T(8,128)S(1)}, bf16[576,1920]{1,0:T(8,128)(2,1)}) custom-call(s32[3]{0:T(128)S(1)} %pad_add_fusion.pos_ref, bf16[192,1920]{1,0:T(8,128)(2,1)S(1)} %join.2.refs_0_, bf16[192,1920]{1,0:T(8,128)(2,1)S(1)} %collective-permute-done.13.before.refs_1_, ...), custom_call_target="tpu_custom_call" | custom-call | flops 2113929216 | tf_op jit(solution)/shard_map/student_near/pallas_call | solution.py:245
  50.3 2.9 %collective-permute-done.10.before.refs_1_ = bf16[192,2304]{1,0:T(8,128)(2,1)S(1)} collective-permute-done((bf16[192,2304]{1,0:T(8,128)(2,1)S(1)}, bf16[192,2304]{1,0:T(8,128)(2,1)S(1)}, u32[]{:S(2)}, u32[]{:S(2)}) %collective-permute-start.10) | collective-permute-done | bytes 884768 | tf_op jit(solution)/shard_map/ppermute | solution.py:98
  54.6 4.9 %collective-permute-done.16.refs_2_.refs_1_ = bf16[192,896]{1,0:T(8,128)(2,1)S(1)} collective-permute-done((bf16[192,896]{1,0:T(8,128)(2,1)S(1)}, bf16[192,896]{1,0:T(8,128)(2,1)S(1)}, u32[]{:S(2)}, u32[]{:S(2)}) %collective-permute-start.16) | collective-permute-done | bytes 344096 | tf_op jit(solution)/shard_map/ppermute | solution.py:98
  59.7 2.7 %collective-permute-start.18 = (bf16[192,1152]{1,0:T(8,128)(2,1)S(1)}, bf16[192,1152]{1,0:T(8,128)(2,1)S(1)}, u32[]{:S(2)}, u32[]{:S(2)}) collective-permute-start(bf16[192,1152]{1,0:T(8,128)(2,1)S(1)} %get-tuple-element.52.refs_5_), channel_id=1, source_target_pairs={{0,48},{8,200},{16,0},{24,216},{32,16},{40,232},{48,32},{56,248},{... | collective-permute-start | bytes 1327112 | tf_op jit(solution)/shard_map/ppermute | solution.py:98
  62.4 2.9 %student_far.1 = (f32[192,512]{1,0:T(8,128)S(1)}, f32[192,512]{1,0:T(8,128)S(1)}, bf16[192,1920]{1,0:T(8,128)(2,1)S(1)}) custom-call(s32[3]{0:T(128)S(1)} %pad_add_fusion.pos_ref, bf16[192,1024]{1,0:T(8,128)(2,1)S(1)} %collective-permute-done.15.refs_1_.refs_0_, bf16[192,896]{1,0:T(8,128)(2,1)S(1)} %collective-permute-done.16.refs_2_.refs_1_, ...), custom_call_target="tpu_custom_call" | custom-call | flops 704643072 | tf_op jit(solution)/shard_map/student_far/pallas_call | solution.py:245
  67.7 3.4 %teacher_near.1 = (f32[576,512]{1,0:T(8,128)S(1)}, f32[576,512]{1,0:T(8,128)S(1)}, bf16[576,2304]{1,0:T(8,128)(2,1)}) custom-call(s32[3]{0:T(128)S(1)} %pad_add_fusion.pos_ref, bf16[192,2304]{1,0:T(8,128)(2,1)S(1)} %join.3.wait_ref.refs_0_, bf16[192,2304]{1,0:T(8,128)(2,1)S(1)} %collective-permute-done.10.before.refs_1_, ...), custom_call_target="tpu_custom_call" | custom-call | flops 2717908992 | tf_op jit(solution)/shard_map/teacher_near/pallas_call | solution.py:245
  76.3 4.8 %teacher_logits.1 = (f32[768,512]{1,0:T(8,128)S(1)}, f32[32,1,1152]{2,1,0:T(1,128)S(1)}) custom-call(s32[3]{0:T(128)S(1)} %pad_add_fusion.pos_ref, f32[576,512]{1,0:T(8,128)S(1)} %get-tuple-element.53.near, f32[192,512]{1,0:T(8,128)S(1)} %get-tuple-element.55.far, f32[576,512]{1,0:T(8,128)S(1)} %collective-permute-done.19.near_got, ...), custom_call_target="tpu_custom_call" | custom-call | tf_op jit(solution)/shard_map/teacher_logits/pallas_call | solution.py:363
  81.2 14.1 %all_to_all.20.x_ref = f32[32,1,1152]{2,1,0:T(1,128)S(1)} all-to-all(f32[32,1,1152]{2,1,0:T(1,128)S(1)} %get-tuple-element.69), channel_id=1, replica_groups=mesh['dp'=32,'vocab'=8] {'dp'}, dimensions={0} | all-to-all | bytes 294912 | tf_op jit(solution)/shard_map/all_to_all | solution.py:656
  95.5 13.3 %all_to_all.21.x_ref = f32[8,1,1152]{2,1,0:T(1,128)S(1)} all-to-all(f32[8,1,1152]{2,1,0:T(1,128)S(1)} %merge_stats.1), channel_id=1, replica_groups=mesh['dp'=32,'vocab'=8] {'vocab'}, dimensions={0} | all-to-all | bytes 73728 | tf_op jit(solution)/shard_map/all_to_all | solution.py:657
  114.8 5.4 %grad_hidden.1 = bf16[384,3584]{1,0:T(8,128)(2,1)} custom-call(bf16[384,512]{1,0:T(8,128)(2,1)S(1)} %get-tuple-element.73.keep_ref, bf16[384,512]{1,0:T(8,128)(2,1)S(1)} %collective-permute-done.23.got_ref, bf16[512,3584]{1,0:T(8,128)(2,1)S(1)} %get-tuple-element.75.own_w, bf16[512,3584]{1,0:T(8,128)(2,1)S(1)} %get-tuple-element.76.other_w), custom_call_target="tpu_custom_call" | custom-call | tf_op jit(solution)/shard_map/grad_hidden/pallas_call | solution.py:535
  120.3 3.7 %all-to-all-start.2 = ((bf16[4,96,3584]{2,1,0:T(8,128)(2,1)}), bf16[4,96,3584]{2,1,0:T(8,128)(2,1)S(1)}, u32[]{:S(2)}, u32[]{:S(2)}) async-start(bf16[4,96,3584]{2,1,0:T(8,128)(2,1)} %bitcast.7), calls=%async_computation.2 | async-start | bytes 5505024 | tf_op jit(solution)/shard_map/all_to_all | solution.py:662
  129.0 8.3 %grad_head.1 = (bf16[3584,512]{1,0:T(8,128)(2,1)}, f32[8,128]{1,0:T(8,128)S(1)}) custom-call(s32[3]{0:T(128)S(1)} %pad_add_fusion.pos_ref, bf16[576,1920]{1,0:T(8,128)(2,1)} %get-tuple-element.63.near_note.near, bf16[192,1920]{1,0:T(8,128)(2,1)S(1)} %copy-done.4, bf16[576,1920]{1,0:T(8,128)(2,1)} %collective-permute-done.24.near_got, ...), custom_call_target="tpu_custom_call" | custom-call | tf_op jit(solution)/shard_map/grad_head/pallas_call | solution.py:596
  137.4 5.8 %all-to-all-done.2.x_ref = bf16[4,96,3584]{2,1,0:T(8,128)(2,1)S(1)} async-done(((bf16[4,96,3584]{2,1,0:T(8,128)(2,1)}), bf16[4,96,3584]{2,1,0:T(8,128)(2,1)S(1)}, u32[]{:S(2)}, u32[]{:S(2)}) %all-to-all-start.2) | async-done | bytes 2752544 | tf_op jit(solution)/shard_map/all_to_all | solution.py:662
  143.5 25.8 %all_to_all.22 = bf16[32,24,448]{2,1,0:T(8,128)(2,1)S(1)} all-to-all(bf16[32,24,448]{2,1,0:T(8,128)(2,1)S(1)} %sum_parts.1), channel_id=1, replica_groups={{0,1,2,3,4,5,6,7,16,17,18,19,20,21,22,23,32,33,34,35,36,37,38,39,48,49,..., dimensions={0} | all-to-all | bytes 1376256 | tf_op jit(solution)/shard_map/all_to_all | solution.py:667
  (77 shorter events, 32.1 us)
Async XLA Ops:
  0.6 19.2 %collective-permute-start.5 = (bf16[3584,512]{1,0:T(8,128)(2,1)}, bf16[3584,512]{1,0:T(8,128)(2,1)}, u32[]{:S(2)}, u32[]{:S(2)}) collective-permute-start(bf16[3584,512]{1,0:T(8,128)(2,1)} %refs_2_.3), channel_id=1, source_target_pairs={{0,8},{8,0},{16,24},{24,16},{32,40},{40,32},{48,56},{56,48},{64,72... | collective-permute-start | bytes 11010056 | tf_op jit(solution)/shard_map/ppermute | solution.py:630
  11.2 8.7 %collective-permute-start.1 = (bf16[48,2304]{1,0:T(8,128)(2,1)S(1)}, bf16[48,2304]{1,0:T(8,128)(2,1)S(1)}, u32[]{:S(2)}, u32[]{:S(2)}) collective-permute-start(bf16[48,2304]{1,0:T(8,128)(2,1)S(1)} %get-tuple-element.44.block), channel_id=1, source_target_pairs={{0,64},{8,24},{16,80},{24,40},{32,96},{40,56},{48,112},{56,8},{64,... | collective-permute-start | bytes 663560 | tf_op jit(solution)/shard_map/ppermute | solution.py:98
  11.3 8.6 %collective-permute-start.2 = (bf16[48,2304]{1,0:T(8,128)(2,1)S(1)}, bf16[48,2304]{1,0:T(8,128)(2,1)S(1)}, u32[]{:S(2)}, u32[]{:S(2)}) collective-permute-start(bf16[48,2304]{1,0:T(8,128)(2,1)S(1)} %get-tuple-element.44.block), channel_id=1, source_target_pairs={{0,192},{8,56},{16,208},{24,8},{32,224},{40,24},{48,240},{56,40},{... | collective-permute-start | bytes 663560 | tf_op jit(solution)/shard_map/ppermute | solution.py:98
  13.9 5.9 %collective-permute-start.3 = (bf16[48,1920]{1,0:T(8,128)(2,1)S(1)}, bf16[48,1920]{1,0:T(8,128)(2,1)S(1)}, u32[]{:S(2)}, u32[]{:S(2)}) collective-permute-start(bf16[48,1920]{1,0:T(8,128)(2,1)S(1)} %get-tuple-element.45.block), channel_id=1, source_target_pairs={{0,64},{8,24},{16,80},{24,40},{32,96},{40,56},{48,112},{56,8},{64,... | collective-permute-start | bytes 552968 | tf_op jit(solution)/shard_map/ppermute | solution.py:98
  13.9 5.9 %collective-permute-start.4 = (bf16[48,1920]{1,0:T(8,128)(2,1)S(1)}, bf16[48,1920]{1,0:T(8,128)(2,1)S(1)}, u32[]{:S(2)}, u32[]{:S(2)}) collective-permute-start(bf16[48,1920]{1,0:T(8,128)(2,1)S(1)} %get-tuple-element.45.block), channel_id=1, source_target_pairs={{0,192},{8,56},{16,208},{24,8},{32,224},{40,24},{48,240},{56,40},{... | collective-permute-start | bytes 552968 | tf_op jit(solution)/shard_map/ppermute | solution.py:98
  19.9 7.5 %collective-permute-start.6 = (bf16[48,1152]{1,0:T(8,128)(2,1)S(1)}, bf16[48,1152]{1,0:T(8,128)(2,1)S(1)}, u32[]{:S(2)}, u32[]{:S(2)}) collective-permute-start(bf16[48,1152]{1,0:T(8,128)(2,1)S(1)} %get-tuple-element.47), channel_id=1, source_target_pairs={{0,64},{8,24},{16,80},{24,40},{32,96},{40,56},{48,112},{56,8},{64,... | collective-permute-start | bytes 331784 | tf_op jit(solution)/shard_map/ppermute | solution.py:98
  20.0 7.4 %collective-permute-start.7 = (bf16[48,1152]{1,0:T(8,128)(2,1)S(1)}, bf16[48,1152]{1,0:T(8,128)(2,1)S(1)}, u32[]{:S(2)}, u32[]{:S(2)}) collective-permute-start(bf16[48,1152]{1,0:T(8,128)(2,1)S(1)} %get-tuple-element.48.refs_0_), channel_id=1, source_target_pairs={{0,192},{8,56},{16,208},{24,8},{32,224},{40,24},{48,240},{56,40},{... | collective-permute-start | bytes 331784 | tf_op jit(solution)/shard_map/ppermute | solution.py:98
  22.6 4.7 %collective-permute-start.8 = (bf16[48,1024]{1,0:T(8,128)(2,1)S(1)}, bf16[48,1024]{1,0:T(8,128)(2,1)S(1)}, u32[]{:S(2)}, u32[]{:S(2)}) collective-permute-start(bf16[48,1024]{1,0:T(8,128)(2,1)S(1)} %get-tuple-element.49), channel_id=1, source_target_pairs={{0,64},{8,24},{16,80},{24,40},{32,96},{40,56},{48,112},{56,8},{64,... | collective-permute-start | bytes 294920 | tf_op jit(solution)/shard_map/ppermute | solution.py:98
  22.6 4.2 %collective-permute-start.9 = (bf16[48,896]{1,0:T(8,128)(2,1)S(1)}, bf16[48,896]{1,0:T(8,128)(2,1)S(1)}, u32[]{:S(2)}, u32[]{:S(2)}) collective-permute-start(bf16[48,896]{1,0:T(8,128)(2,1)S(1)} %get-tuple-element.46.refs_0_), channel_id=1, source_target_pairs={{0,192},{8,56},{16,208},{24,8},{32,224},{40,24},{48,240},{56,40},{... | collective-permute-start | bytes 258056 | tf_op jit(solution)/shard_map/ppermute | solution.py:98
  28.3 31.3 %collective-permute-start.12 = (bf16[2304,512]{1,0:T(8,128)(2,1)S(1)}, bf16[2304,512]{1,0:T(8,128)(2,1)S(1)}, u32[]{:S(2)}, u32[]{:S(2)}) collective-permute-start(bf16[2304,512]{1,0:T(8,128)(2,1)S(1)} %half_head.1), channel_id=1, source_target_pairs={{0,8},{8,0},{16,24},{24,16},{32,40},{40,32},{48,56},{56,48},{64,72... | collective-permute-start | bytes 7077896 | tf_op jit(solution)/shard_map/ppermute | solution.py:630
  31.7 12.0 %collective-permute-start.13 = (bf16[192,1920]{1,0:T(8,128)(2,1)S(1)}, bf16[192,1920]{1,0:T(8,128)(2,1)S(1)}, u32[]{:S(2)}, u32[]{:S(2)}) collective-permute-start(bf16[192,1920]{1,0:T(8,128)(2,1)S(1)} %join.2.refs_0_), channel_id=1, source_target_pairs={{0,16},{8,72},{16,32},{24,88},{32,48},{40,104},{48,0},{56,120},{64... | collective-permute-start | bytes 2211848 | tf_op jit(solution)/shard_map/ppermute | solution.py:98
  31.7 12.0 %collective-permute-start.14 = (bf16[192,1920]{1,0:T(8,128)(2,1)S(1)}, bf16[192,1920]{1,0:T(8,128)(2,1)S(1)}, u32[]{:S(2)}, u32[]{:S(2)}) collective-permute-start(bf16[192,1920]{1,0:T(8,128)(2,1)S(1)} %join.2.refs_0_), channel_id=1, source_target_pairs={{0,48},{8,200},{16,0},{24,216},{32,16},{40,232},{48,32},{56,248},{... | collective-permute-start | bytes 2211848 | tf_op jit(solution)/shard_map/ppermute | solution.py:98
  34.6 18.6 %collective-permute-start.10 = (bf16[192,2304]{1,0:T(8,128)(2,1)S(1)}, bf16[192,2304]{1,0:T(8,128)(2,1)S(1)}, u32[]{:S(2)}, u32[]{:S(2)}) collective-permute-start(bf16[192,2304]{1,0:T(8,128)(2,1)S(1)} %join.3.wait_ref.refs_0_), channel_id=1, source_target_pairs={{0,16},{8,72},{16,32},{24,88},{32,48},{40,104},{48,0},{56,120},{64... | collective-permute-start | bytes 2654216 | tf_op jit(solution)/shard_map/ppermute | solution.py:98
  34.6 20.1 %collective-permute-start.11 = (bf16[192,2304]{1,0:T(8,128)(2,1)S(1)}, bf16[192,2304]{1,0:T(8,128)(2,1)S(1)}, u32[]{:S(2)}, u32[]{:S(2)}) collective-permute-start(bf16[192,2304]{1,0:T(8,128)(2,1)S(1)} %join.3.wait_ref.refs_0_), channel_id=1, source_target_pairs={{0,48},{8,200},{16,0},{24,216},{32,16},{40,232},{48,32},{56,248},{... | collective-permute-start | bytes 2654216 | tf_op jit(solution)/shard_map/ppermute | solution.py:98
  49.4 24.6 %collective-permute-start.21 = (f32[576,512]{1,0:T(8,128)S(1)}, f32[576,512]{1,0:T(8,128)S(1)}, u32[]{:S(2)}, u32[]{:S(2)}) collective-permute-start(f32[576,512]{1,0:T(8,128)S(1)} %get-tuple-element.61), channel_id=1, source_target_pairs={{0,8},{8,0},{16,24},{24,16},{32,40},{40,32},{48,56},{56,48},{64,72... | collective-permute-start | bytes 3538952 | tf_op jit(solution)/shard_map/ppermute | solution.py:630
  50.2 9.3 %collective-permute-start.15 = (bf16[192,1024]{1,0:T(8,128)(2,1)S(1)}, bf16[192,1024]{1,0:T(8,128)(2,1)S(1)}, u32[]{:S(2)}, u32[]{:S(2)}) collective-permute-start(bf16[192,1024]{1,0:T(8,128)(2,1)S(1)} %get-tuple-element.50), channel_id=1, source_target_pairs={{0,16},{8,72},{16,32},{24,88},{32,48},{40,104},{48,0},{56,120},{64... | collective-permute-start | bytes 1179656 | tf_op jit(solution)/shard_map/ppermute | solution.py:98
  53.2 6.4 %collective-permute-start.16 = (bf16[192,896]{1,0:T(8,128)(2,1)S(1)}, bf16[192,896]{1,0:T(8,128)(2,1)S(1)}, u32[]{:S(2)}, u32[]{:S(2)}) collective-permute-start(bf16[192,896]{1,0:T(8,128)(2,1)S(1)} %get-tuple-element.51.refs_6_), channel_id=1, source_target_pairs={{0,48},{8,200},{16,0},{24,216},{32,16},{40,232},{48,32},{56,248},{... | collective-permute-start | bytes 1032200 | tf_op jit(solution)/shard_map/ppermute | solution.py:98
  59.6 11.6 %collective-permute-start.17 = (bf16[192,1152]{1,0:T(8,128)(2,1)S(1)}, bf16[192,1152]{1,0:T(8,128)(2,1)S(1)}, u32[]{:S(2)}, u32[]{:S(2)}) collective-permute-start(bf16[192,1152]{1,0:T(8,128)(2,1)S(1)} %get-tuple-element.54), channel_id=1, source_target_pairs={{0,16},{8,72},{16,32},{24,88},{32,48},{40,104},{48,0},{56,120},{64... | collective-permute-start | bytes 1327112 | tf_op jit(solution)/shard_map/ppermute | solution.py:98
  59.7 11.5 %collective-permute-start.18 = (bf16[192,1152]{1,0:T(8,128)(2,1)S(1)}, bf16[192,1152]{1,0:T(8,128)(2,1)S(1)}, u32[]{:S(2)}, u32[]{:S(2)}) collective-permute-start(bf16[192,1152]{1,0:T(8,128)(2,1)S(1)} %get-tuple-element.52.refs_5_), channel_id=1, source_target_pairs={{0,48},{8,200},{16,0},{24,216},{32,16},{40,232},{48,32},{56,248},{... | collective-permute-start | bytes 1327112 | tf_op jit(solution)/shard_map/ppermute | solution.py:98
  65.4 8.7 %collective-permute-start.22 = (f32[192,512]{1,0:T(8,128)S(1)}, f32[192,512]{1,0:T(8,128)S(1)}, u32[]{:S(2)}, u32[]{:S(2)}) collective-permute-start(f32[192,512]{1,0:T(8,128)S(1)} %get-tuple-element.62), channel_id=1, source_target_pairs={{0,8},{8,0},{16,24},{24,16},{32,40},{40,32},{48,56},{56,48},{64,72... | collective-permute-start | bytes 1179656 | tf_op jit(solution)/shard_map/ppermute | solution.py:630
  71.1 5.2 %collective-permute-start.19 = (f32[576,512]{1,0:T(8,128)S(1)}, f32[576,512]{1,0:T(8,128)S(1)}, u32[]{:S(2)}, u32[]{:S(2)}) collective-permute-start(f32[576,512]{1,0:T(8,128)S(1)} %get-tuple-element.56), channel_id=1, source_target_pairs={{0,8},{8,0},{16,24},{24,16},{32,40},{40,32},{48,56},{56,48},{64,72... | collective-permute-start | bytes 3538952 | tf_op jit(solution)/shard_map/ppermute | solution.py:630
  111.7 3.2 %collective-permute-start.23 = (bf16[384,512]{1,0:T(8,128)(2,1)S(1)}, bf16[384,512]{1,0:T(8,128)(2,1)S(1)}, u32[]{:S(2)}, u32[]{:S(2)}) collective-permute-start(bf16[384,512]{1,0:T(8,128)(2,1)S(1)} %get-tuple-element.74), channel_id=1, source_target_pairs={{0,8},{8,0},{16,24},{24,16},{32,40},{40,32},{48,56},{56,48},{64,72... | collective-permute-start | bytes 1179656 | tf_op jit(solution)/shard_map/ppermute | solution.py:630
  113.5 13.3 %collective-permute-start.24 = (bf16[576,1920]{1,0:T(8,128)(2,1)}, bf16[576,1920]{1,0:T(8,128)(2,1)}, u32[]{:S(2)}, u32[]{:S(2)}) collective-permute-start(bf16[576,1920]{1,0:T(8,128)(2,1)} %get-tuple-element.63.near_note.near), channel_id=1, source_target_pairs={{0,8},{8,0},{16,24},{24,16},{32,40},{40,32},{48,56},{56,48},{64,72... | collective-permute-start | bytes 6635528 | tf_op jit(solution)/shard_map/ppermute | solution.py:630
  120.3 22.8 %all-to-all-start.2 = ((bf16[4,96,3584]{2,1,0:T(8,128)(2,1)}), bf16[4,96,3584]{2,1,0:T(8,128)(2,1)S(1)}, u32[]{:S(2)}, u32[]{:S(2)}) async-start(bf16[4,96,3584]{2,1,0:T(8,128)(2,1)} %bitcast.7), calls=%async_computation.2 | async-start | bytes 5505024 | tf_op jit(solution)/shard_map/all_to_all | solution.py:662
  (12 other events, 71.4 us)

commit v5 on v4

--- a/solution.py
+++ b/solution.py
@@ -55,11 +55,15 @@
     return pl.BlockSpec(shape, lambda *_: (0,) * len(shape))
 
 
+def once(shape):
+    return pl.BlockSpec(shape, lambda *_: (0,) * len(shape), pipeline_mode=pl.Buffered(1))
+
+
 def call(kernel, name, ins, shapes, *waits):
     return pl.pallas_call(
         kernel,
         grid=(1,),
-        in_specs=[whole(v.shape) for v in ins] + [AFTER] * len(waits),
+        in_specs=[once(v.shape) for v in ins] + [AFTER] * len(waits),
         out_specs=[whole(v) for v in shapes],
         out_shape=[jax.ShapeDtypeStruct(v, bf16) for v in shapes],
         compiler_params=params(),
@@ -108,11 +112,12 @@
     t_line = joined([t, *t_near, *t_far], s_line)
     s_near, t_near = two(s_line, s_line), two(t_line, t_line)
     teacher_other = other(half_for_other(pos, teacher_head, t_line, 3))
-    s_half = cut_halves(*s_near, s_cut, t_line)
+    *heads, turned_done = turned(student_head, student_other, 7)
+    s_half = cut_halves(*s_near, s_cut, t_line, turned_done)
     s_far = two(*s_half)
-    t_half = cut_halves(*t_near, t_cut, teacher_other, *s_far)
+    t_half = cut_halves(*t_near, t_cut, teacher_other)
     s_pieces, t_pieces = [s_line, *s_near, *s_far], [t_line, *t_near, *two(*t_half)]
-    return s_pieces, t_pieces, s_half[1], t_half[1], student_other, teacher_other
+    return s_pieces, t_pieces, t_half[1], student_other, teacher_other, heads
 
 
 def half_kernel(pos_ref, w_ref, wait_ref, out_ref):
@@ -144,74 +149,64 @@
     return pl.multiple_of((x * SIDE + y) * size, 16)
 
 
-def pack_kernel(tok, meta, ints_ref, s_hbm, t_hbm, keep_ref, send_ref, s_ref, t_ref, sem):
-    loads = [pltpu.make_async_copy(s_hbm, s_ref, sem.at[0]), pltpu.make_async_copy(t_hbm, t_ref, sem.at[1])]
-    for load in loads:
-        load.start()
-    rows, s_half, t_half = s_ref.shape[0], s_ref.shape[1] // 2, t_ref.shape[1] // 2
-    core, live_count, filled, dest = ints_ref[2], ints_ref[3], ints_ref[4], 5
-    lane = lax.broadcasted_iota(jnp.int32, (rows, meta), 1)
-    row = lax.broadcasted_iota(jnp.int32, (rows, meta), 0)
-    live = jnp.where(row < live_count, 1, 0)
-    none = tok * 2 * SIDE * SIDE
-    target = jnp.full((rows, meta), none, jnp.int32)
-    for i in range(tok):
-        target = jnp.where(row == i, ints_ref[dest + i], target)
-    target = jnp.where(row < filled, target, none)
-    notes = jnp.where(lane == 0, live, jnp.where(lane == 1, target // 32, target % 32))
-    notes = notes.astype(f32).astype(bf16)
-    first = core == 0
-    for load in loads:
-        load.wait()
-    for ref, low in ((keep_ref, first), (send_ref, jnp.logical_not(first))):
-        ref[:, :s_half] = jnp.where(low, s_ref[:, :s_half], s_ref[:, s_half:])
-        ref[:, s_half : s_half + meta] = notes
-        ref[:, s_half + meta :] = jnp.where(low, t_ref[:, :t_half], t_ref[:, t_half:])
-
-
 SMEM = pl.BlockSpec(memory_space=pltpu.SMEM)
 HBM = pl.BlockSpec(memory_space=pltpu.HBM)
 
 
-def pack(ints, s, t, meta):
-    tok = s.shape[0]
-    width = s.shape[1] // 2 + meta + t.shape[1] // 2
-    return pl.pallas_call(
-        functools.partial(pack_kernel, tok, meta),
+def notes_of(table, tok):
+    size = table.shape[1]
+    dest = jnp.transpose(jnp.broadcast_to(table, (size, size)))[:tok, :]
+    row = lax.broadcasted_iota(jnp.int32, (tok, size), 0)
+    lane = lax.broadcasted_iota(jnp.int32, (tok, size), 1)
+    live = jnp.where(row < table[:, tok : tok + 1], 1, 0)
+    target = jnp.where(row < table[:, tok + 1 : tok + 2], dest, tok * 2 * SIDE * SIDE)
+    notes = jnp.where(lane == 0, live, jnp.where(lane == 1, target // 32, target % 32))
+    return notes.astype(f32)
+
+
+def halves(pos_ref, table, s_ref, t_ref):
+    first, tok = pos_ref[2] == 0, s_ref.shape[0]
+    s, t = [
+        jnp.where(first, v[:, : v.shape[1] // 2].astype(f32), v[:, v.shape[1] // 2 :].astype(f32))
+        for v in (s_ref, t_ref)
+    ]
+    return jnp.concatenate([s, notes_of(table[...], tok)], axis=1), t
+
+
+def keep_kernel(pos_ref, table, s_ref, t_ref, a_ref, b_ref):
+    a_ref[...], b_ref[...] = halves(pos_ref, table, s_ref, t_ref)
+
+
+def pair_kernel(pos_ref, own_a, own_b, table, s_ref, t_ref, *refs):
+    a_ref, b_ref = refs[-2:]
+    first = pos_ref[2] == 0
+    for own, got, out in zip((own_a[...], own_b[...]), halves(pos_ref, table, s_ref, t_ref), (a_ref, b_ref)):
+        low, high = jnp.where(first, own, got), jnp.where(first, got, own)
+        out[...] = jnp.concatenate([low, high], axis=0).astype(bf16)
+
+
+def pair(pos, own, got, meta, *waits):
+    tok, depth = own[1].shape
+    widths = (depth // 2 + meta, own[2].shape[1] // 2)
+    kept = pl.pallas_call(
+        keep_kernel,
         grid=(1,),
-        in_specs=[SMEM, HBM, HBM],
-        out_specs=[whole((tok, width))] * 2,
-        out_shape=[jax.ShapeDtypeStruct((tok, width), bf16)] * 2,
-        scratch_shapes=[pltpu.VMEM(s.shape, bf16), pltpu.VMEM(t.shape, bf16), pltpu.SemaphoreType.DMA((2,))],
-        compiler_params=params(),
-        name="pack",
-    )(ints, s, t)
-
-
-def pair_kernel(pos_ref, own_ref, got_ref, a_ref, b_ref):
-    first = pos_ref[2] == 0
-    own, got = own_ref[...].astype(f32), got_ref[...].astype(f32)
-    low = jnp.where(first, own, got)
-    high = jnp.where(first, got, own)
-    both = jnp.concatenate([low, high], axis=0).astype(bf16)
-    a_ref[...] = both[:, : a_ref.shape[1]]
-    b_ref[...] = both[:, a_ref.shape[1] :]
-
-
-def pair(pos, own, got, cut):
-    tok, width = own.shape
+        in_specs=[SMEM] + [once(v.shape) for v in own],
+        out_specs=[whole((tok, v)) for v in widths],
+        out_shape=[jax.ShapeDtypeStruct((tok, v), f32) for v in widths],
+        compiler_params=params(),
+        name="keep",
+    )(pos, *own)
+    args = [*kept, *got]
     return pl.pallas_call(
         pair_kernel,
         grid=(1,),
-        in_specs=[SMEM, whole(own.shape), whole(got.shape)],
-        out_specs=[whole((2 * tok, cut)), whole((2 * tok, width - cut))],
-        out_shape=[
-            jax.ShapeDtypeStruct((2 * tok, cut), bf16),
-            jax.ShapeDtypeStruct((2 * tok, width - cut), bf16),
-        ],
+        in_specs=[SMEM] + [once(v.shape) for v in args] + [AFTER] * len(waits),
+        out_specs=[whole((2 * tok, v)) for v in widths],
+        out_shape=[jax.ShapeDtypeStruct((2 * tok, v), bf16) for v in widths],
         compiler_params=params(),
         name="pair",
-    )(pos, own, got)
+    )(pos, *args, *waits)
 
 
 def near_kernel(p0, p1, p2, rows):
@@ -230,33 +225,43 @@
 
 def logits_kernel(fill, count, pos_ref, *refs):
     own_w, other_w = refs[count : count + 2]
-    own_ref, other_ref, rows = refs[-3:]
+    own_ref, other_ref, rows, own_buf, other_buf, sem = refs[-6:]
+    depth = own_buf.shape[0]
+    mine = pl.ds(pl.multiple_of(pos_ref[2] * depth, 256), depth)
+    loads = [
+        pltpu.make_async_copy(
+            other_w if other_w.shape[0] == depth else other_w.at[mine, :], other_buf, sem.at[0]
+        ),
+        pltpu.make_async_copy(own_w.at[mine, :], own_buf, sem.at[1]),
+    ]
+    for load in loads:
+        load.start()
     fill(*refs[:count], rows)
-    depth = own_w.shape[0]
-    other_ref[...] = jnp.dot(rows[:, :depth], other_w[...], preferred_element_type=f32)
-    own_ref[...] = jnp.dot(rows[:, :depth], own_w[...], preferred_element_type=f32)
-
-
-def partial_logits(kernel, name, pos, pieces, notes, own_w, other_w, *waits):
+    loads[0].wait()
+    other_ref[...] = jnp.dot(rows[:, :depth], other_buf[...], preferred_element_type=f32)
+    loads[1].wait()
+    own_ref[...] = jnp.dot(rows[:, :depth], own_buf[...], preferred_element_type=f32)
+
+
+def partial_logits(kernel, name, pos, pieces, notes, own_w, other_w, *waits, flops=0):
     n = pieces[0].shape[0] if len(pieces) == 2 else sum(p.shape[0] for p in pieces)
     depth, cols = own_w.shape[0] // 2, own_w.shape[1]
-    half = pl.BlockSpec((depth, cols), lambda k, pos: (pos[2], 0))
-    other = half if other_w.shape == own_w.shape else whole(other_w.shape)
+    rows = (n, depth + notes)
+    keep = notes > 0
     return pl.pallas_call(
         functools.partial(logits_kernel, kernel, len(pieces)),
         grid_spec=pltpu.PrefetchScalarGridSpec(
             num_scalar_prefetch=1,
             grid=(1,),
-            in_specs=[whole(p.shape) for p in pieces] + [half, other] + [AFTER] * len(waits),
-            out_specs=[whole((n, cols)), whole((n, cols)), whole((n, depth + notes))],
+            in_specs=[once(p.shape) for p in pieces] + [AFTER] * (2 + len(waits)),
+            out_specs=[whole((n, cols)), whole((n, cols))] + [whole(rows)] * keep,
+            scratch_shapes=[pltpu.VMEM(rows, bf16)] * (not keep)
+            + [pltpu.VMEM((depth, cols), bf16)] * 2
+            + [pltpu.SemaphoreType.DMA((2,))],
         ),
-        out_shape=[
-            jax.ShapeDtypeStruct((n, cols), f32),
-            jax.ShapeDtypeStruct((n, cols), f32),
-            jax.ShapeDtypeStruct((n, depth + notes), bf16),
-        ],
-        compiler_params=params(28),
-        cost_estimate=cost(4 * n * depth * cols, 0),
+        out_shape=[jax.ShapeDtypeStruct((n, cols), f32)] * 2 + [jax.ShapeDtypeStruct(rows, bf16)] * keep,
+        compiler_params=params(20),
+        cost_estimate=cost(flops, 0),
         name=name,
     )(pos, *pieces, own_w, other_w, *waits)
 
@@ -276,8 +281,10 @@
             out_ref[pl.ds(start, size), :] += (near_got if i < 3 else far_got)[at, :]
 
 
-def student_kernel(pos_ref, near, far, near_got, far_got, near_note, far_note, s_ref, lse_ref, target_ref, rank_ref, notes):
-    place(s_ref, pos_ref, near, far, near_got, far_got)
+def student_kernel(
+    pos_ref, near, far, near_got, far_got, near_note, far_note, s_ref, lse_ref, slot_ref, rank_ref, notes, full
+):
+    place(full, pos_ref, near, far, near_got, far_got)
     size = far_note.shape[0] // SIDE
     for i in range(SIDE):
         note = far_note[...] if i == 3 else near_note[i * SIDE * size : (i + 1) * SIDE * size, :]
@@ -286,13 +293,23 @@
             start = block_start(pos_ref, i, j, pos_ref[2], size)
             notes[pl.ds(start, size), :] = note[j * size : (j + 1) * size, :]
     flat = jnp.transpose(notes[...])
-    target_ref[...] = (flat[1:2, :] * 32.0 + flat[2:3, :]).astype(jnp.int32)
-    rows = notes.shape[0]
-    earlier = lax.broadcasted_iota(jnp.int32, (rows, rows), 0) < lax.broadcasted_iota(jnp.int32, (rows, rows), 1)
+    rows, live_rows = notes.shape[0], s_ref.shape[0]
+    first = lax.broadcasted_iota(jnp.int32, (rows, rows), 0)
+    earlier = first < lax.broadcasted_iota(jnp.int32, (rows, rows), 1)
     live = jnp.broadcast_to(flat[0:1, :], (16, rows))
     rank = jnp.dot(live.astype(bf16), earlier.astype(f32).astype(bf16), preferred_element_type=f32)
-    rank_ref[...] = jnp.where(live > 0, rank, float(rows)).astype(jnp.int32)[0:1, :]
-    s = s_ref[...]
+    rank = jnp.where(live > 0, rank, float(rows))
+    rank_ref[...] = rank[0:1, :].astype(jnp.int32)
+    target = (flat[1:2, :] * 32.0 + flat[2:3, :]).astype(jnp.int32)
+    high = jnp.floor(rank / 32.0)
+    digit = lax.broadcasted_iota(jnp.int32, (16, rows), 0)
+    digits = jnp.where(digit == 0, high, rank - high * 32.0)
+    found = jnp.dot(digits.astype(bf16), (first == target).astype(f32).astype(bf16), preferred_element_type=f32)
+    place_of = found[0:1, :] * 32.0 + found[1:2, :]
+    slot_ref[...] = jnp.where(target < rows, place_of, float(rows)).astype(jnp.int32)
+    chosen = lax.broadcasted_iota(jnp.int32, (live_rows, rows), 0) == rank[0:1, :].astype(jnp.int32)
+    s = picked(chosen.astype(f32).astype(bf16), full[...])
+    s_ref[...] = s
     top = jnp.max(s, axis=1, keepdims=True)
     lse = top + jnp.log(jnp.sum(jnp.exp(s - top), axis=1, keepdims=True))
     lse_ref[...] = jnp.broadcast_to(lse, lse_ref.shape)
@@ -303,21 +320,17 @@
     rows = near.shape[0] + far.shape[0]
     at = depth // meta
     notes = [pl.BlockSpec((v.shape[0], meta), lambda k, pos: (0, at)) for v in (near_rows, far_rows)]
+    outs = [((rows // 2, cols), f32), ((rows // 2, 128), f32), ((1, rows), jnp.int32), ((1, rows), jnp.int32)]
     return pl.pallas_call(
         student_kernel,
         grid_spec=pltpu.PrefetchScalarGridSpec(
             num_scalar_prefetch=1,
             grid=(1,),
-            in_specs=[whole(near.shape), whole(far.shape)] * 2 + notes,
-            out_specs=[whole((rows, cols)), whole((rows, 128)), whole((1, rows)), whole((1, rows))],
-            scratch_shapes=[pltpu.VMEM((rows, meta), f32)],
+            in_specs=[once(near.shape), once(far.shape)] * 2 + notes,
+            out_specs=[whole(shape) for shape, _ in outs],
+            scratch_shapes=[pltpu.VMEM((rows, meta), f32), pltpu.VMEM((rows, cols), f32)],
         ),
-        out_shape=[
-            jax.ShapeDtypeStruct((rows, cols), f32),
-            jax.ShapeDtypeStruct((rows, 128), f32),
-            jax.ShapeDtypeStruct((1, rows), jnp.int32),
-            jax.ShapeDtypeStruct((1, rows), jnp.int32),
-        ],
+        out_shape=[jax.ShapeDtypeStruct(*out) for out in outs],
         compiler_params=params(20),
         cost_estimate=cost(1e11, 0),
         name="student_logits",
@@ -335,49 +348,43 @@
     return out
 
 
-def teacher_kernel(pos_ref, near, far, near_got, far_got, target_ref, rank_ref, s_ref, lse_ref, t_ref, stat_ref, slots):
-    rows, cols = slots.shape
+def teacher_kernel(pos_ref, near, far, near_got, far_got, slot_ref, s_ref, lse_ref, t_ref, stat_ref, slots):
+    rows, live = slots.shape[0], s_ref.shape[0]
     place(slots, pos_ref, near, far, near_got, far_got)
-    token = lax.broadcasted_iota(jnp.int32, (rows, rows), 0)
-    pick = (token == target_ref[...]).astype(f32).astype(bf16)
-    t = picked(pick, slots[...])
+    pick = lax.broadcasted_iota(jnp.int32, (live, rows), 0) == slot_ref[...]
+    t = picked(pick.astype(f32).astype(bf16), slots[...])
     t_ref[...] = t
     top = jnp.max(t, axis=1, keepdims=True)
     weight = jnp.exp(t - top)
     total = jnp.sum(weight, axis=1, keepdims=True)
     cross = jnp.sum(weight * (t - s_ref[...]), axis=1, keepdims=True) / total
     lse = top + jnp.log(total)
-    lane = lax.broadcasted_iota(jnp.int32, (rows, 128), 1)
-    stats = jnp.where(lane == 0, lse_ref[...], jnp.where(lane == 1, lse, cross))
-    live = stat_ref.shape[2] // 3
-    chosen = (lax.broadcasted_iota(jnp.int32, (live, rows), 0) == rank_ref[...]).astype(f32).astype(bf16)
-    flat = jnp.transpose(picked(chosen, stats))
+    lane = lax.broadcasted_iota(jnp.int32, (live, 128), 1)
+    flat = jnp.transpose(jnp.where(lane == 0, lse_ref[...], jnp.where(lane == 1, lse, cross)))
     line = jnp.concatenate([flat[i : i + 1, :] for i in range(3)], axis=1)
     for i in range(stat_ref.shape[0]):
         stat_ref[i] = line
 
 
-def teacher_logits(pos, near, far, near_got, far_got, target, rank, s, lse, copies):
-    rows, cols = s.shape
-    sent = (copies, 1, 3 * (rows // 2))
+def teacher_logits(pos, near, far, near_got, far_got, slot, s, lse, copies):
+    live, cols = s.shape
+    rows = near.shape[0] + far.shape[0]
+    sent = (copies, 1, 3 * live)
+    args = (near, far, near_got, far_got, slot, s, lse)
     return pl.pallas_call(
         teacher_kernel,
         grid_spec=pltpu.PrefetchScalarGridSpec(
             num_scalar_prefetch=1,
             grid=(1,),
-            in_specs=[whole(near.shape), whole(far.shape)] * 2
-            + [whole((1, rows)), whole((1, rows)), whole((rows, cols)), whole((rows, 128))],
-            out_specs=[whole((rows, cols)), whole(sent)],
+            in_specs=[once(v.shape) for v in args],
+            out_specs=[whole((live, cols)), whole(sent)],
             scratch_shapes=[pltpu.VMEM((rows, cols), f32)],
         ),
-        out_shape=[
-            jax.ShapeDtypeStruct((rows, cols), f32),
-            jax.ShapeDtypeStruct(sent, f32),
-        ],
-        compiler_params=params(28),
+        out_shape=[jax.ShapeDtypeStruct((live, cols), f32), jax.ShapeDtypeStruct(sent, f32)],
+        compiler_params=params(20),
         cost_estimate=cost(0, 0),
         name="teacher_logits",
-    )(pos, near, far, near_got, far_got, target, rank, s, lse)
+    )(pos, *args)
 
 
 def merged(x):
@@ -402,7 +409,7 @@
     return pl.pallas_call(
         merge_kernel,
         grid=(1,),
-        in_specs=[whole(x.shape)],
+        in_specs=[once(x.shape)],
         out_specs=whole(out),
         out_shape=jax.ShapeDtypeStruct(out, f32),
         compiler_params=params(),
@@ -421,7 +428,7 @@
     return pl.pallas_call(
         norm_kernel,
         grid=(1,),
-        in_specs=[whole(x.shape)],
+        in_specs=[once(x.shape)],
         out_specs=[whole((1, 2 * n)), whole((1, 1))],
         out_shape=[jax.ShapeDtypeStruct((1, 2 * n), f32), jax.ShapeDtypeStruct((1, 1), f32)],
         compiler_params=params(),
@@ -440,16 +447,14 @@
 
 
 def gap_kernel(grad_scale, tok, pos_ref, s_ref, t_ref, norm_ref, rank_ref, send_ref, keep_ref, own_ref, other_ref, full, part):
-    rows = s_ref.shape[0]
-    live = norm_ref.shape[1] // 2
+    live, rows = s_ref.shape[0], full.shape[0]
+    norm = norm_ref[...]
+    gap = jnp.exp(s_ref[...] - column(norm[:, :live])) - jnp.exp(t_ref[...] - column(norm[:, live:]))
     rank = column(rank_ref[...].astype(f32))
-    place = lax.broadcasted_iota(jnp.int32, (rows, live), 1).astype(f32)
-    lane = lax.broadcasted_iota(jnp.int32, (live, 128), 1)
-    norm = norm_ref[...]
-    pair = jnp.where(lane == 0, column(norm[:, :live]), column(norm[:, live:]))
-    norm = jnp.where(rank < live, picked((place == rank).astype(f32).astype(bf16), pair), jnp.inf)
-    gap = jnp.exp(s_ref[...] - norm[:, 0:1]) - jnp.exp(t_ref[...] - norm[:, 1:2])
-    full[...] = gap * grad_scale
+    back = lax.broadcasted_iota(jnp.int32, (rows, live), 1).astype(f32) == rank
+    full[...] = jnp.dot(
+        back.astype(f32).astype(bf16), (gap * grad_scale).astype(bf16), preferred_element_type=f32
+    )
     core = pos_ref[2]
     for ref, c in ((send_ref, 1 - core), (keep_ref, core)):
         for j in range(rows // (2 * tok)):
@@ -468,23 +473,19 @@
 
 
 def logit_gap(pos, s, t, norm, rank, grad_scale, tok):
-    rows, cols = s.shape
+    cols, rows = s.shape[1], rank.shape[1]
     half = (rows // 2, cols)
+    args = (s, t, norm, rank)
     return pl.pallas_call(
         functools.partial(gap_kernel, grad_scale, tok),
         grid=(1,),
-        in_specs=[SMEM, whole((rows, cols)), whole((rows, cols)), whole(norm.shape), whole(rank.shape)],
+        in_specs=[SMEM] + [once(v.shape) for v in args],
         out_specs=[whole(half), whole(half), whole((rows, cols)), whole((rows, cols))],
-        out_shape=[
-            jax.ShapeDtypeStruct((rows // 2, cols), bf16),
-            jax.ShapeDtypeStruct((rows // 2, cols), bf16),
-            jax.ShapeDtypeStruct((rows, cols), bf16),
-            jax.ShapeDtypeStruct((rows, cols), bf16),
-        ],
-        scratch_shapes=[pltpu.VMEM((rows, cols), f32), pltpu.VMEM((rows // 2, cols), f32)],
+        out_shape=[jax.ShapeDtypeStruct(v, bf16) for v in (half, half, (rows, cols), (rows, cols))],
+        scratch_shapes=[pltpu.VMEM((rows, cols), f32), pltpu.VMEM(half, f32)],
         compiler_params=params(20),
         name="logit_gap",
-    )(pos, s, t, norm, rank)
+    )(pos, *args)
 
 
 def turn_kernel(own_ref, other_ref, own_out, other_out, done_ref):
@@ -535,7 +536,7 @@
     return pl.pallas_call(
         hidden_kernel,
         grid=(chunks,),
-        in_specs=[whole((rows, cols)), whole((rows, cols)), head, head],
+        in_specs=[once((rows, cols)), once((rows, cols)), head, head],
         out_specs=HBM,
         out_shape=pltpu.HBM((rows, depth), bf16),
         scratch_shapes=[pltpu.VMEM((chunks, rows, kb), bf16), pltpu.SemaphoreType.DMA((chunks,))],
@@ -560,7 +561,7 @@
     return pl.pallas_call(
         sum_kernel,
         grid=(1,),
-        in_specs=[whole(parts.shape), AFTER],
+        in_specs=[once(parts.shape), AFTER],
         out_specs=whole(out),
         out_shape=jax.ShapeDtypeStruct(out, bf16),
         compiler_params=params(20),
@@ -598,11 +599,11 @@
         grid_spec=pltpu.PrefetchScalarGridSpec(
             num_scalar_prefetch=1,
             grid=(2,),
-            in_specs=[whole(v.shape) for v in args],
+            in_specs=[once(v.shape) for v in args],
             out_specs=[pl.BlockSpec((depth, cols), lambda k, pos: (k, 0)), whole((8, 128))],
         ),
         out_shape=[jax.ShapeDtypeStruct((2 * depth, cols), bf16), jax.ShapeDtypeStruct((8, 128), f32)],
-        compiler_params=params(32),
+        compiler_params=params(24),
         cost_estimate=cost(0, 0),
         name="grad_head",
     )(pos, *args)
@@ -629,29 +630,33 @@
     swap = [(i, i ^ 1) for i in range(shards)]
     other = lambda v: lax.ppermute(v, "dp", swap)
 
-    ints = jnp.concatenate([pos, live_count, teacher_count, teacher_dest])
-    keep, send = pack(ints, student_hidden, teacher_hidden, meta)
-    a, b = pair(pos, keep, other(send), first)
-    s_pieces, t_pieces, s_last_half, t_last_half, student_other, teacher_other = gathered(
+    table = jnp.concatenate([teacher_dest, live_count, teacher_count])
+    table = jnp.pad(table, (0, meta - tok - 2)).reshape(1, meta)
+    own = [table, student_hidden, teacher_hidden]
+    a, b = pair(pos, own, [other(v) for v in own], meta)
+    s_pieces, t_pieces, t_last_half, student_other, teacher_other, heads = gathered(
         a, b, pos, student_head, teacher_head, other, shards
     )
-    *heads, turned_done = turned(student_head, student_other, 7)
 
     s_near, s_send, near = partial_logits(
-        near_kernel, "student_near", pos, s_pieces[:3], meta, student_head, student_other, turned_done, s_last_half
+        near_kernel, "student_near", pos, s_pieces[:3], meta, student_head, student_other
     )
     s_near_got = other(s_send)
-    t_near, t_send, _ = partial_logits(
-        near_kernel, "teacher_near", pos, t_pieces[:3], 0, teacher_head, teacher_other, t_last_half
+    t_near, t_send = partial_logits(
+        near_kernel, "teacher_near", pos, t_pieces[:3], 0, teacher_head, teacher_other, t_last_half, flops=1e11
     )
     t_near_got = other(t_send)
-    s_far, s_send, far = partial_logits(far_kernel, "student_far", pos, s_pieces[3:], meta, student_head, student_other)
-    t_far, t_send, _ = partial_logits(far_kernel, "teacher_far", pos, t_pieces[3:], 0, teacher_head, teacher_other)
-    s_far_got, t_far_got = other(s_send), other(t_send)
-    s, s_lse, target, rank = student_logits(
-        pos, s_near, s_far, s_near_got, s_far_got, near, far, s_half, meta
-    )
-    t, stats = teacher_logits(pos, t_near, t_far, t_near_got, t_far_got, target, rank, s, s_lse, shards)
+    s_far, s_send, far = partial_logits(
+        far_kernel, "student_far", pos, s_pieces[3:], meta, student_head, student_other, t_last_half
+    )
+    s, s_lse, slot, rank = student_logits(
+        pos, s_near, s_far, s_near_got, other(s_send), near, far, s_half, meta
+    )
+    t_far, t_send = partial_logits(
+        far_kernel, "teacher_far", pos, t_pieces[3:], 0, teacher_head, teacher_other
+    )
+    t_far_got = other(t_send)
+    t, stats = teacher_logits(pos, t_near, t_far, t_near_got, t_far_got, slot, s, s_lse, shards)
 
     stats = lax.all_to_all(stats, "dp", 0, 0)
     stats = lax.all_to_all(merge(stats, slices), "vocab", 0, 0)

time: 171 us -> 164 us (0.959)
  waiting for transfers between devices: 24.1 us -> 18.9 us
  Pallas kernels: 47.3 us -> 45 us
    ppermute x16, waiting for transfers between devices: 13.7 us -> 8.13 us  [ways(): return lambda a, b: [lax.ppermute(a, 'dp', up), lax.ppermute(b, 'dp', down)]]
    pallas_call x1, Pallas kernels: 4.84 us -> 2.35 us  [teacher_logits(): pl.pallas_call(teacher_kernel, grid_spec=pltpu.PrefetchScalarGridSpec(num...]
    ppermute x10 -> x12, starting transfers between devices: 13.2 us -> 12.5 us  [per_device(): other = lambda v: lax.ppermute(v, 'dp', swap)]
    ppermute x10 -> x12, waiting for transfers between devices: 4.65 us -> 4.77 us  [per_device(): other = lambda v: lax.ppermute(v, 'dp', swap)]
  transfers between devices with their start and end apart: 27 -> 29, of which waited for: 10 -> 11; matrix products, arithmetic and copies ran while one was open for 0% -> 0% of each run, Pallas kernels for 22% -> 24%
where the time goes in v5:
time: 164 us
  blocking collectives  53.6 us (33%)
  Pallas kernels  45 us (27%)
  starting transfers between devices  38.3 us (23%)
  waiting for transfers between devices  18.9 us (12%)
  local copies, waits for them, and re-layouts  4.13 us (3%)
  between operations  2.23 us (1%)
    all_to_all x1, blocking collectives, per_device(): lax.all_to_all(summed(parts, slices, done), ('dp', 'vocab'), 0, 0, axis_i...  25.8 us
    ppermute x16, starting transfers between devices, ways(): return lambda a, b: [lax.ppermute(a, 'dp', up), lax.ppermute(b, 'dp', down)]  22.2 us
    all_to_all x1, blocking collectives, per_device(): stats = lax.all_to_all(stats, 'dp', 0, 0)  14.4 us
    pallas_call x4, Pallas kernels, partial_logits(): pl.pallas_call(functools.partial(logits_kernel, kernel, len(pieces)), gri...  14.1 us
    all_to_all x1, blocking collectives, per_device(): stats = lax.all_to_all(merge(stats, slices), 'vocab', 0, 0)  13.3 us
    ppermute x12, starting transfers between devices, per_device(): other = lambda v: lax.ppermute(v, 'dp', swap)  12.5 us
    pallas_call x1, Pallas kernels, grad_head_of(): pl.pallas_call(head_kernel, grid_spec=pltpu.PrefetchScalarGridSpec(num_sc...  8.33 us
    ppermute x16, waiting for transfers between devices, ways(): return lambda a, b: [lax.ppermute(a, 'dp', up), lax.ppermute(b, 'dp', down)]  8.13 us
  transfers between devices with their start and end apart: 29, of which 11 were waited for; matrix products, arithmetic and copies ran while one was open for 0% of the time, Pallas kernels for 24%

profile of v5, /device:TPU:1, one launch (start us, length us, event | category | flops | bytes accessed | tf_op | source)
XLA Modules:
  0.0 163.8 jit_solution(15026788543003202632)
XLA Ops:
  0.6 3.3 %collective-permute-start.7 = (bf16[3584,512]{1,0:T(8,128)(2,1)}, bf16[3584,512]{1,0:T(8,128)(2,1)}, u32[]{:S(2)}, u32[]{:S(2)}) collective-permute-start(bf16[3584,512]{1,0:T(8,128)(2,1)} %refs_2_.3), channel_id=1, source_target_pairs={{0,8},{8,0},{16,24},{24,16},{32,40},{40,32},{48,56},{56,48},{64,72... | collective-permute-start | bytes 11010056 | tf_op jit(solution)/shard_map/ppermute | solution.py:631
  11.4 2.7 %collective-permute-start.4 = (bf16[48,2304]{1,0:T(8,128)(2,1)S(1)}, bf16[48,2304]{1,0:T(8,128)(2,1)S(1)}, u32[]{:S(2)}, u32[]{:S(2)}) collective-permute-start(bf16[48,2304]{1,0:T(8,128)(2,1)S(1)} %get-tuple-element.44.block), channel_id=1, source_target_pairs={{0,192},{8,56},{16,208},{24,8},{32,224},{40,24},{48,240},{56,40},{... | collective-permute-start | bytes 663560 | tf_op jit(solution)/shard_map/ppermute | solution.py:102
  14.1 2.7 %collective-permute-start.6 = (bf16[48,1920]{1,0:T(8,128)(2,1)S(1)}, bf16[48,1920]{1,0:T(8,128)(2,1)S(1)}, u32[]{:S(2)}, u32[]{:S(2)}) collective-permute-start(bf16[48,1920]{1,0:T(8,128)(2,1)S(1)} %get-tuple-element.45.block), channel_id=1, source_target_pairs={{0,192},{8,56},{16,208},{24,8},{32,224},{40,24},{48,240},{56,40},{... | collective-permute-start | bytes 552968 | tf_op jit(solution)/shard_map/ppermute | solution.py:102
  16.8 3.2 %collective-permute-done.5.before = bf16[48,1920]{1,0:T(8,128)(2,1)S(1)} collective-permute-done((bf16[48,1920]{1,0:T(8,128)(2,1)S(1)}, bf16[48,1920]{1,0:T(8,128)(2,1)S(1)}, u32[]{:S(2)}, u32[]{:S(2)}) %collective-permute-start.5) | collective-permute-done | bytes 184352 | tf_op jit(solution)/shard_map/ppermute | solution.py:102
  20.2 2.7 %collective-permute-start.9 = (bf16[48,1152]{1,0:T(8,128)(2,1)S(1)}, bf16[48,1152]{1,0:T(8,128)(2,1)S(1)}, u32[]{:S(2)}, u32[]{:S(2)}) collective-permute-start(bf16[48,1152]{1,0:T(8,128)(2,1)S(1)} %get-tuple-element.48.refs_0_), channel_id=1, source_target_pairs={{0,192},{8,56},{16,208},{24,8},{32,224},{40,24},{48,240},{56,40},{... | collective-permute-start | bytes 331784 | tf_op jit(solution)/shard_map/ppermute | solution.py:102
  22.8 2.7 %collective-permute-start.11 = (bf16[48,896]{1,0:T(8,128)(2,1)S(1)}, bf16[48,896]{1,0:T(8,128)(2,1)S(1)}, u32[]{:S(2)}, u32[]{:S(2)}) collective-permute-start(bf16[48,896]{1,0:T(8,128)(2,1)S(1)} %get-tuple-element.46.refs_0_), channel_id=1, source_target_pairs={{0,192},{8,56},{16,208},{24,8},{32,224},{40,24},{48,240},{56,40},{... | collective-permute-start | bytes 258056 | tf_op jit(solution)/shard_map/ppermute | solution.py:102
  28.5 3.6 %collective-permute-start.14 = (bf16[2304,512]{1,0:T(8,128)(2,1)S(1)}, bf16[2304,512]{1,0:T(8,128)(2,1)S(1)}, u32[]{:S(2)}, u32[]{:S(2)}) collective-permute-start(bf16[2304,512]{1,0:T(8,128)(2,1)S(1)} %half_head.1), channel_id=1, source_target_pairs={{0,8},{8,0},{16,24},{24,16},{32,40},{40,32},{48,56},{56,48},{64,72... | collective-permute-start | bytes 7077896 | tf_op jit(solution)/shard_map/ppermute | solution.py:631
  32.0 2.8 %collective-permute-start.20 = (bf16[192,1920]{1,0:T(8,128)(2,1)S(1)}, bf16[192,1920]{1,0:T(8,128)(2,1)S(1)}, u32[]{:S(2)}, u32[]{:S(2)}) collective-permute-start(bf16[192,1920]{1,0:T(8,128)(2,1)S(1)} %join.2.refs_0_), channel_id=1, source_target_pairs={{0,48},{8,200},{16,0},{24,216},{32,16},{40,232},{48,32},{56,248},{... | collective-permute-start | bytes 2211848 | tf_op jit(solution)/shard_map/ppermute | solution.py:102
  34.9 2.7 %collective-permute-start.13 = (bf16[192,2304]{1,0:T(8,128)(2,1)S(1)}, bf16[192,2304]{1,0:T(8,128)(2,1)S(1)}, u32[]{:S(2)}, u32[]{:S(2)}) collective-permute-start(bf16[192,2304]{1,0:T(8,128)(2,1)S(1)} %join.3.wait_ref.refs_0_), channel_id=1, source_target_pairs={{0,48},{8,200},{16,0},{24,216},{32,16},{40,232},{48,32},{56,248},{... | collective-permute-start | bytes 2654216 | tf_op jit(solution)/shard_map/ppermute | solution.py:102
  37.5 5.8 %turn.1 = (bf16[512,3584]{1,0:T(8,128)(2,1)S(1)}, bf16[512,3584]{1,0:T(8,128)(2,1)S(1)}, f32[8,128]{1,0:T(8,128)S(1)}) custom-call(bf16[3584,512]{1,0:T(8,128)(2,1)S(1)} %copy-done, bf16[3584,512]{1,0:T(8,128)(2,1)} %collective-permute-done.7.refs_0_.refs_4_.other_ref.refs_3_), custom_call_target="tpu_custom_call" | custom-call | bytes 29360128 | tf_op jit(solution)/shard_map/turn/pallas_call | solution.py:500
  46.9 4.7 %student_near.1 = (f32[576,512]{1,0:T(8,128)S(1)}, f32[576,512]{1,0:T(8,128)S(1)}, bf16[576,1920]{1,0:T(8,128)(2,1)}) custom-call(s32[3]{0:T(128)S(1)} %pad_add_fusion.pos_ref, bf16[192,1920]{1,0:T(8,128)(2,1)S(1)} %join.2.refs_0_, bf16[192,1920]{1,0:T(8,128)(2,1)S(1)} %collective-permute-done.19.refs_1_.before, ...), custom_call_target="tpu_custom_call" | custom-call | tf_op jit(solution)/shard_map/student_near/pallas_call | solution.py:251
  54.5 2.9 %collective-permute-start.16 = (bf16[192,1152]{1,0:T(8,128)(2,1)S(1)}, bf16[192,1152]{1,0:T(8,128)(2,1)S(1)}, u32[]{:S(2)}, u32[]{:S(2)}) collective-permute-start(bf16[192,1152]{1,0:T(8,128)(2,1)S(1)} %get-tuple-element.50.refs_5_.refs_4_), channel_id=1, source_target_pairs={{0,48},{8,200},{16,0},{24,216},{32,16},{40,232},{48,32},{56,248},{... | collective-permute-start | bytes 1327112 | tf_op jit(solution)/shard_map/ppermute | solution.py:102
  57.7 3.1 %student_far.1 = (f32[192,512]{1,0:T(8,128)S(1)}, f32[192,512]{1,0:T(8,128)S(1)}, bf16[192,1920]{1,0:T(8,128)(2,1)S(1)}) custom-call(s32[3]{0:T(128)S(1)} %pad_add_fusion.pos_ref, bf16[192,1024]{1,0:T(8,128)(2,1)S(1)} %collective-permute-done.21.refs_0_, bf16[192,896]{1,0:T(8,128)(2,1)S(1)} %collective-permute-done.22.refs_1_, ...), custom_call_target="tpu_custom_call" | custom-call | tf_op jit(solution)/shard_map/student_far/pallas_call | solution.py:251
  61.7 4.1 %teacher_near.1 = (f32[576,512]{1,0:T(8,128)S(1)}, f32[576,512]{1,0:T(8,128)S(1)}) custom-call(s32[3]{0:T(128)S(1)} %pad_add_fusion.pos_ref, bf16[192,2304]{1,0:T(8,128)(2,1)S(1)} %join.3.wait_ref.refs_0_, bf16[192,2304]{1,0:T(8,128)(2,1)S(1)} %collective-permute-done.12.before.refs_1_, bf16[192,2304]{1,0:T(8,128)(2,1)S(1)} %collective-permute-done.13.after.refs_2_, ...), custom_call_target="tpu_custom_call" | custom-call | flops 99999997952 | tf_op jit(solution)/shard_map/teacher_near/pallas_call | solution.py:251
  65.9 2.2 %teacher_far.1 = (f32[192,512]{1,0:T(8,128)S(1)}, f32[192,512]{1,0:T(8,128)S(1)}) custom-call(s32[3]{0:T(128)S(1)} %pad_add_fusion.pos_ref, bf16[192,1152]{1,0:T(8,128)(2,1)S(1)} %collective-permute-done.15.refs_0_, bf16[192,1152]{1,0:T(8,128)(2,1)S(1)} %collective-permute-done.16.refs_1_, bf16[4608,512]{1,0:T(8,128)(2,1)S(1)} %bitcast.8, ...), custom_call_target="tpu_custom_call" | custom-call | tf_op jit(solution)/shard_map/teacher_far/pallas_call | solution.py:251
  69.0 3.5 %student_logits.1 = (f32[384,512]{1,0:T(8,128)S(1)}, f32[384,128]{1,0:T(8,128)S(1)}, s32[1,768]{1,0:T(1,128)S(1)}, s32[1,768]{1,0:T(1,128)S(1)}) custom-call(s32[3]{0:T(128)S(1)} %pad_add_fusion.pos_ref, f32[576,512]{1,0:T(8,128)S(1)} %get-tuple-element.56.near, f32[192,512]{1,0:T(8,128)S(1)} %get-tuple-element.60.far, ...), custom_call_target="tpu_custom_call" | custom-call | flops 99999997952 | tf_op jit(solution)/shard_map/student_logits/pallas_call | solution.py:324
  72.5 2.3 %teacher_logits.1 = (f32[384,512]{1,0:T(8,128)S(1)}, f32[32,1,1152]{2,1,0:T(1,128)S(1)}) custom-call(s32[3]{0:T(128)S(1)} %pad_add_fusion.pos_ref, f32[576,512]{1,0:T(8,128)S(1)} %get-tuple-element.51.near, f32[192,512]{1,0:T(8,128)S(1)} %get-tuple-element.53.far, f32[576,512]{1,0:T(8,128)S(1)} %collective-permute-done.17.near_got, ...), custom_call_target="tpu_custom_call" | custom-call | tf_op jit(solution)/shard_map/teacher_logits/pallas_call | solution.py:374
  74.8 14.4 %all_to_all.20.x_ref = f32[32,1,1152]{2,1,0:T(1,128)S(1)} all-to-all(f32[32,1,1152]{2,1,0:T(1,128)S(1)} %get-tuple-element.68), channel_id=1, replica_groups=mesh['dp'=32,'vocab'=8] {'dp'}, dimensions={0} | all-to-all | bytes 294912 | tf_op jit(solution)/shard_map/all_to_all | solution.py:661
  89.5 13.3 %all_to_all.21.x_ref = f32[8,1,1152]{2,1,0:T(1,128)S(1)} all-to-all(f32[8,1,1152]{2,1,0:T(1,128)S(1)} %merge_stats.1), channel_id=1, replica_groups=mesh['dp'=32,'vocab'=8] {'vocab'}, dimensions={0} | all-to-all | bytes 73728 | tf_op jit(solution)/shard_map/all_to_all | solution.py:662
  108.5 5.4 %grad_hidden.1 = bf16[384,3584]{1,0:T(8,128)(2,1)} custom-call(bf16[384,512]{1,0:T(8,128)(2,1)S(1)} %get-tuple-element.73.keep_ref, bf16[384,512]{1,0:T(8,128)(2,1)S(1)} %collective-permute-done.25.got_ref, bf16[512,3584]{1,0:T(8,128)(2,1)S(1)} %get-tuple-element.75.own_w, bf16[512,3584]{1,0:T(8,128)(2,1)S(1)} %get-tuple-element.76.other_w), custom_call_target="tpu_custom_call" | custom-call | tf_op jit(solution)/shard_map/grad_hidden/pallas_call | solution.py:536
  114.0 3.7 %all-to-all-start.2 = ((bf16[4,96,3584]{2,1,0:T(8,128)(2,1)}), bf16[4,96,3584]{2,1,0:T(8,128)(2,1)S(1)}, u32[]{:S(2)}, u32[]{:S(2)}) async-start(bf16[4,96,3584]{2,1,0:T(8,128)(2,1)} %bitcast.9), calls=%async_computation.2 | async-start | bytes 5505024 | tf_op jit(solution)/shard_map/all_to_all | solution.py:667
  122.4 8.3 %grad_head.1 = (bf16[3584,512]{1,0:T(8,128)(2,1)}, f32[8,128]{1,0:T(8,128)S(1)}) custom-call(s32[3]{0:T(128)S(1)} %pad_add_fusion.pos_ref, bf16[576,1920]{1,0:T(8,128)(2,1)} %get-tuple-element.63.near_note.near, bf16[192,1920]{1,0:T(8,128)(2,1)S(1)} %copy-done.4, bf16[576,1920]{1,0:T(8,128)(2,1)} %collective-permute-done.26.near_got, ...), custom_call_target="tpu_custom_call" | custom-call | tf_op jit(solution)/shard_map/grad_head/pallas_call | solution.py:597
  130.8 6.0 %all-to-all-done.2.x_ref = bf16[4,96,3584]{2,1,0:T(8,128)(2,1)S(1)} async-done(((bf16[4,96,3584]{2,1,0:T(8,128)(2,1)}), bf16[4,96,3584]{2,1,0:T(8,128)(2,1)S(1)}, u32[]{:S(2)}, u32[]{:S(2)}) %all-to-all-start.2) | async-done | bytes 2752544 | tf_op jit(solution)/shard_map/all_to_all | solution.py:667
  137.2 25.8 %all_to_all.22 = bf16[32,24,448]{2,1,0:T(8,128)(2,1)S(1)} all-to-all(bf16[32,24,448]{2,1,0:T(8,128)(2,1)S(1)} %sum_parts.1), channel_id=1, replica_groups={{0,1,2,3,4,5,6,7,16,17,18,19,20,21,22,23,32,33,34,35,36,37,38,39,48,49,..., dimensions={0} | all-to-all | bytes 1376256 | tf_op jit(solution)/shard_map/all_to_all | solution.py:672
  (82 shorter events, 29.6 us)
Async XLA Ops:
  0.6 19.4 %collective-permute-start.7 = (bf16[3584,512]{1,0:T(8,128)(2,1)}, bf16[3584,512]{1,0:T(8,128)(2,1)}, u32[]{:S(2)}, u32[]{:S(2)}) collective-permute-start(bf16[3584,512]{1,0:T(8,128)(2,1)} %refs_2_.3), channel_id=1, source_target_pairs={{0,8},{8,0},{16,24},{24,16},{32,40},{40,32},{48,56},{56,48},{64,72... | collective-permute-start | bytes 11010056 | tf_op jit(solution)/shard_map/ppermute | solution.py:631
  4.0 6.6 %collective-permute-start.1 = (bf16[24,3584]{1,0:T(8,128)(2,1)}, bf16[24,3584]{1,0:T(8,128)(2,1)S(1)}, u32[]{:S(2)}, u32[]{:S(2)}) collective-permute-start(bf16[24,3584]{1,0:T(8,128)(2,1)} %s_ref.1), channel_id=1, source_target_pairs={{0,8},{8,0},{16,24},{24,16},{32,40},{40,32},{48,56},{56,48},{64,72... | collective-permute-start | bytes 516104 | tf_op jit(solution)/shard_map/ppermute | solution.py:631
  4.1 6.6 %collective-permute-start.2 = (bf16[24,4608]{1,0:T(8,128)(2,1)}, bf16[24,4608]{1,0:T(8,128)(2,1)S(1)}, u32[]{:S(2)}, u32[]{:S(2)}) collective-permute-start(bf16[24,4608]{1,0:T(8,128)(2,1)} %t_ref.1), channel_id=1, source_target_pairs={{0,8},{8,0},{16,24},{24,16},{32,40},{40,32},{48,56},{56,48},{64,72... | collective-permute-start | bytes 663560 | tf_op jit(solution)/shard_map/ppermute | solution.py:631
  11.3 8.7 %collective-permute-start.3 = (bf16[48,2304]{1,0:T(8,128)(2,1)S(1)}, bf16[48,2304]{1,0:T(8,128)(2,1)S(1)}, u32[]{:S(2)}, u32[]{:S(2)}) collective-permute-start(bf16[48,2304]{1,0:T(8,128)(2,1)S(1)} %get-tuple-element.44.block), channel_id=1, source_target_pairs={{0,64},{8,24},{16,80},{24,40},{32,96},{40,56},{48,112},{56,8},{64,... | collective-permute-start | bytes 663560 | tf_op jit(solution)/shard_map/ppermute | solution.py:102
  11.4 8.6 %collective-permute-start.4 = (bf16[48,2304]{1,0:T(8,128)(2,1)S(1)}, bf16[48,2304]{1,0:T(8,128)(2,1)S(1)}, u32[]{:S(2)}, u32[]{:S(2)}) collective-permute-start(bf16[48,2304]{1,0:T(8,128)(2,1)S(1)} %get-tuple-element.44.block), channel_id=1, source_target_pairs={{0,192},{8,56},{16,208},{24,8},{32,224},{40,24},{48,240},{56,40},{... | collective-permute-start | bytes 663560 | tf_op jit(solution)/shard_map/ppermute | solution.py:102
  14.1 5.9 %collective-permute-start.5 = (bf16[48,1920]{1,0:T(8,128)(2,1)S(1)}, bf16[48,1920]{1,0:T(8,128)(2,1)S(1)}, u32[]{:S(2)}, u32[]{:S(2)}) collective-permute-start(bf16[48,1920]{1,0:T(8,128)(2,1)S(1)} %get-tuple-element.45.block), channel_id=1, source_target_pairs={{0,64},{8,24},{16,80},{24,40},{32,96},{40,56},{48,112},{56,8},{64,... | collective-permute-start | bytes 552968 | tf_op jit(solution)/shard_map/ppermute | solution.py:102
  14.1 5.9 %collective-permute-start.6 = (bf16[48,1920]{1,0:T(8,128)(2,1)S(1)}, bf16[48,1920]{1,0:T(8,128)(2,1)S(1)}, u32[]{:S(2)}, u32[]{:S(2)}) collective-permute-start(bf16[48,1920]{1,0:T(8,128)(2,1)S(1)} %get-tuple-element.45.block), channel_id=1, source_target_pairs={{0,192},{8,56},{16,208},{24,8},{32,224},{40,24},{48,240},{56,40},{... | collective-permute-start | bytes 552968 | tf_op jit(solution)/shard_map/ppermute | solution.py:102
  20.1 7.5 %collective-permute-start.8 = (bf16[48,1152]{1,0:T(8,128)(2,1)S(1)}, bf16[48,1152]{1,0:T(8,128)(2,1)S(1)}, u32[]{:S(2)}, u32[]{:S(2)}) collective-permute-start(bf16[48,1152]{1,0:T(8,128)(2,1)S(1)} %get-tuple-element.47), channel_id=1, source_target_pairs={{0,64},{8,24},{16,80},{24,40},{32,96},{40,56},{48,112},{56,8},{64,... | collective-permute-start | bytes 331784 | tf_op jit(solution)/shard_map/ppermute | solution.py:102
  20.2 7.4 %collective-permute-start.9 = (bf16[48,1152]{1,0:T(8,128)(2,1)S(1)}, bf16[48,1152]{1,0:T(8,128)(2,1)S(1)}, u32[]{:S(2)}, u32[]{:S(2)}) collective-permute-start(bf16[48,1152]{1,0:T(8,128)(2,1)S(1)} %get-tuple-element.48.refs_0_), channel_id=1, source_target_pairs={{0,192},{8,56},{16,208},{24,8},{32,224},{40,24},{48,240},{56,40},{... | collective-permute-start | bytes 331784 | tf_op jit(solution)/shard_map/ppermute | solution.py:102
  22.8 4.7 %collective-permute-start.10 = (bf16[48,1024]{1,0:T(8,128)(2,1)S(1)}, bf16[48,1024]{1,0:T(8,128)(2,1)S(1)}, u32[]{:S(2)}, u32[]{:S(2)}) collective-permute-start(bf16[48,1024]{1,0:T(8,128)(2,1)S(1)} %get-tuple-element.49), channel_id=1, source_target_pairs={{0,64},{8,24},{16,80},{24,40},{32,96},{40,56},{48,112},{56,8},{64,... | collective-permute-start | bytes 294920 | tf_op jit(solution)/shard_map/ppermute | solution.py:102
  28.5 25.8 %collective-permute-start.14 = (bf16[2304,512]{1,0:T(8,128)(2,1)S(1)}, bf16[2304,512]{1,0:T(8,128)(2,1)S(1)}, u32[]{:S(2)}, u32[]{:S(2)}) collective-permute-start(bf16[2304,512]{1,0:T(8,128)(2,1)S(1)} %half_head.1), channel_id=1, source_target_pairs={{0,8},{8,0},{16,24},{24,16},{32,40},{40,32},{48,56},{56,48},{64,72... | collective-permute-start | bytes 7077896 | tf_op jit(solution)/shard_map/ppermute | solution.py:631
  32.0 12.0 %collective-permute-start.19 = (bf16[192,1920]{1,0:T(8,128)(2,1)S(1)}, bf16[192,1920]{1,0:T(8,128)(2,1)S(1)}, u32[]{:S(2)}, u32[]{:S(2)}) collective-permute-start(bf16[192,1920]{1,0:T(8,128)(2,1)S(1)} %join.2.refs_0_), channel_id=1, source_target_pairs={{0,16},{8,72},{16,32},{24,88},{32,48},{40,104},{48,0},{56,120},{64... | collective-permute-start | bytes 2211848 | tf_op jit(solution)/shard_map/ppermute | solution.py:102
  32.0 12.0 %collective-permute-start.20 = (bf16[192,1920]{1,0:T(8,128)(2,1)S(1)}, bf16[192,1920]{1,0:T(8,128)(2,1)S(1)}, u32[]{:S(2)}, u32[]{:S(2)}) collective-permute-start(bf16[192,1920]{1,0:T(8,128)(2,1)S(1)} %join.2.refs_0_), channel_id=1, source_target_pairs={{0,48},{8,200},{16,0},{24,216},{32,16},{40,232},{48,32},{56,248},{... | collective-permute-start | bytes 2211848 | tf_op jit(solution)/shard_map/ppermute | solution.py:102
  34.9 18.6 %collective-permute-start.12 = (bf16[192,2304]{1,0:T(8,128)(2,1)S(1)}, bf16[192,2304]{1,0:T(8,128)(2,1)S(1)}, u32[]{:S(2)}, u32[]{:S(2)}) collective-permute-start(bf16[192,2304]{1,0:T(8,128)(2,1)S(1)} %join.3.wait_ref.refs_0_), channel_id=1, source_target_pairs={{0,16},{8,72},{16,32},{24,88},{32,48},{40,104},{48,0},{56,120},{64... | collective-permute-start | bytes 2654216 | tf_op jit(solution)/shard_map/ppermute | solution.py:102
  34.9 19.4 %collective-permute-start.13 = (bf16[192,2304]{1,0:T(8,128)(2,1)S(1)}, bf16[192,2304]{1,0:T(8,128)(2,1)S(1)}, u32[]{:S(2)}, u32[]{:S(2)}) collective-permute-start(bf16[192,2304]{1,0:T(8,128)(2,1)S(1)} %join.3.wait_ref.refs_0_), channel_id=1, source_target_pairs={{0,48},{8,200},{16,0},{24,216},{32,16},{40,232},{48,32},{56,248},{... | collective-permute-start | bytes 2654216 | tf_op jit(solution)/shard_map/ppermute | solution.py:102
  44.1 13.6 %collective-permute-start.21 = (bf16[192,1024]{1,0:T(8,128)(2,1)S(1)}, bf16[192,1024]{1,0:T(8,128)(2,1)S(1)}, u32[]{:S(2)}, u32[]{:S(2)}) collective-permute-start(bf16[192,1024]{1,0:T(8,128)(2,1)S(1)} %get-tuple-element.58), channel_id=1, source_target_pairs={{0,16},{8,72},{16,32},{24,88},{32,48},{40,104},{48,0},{56,120},{64... | collective-permute-start | bytes 1179656 | tf_op jit(solution)/shard_map/ppermute | solution.py:102
  45.0 12.4 %collective-permute-start.22 = (bf16[192,896]{1,0:T(8,128)(2,1)S(1)}, bf16[192,896]{1,0:T(8,128)(2,1)S(1)}, u32[]{:S(2)}, u32[]{:S(2)}) collective-permute-start(bf16[192,896]{1,0:T(8,128)(2,1)S(1)} %get-tuple-element.59), channel_id=1, source_target_pairs={{0,48},{8,200},{16,0},{24,216},{32,16},{40,232},{48,32},{56,248},{... | collective-permute-start | bytes 1032200 | tf_op jit(solution)/shard_map/ppermute | solution.py:102
  53.5 15.5 %collective-permute-start.23 = (f32[576,512]{1,0:T(8,128)S(1)}, f32[576,512]{1,0:T(8,128)S(1)}, u32[]{:S(2)}, u32[]{:S(2)}) collective-permute-start(f32[576,512]{1,0:T(8,128)S(1)} %get-tuple-element.61), channel_id=1, source_target_pairs={{0,8},{8,0},{16,24},{24,16},{32,40},{40,32},{48,56},{56,48},{64,72... | collective-permute-start | bytes 3538952 | tf_op jit(solution)/shard_map/ppermute | solution.py:631
  54.3 11.6 %collective-permute-start.15 = (bf16[192,1152]{1,0:T(8,128)(2,1)S(1)}, bf16[192,1152]{1,0:T(8,128)(2,1)S(1)}, u32[]{:S(2)}, u32[]{:S(2)}) collective-permute-start(bf16[192,1152]{1,0:T(8,128)(2,1)S(1)} %get-tuple-element.52), channel_id=1, source_target_pairs={{0,16},{8,72},{16,32},{24,88},{32,48},{40,104},{48,0},{56,120},{64... | collective-permute-start | bytes 1327112 | tf_op jit(solution)/shard_map/ppermute | solution.py:102
  54.5 11.4 %collective-permute-start.16 = (bf16[192,1152]{1,0:T(8,128)(2,1)S(1)}, bf16[192,1152]{1,0:T(8,128)(2,1)S(1)}, u32[]{:S(2)}, u32[]{:S(2)}) collective-permute-start(bf16[192,1152]{1,0:T(8,128)(2,1)S(1)} %get-tuple-element.50.refs_5_.refs_4_), channel_id=1, source_target_pairs={{0,48},{8,200},{16,0},{24,216},{32,16},{40,232},{48,32},{56,248},{... | collective-permute-start | bytes 1327112 | tf_op jit(solution)/shard_map/ppermute | solution.py:102
  60.8 8.1 %collective-permute-start.24 = (f32[192,512]{1,0:T(8,128)S(1)}, f32[192,512]{1,0:T(8,128)S(1)}, u32[]{:S(2)}, u32[]{:S(2)}) collective-permute-start(f32[192,512]{1,0:T(8,128)S(1)} %get-tuple-element.62), channel_id=1, source_target_pairs={{0,8},{8,0},{16,24},{24,16},{32,40},{40,32},{48,56},{56,48},{64,72... | collective-permute-start | bytes 1179656 | tf_op jit(solution)/shard_map/ppermute | solution.py:631
  65.8 6.6 %collective-permute-start.17 = (f32[576,512]{1,0:T(8,128)S(1)}, f32[576,512]{1,0:T(8,128)S(1)}, u32[]{:S(2)}, u32[]{:S(2)}) collective-permute-start(f32[576,512]{1,0:T(8,128)S(1)} %get-tuple-element.54), channel_id=1, source_target_pairs={{0,8},{8,0},{16,24},{24,16},{32,40},{40,32},{48,56},{56,48},{64,72... | collective-permute-start | bytes 3538952 | tf_op jit(solution)/shard_map/ppermute | solution.py:631
  107.2 11.0 %collective-permute-start.26 = (bf16[576,1920]{1,0:T(8,128)(2,1)}, bf16[576,1920]{1,0:T(8,128)(2,1)}, u32[]{:S(2)}, u32[]{:S(2)}) collective-permute-start(bf16[576,1920]{1,0:T(8,128)(2,1)} %get-tuple-element.63.near_note.near), channel_id=1, source_target_pairs={{0,8},{8,0},{16,24},{24,16},{32,40},{40,32},{48,56},{56,48},{64,72... | collective-permute-start | bytes 6635528 | tf_op jit(solution)/shard_map/ppermute | solution.py:631
  114.0 22.8 %all-to-all-start.2 = ((bf16[4,96,3584]{2,1,0:T(8,128)(2,1)}), bf16[4,96,3584]{2,1,0:T(8,128)(2,1)S(1)}, u32[]{:S(2)}, u32[]{:S(2)}) async-start(bf16[4,96,3584]{2,1,0:T(8,128)(2,1)} %bitcast.9), calls=%async_computation.2 | async-start | bytes 5505024 | tf_op jit(solution)/shard_map/all_to_all | solution.py:667
  (14 other events, 79.6 us)

commit v6 on v5

--- a/solution.py
+++ b/solution.py
@@ -96,14 +96,18 @@
     return call(join_kernel, "join", parts, [shape], *waits)[0]
 
 
-def gathered(s, t, pos, student_head, teacher_head, other, shards):
+def after(value, wait):
+    return lax.optimization_barrier((value, wait))[0]
+
+
+def gathered(s, t, student_head, teacher_head, other, shards):
     def ways(stage):
         up, down = shifted(stage, 1, shards), shifted(stage, -1, shards)
         return lambda a, b: [lax.ppermute(a, "dp", up), lax.ppermute(b, "dp", down)]
 
     s_cut, t_cut = s.shape[1] // 256 * 128 + 128, t.shape[1] // 2
     one, two = ways(0), ways(1)
-    student_other = other(student_head)
+    student_other = other(after(student_head, s))
     s_near, t_near = one(s, s), one(t, t)
     s_half = cut_halves(*s_near, s_cut, student_other)
     t_half = cut_halves(*t_near, t_cut, s_half[1])
@@ -111,35 +115,13 @@
     s_line = joined([s, *s_near, *s_far], t_half[1])
     t_line = joined([t, *t_near, *t_far], s_line)
     s_near, t_near = two(s_line, s_line), two(t_line, t_line)
-    teacher_other = other(half_for_other(pos, teacher_head, t_line, 3))
+    teacher_other = other(after(teacher_head, t_line))
     *heads, turned_done = turned(student_head, student_other, 7)
     s_half = cut_halves(*s_near, s_cut, t_line, turned_done)
     s_far = two(*s_half)
     t_half = cut_halves(*t_near, t_cut, teacher_other)
     s_pieces, t_pieces = [s_line, *s_near, *s_far], [t_line, *t_near, *two(*t_half)]
     return s_pieces, t_pieces, t_half[1], student_other, teacher_other, heads
-
-
-def half_kernel(pos_ref, w_ref, wait_ref, out_ref):
-    out_ref[...] = w_ref[...]
-
-
-def half_for_other(pos, w, wait, chunks):
-    depth, cols = w.shape[0] // 2, w.shape[1]
-    kb = depth // chunks
-    return pl.pallas_call(
-        half_kernel,
-        grid_spec=pltpu.PrefetchScalarGridSpec(
-            num_scalar_prefetch=1,
-            grid=(chunks,),
-            in_specs=[pl.BlockSpec((kb, cols), lambda k, pos: ((1 - pos[2]) * chunks + k, 0)), AFTER],
-            out_specs=pl.BlockSpec((kb, cols), lambda k, pos: (k, 0)),
-        ),
-        out_shape=jax.ShapeDtypeStruct((depth, cols), w.dtype),
-        compiler_params=params(),
-        cost_estimate=cost(0, 0),
-        name="half_head",
-    )(pos, w, wait)
 
 
 def block_start(pos_ref, i, j, core, size):
@@ -266,6 +248,58 @@
     )(pos, *pieces, own_w, other_w, *waits)
 
 
+def middle_kernel(pos_ref, s_left, s_right, t0, t1, t2, s_w, s_w_other, t_w, t_w_other, *refs):
+    s_own, s_send, s_rows, t_own, t_send, t_rows, s_buf, s_buf_other, t_buf, t_buf_other, sem = refs[-11:]
+
+    def half(w, depth):
+        if w.shape[0] == depth:
+            return w
+        return w.at[pl.ds(pl.multiple_of(pos_ref[2] * depth, 256), depth), :]
+
+    pairs = ((s_w_other, s_buf_other), (s_w, s_buf), (t_w_other, t_buf_other), (t_w, t_buf))
+    loads = [
+        pltpu.make_async_copy(half(w, buf.shape[0]), buf, sem.at[i]) for i, (w, buf) in enumerate(pairs)
+    ]
+    for load in loads:
+        load.start()
+    far_kernel(s_left, s_right, s_rows)
+    depth = s_buf.shape[0]
+    loads[0].wait()
+    s_send[...] = jnp.dot(s_rows[:, :depth], s_buf_other[...], preferred_element_type=f32)
+    loads[1].wait()
+    s_own[...] = jnp.dot(s_rows[:, :depth], s_buf[...], preferred_element_type=f32)
+    near_kernel(t0, t1, t2, t_rows)
+    loads[2].wait()
+    t_send[...] = jnp.dot(t_rows[...], t_buf_other[...], preferred_element_type=f32)
+    loads[3].wait()
+    t_own[...] = jnp.dot(t_rows[...], t_buf[...], preferred_element_type=f32)
+
+
+def middle_logits(pos, s_far, t_near, s_heads, t_heads, notes, *waits):
+    cols = s_heads[0].shape[1]
+    s_n, s_depth = s_far[0].shape[0], s_heads[0].shape[0] // 2
+    t_n, t_depth = 3 * t_near[0].shape[0], t_heads[0].shape[0] // 2
+    args = [*s_far, *t_near]
+    outs = [((s_n, cols), f32)] * 2 + [((s_n, s_depth + notes), bf16)] + [((t_n, cols), f32)] * 2
+    return pl.pallas_call(
+        middle_kernel,
+        grid_spec=pltpu.PrefetchScalarGridSpec(
+            num_scalar_prefetch=1,
+            grid=(1,),
+            in_specs=[once(v.shape) for v in args] + [AFTER] * (4 + len(waits)),
+            out_specs=[whole(shape) for shape, _ in outs],
+            scratch_shapes=[pltpu.VMEM((t_n, t_depth), bf16)]
+            + [pltpu.VMEM((s_depth, cols), bf16)] * 2
+            + [pltpu.VMEM((t_depth, cols), bf16)] * 2
+            + [pltpu.SemaphoreType.DMA((4,))],
+        ),
+        out_shape=[jax.ShapeDtypeStruct(*out) for out in outs],
+        compiler_params=params(24),
+        cost_estimate=cost(1e11, 0),
+        name="middle_logits",
+    )(pos, *args, *s_heads, *t_heads, *waits)
+
+
 def place(out_ref, pos_ref, near, far, near_got, far_got):
     size = near.shape[0] // (3 * SIDE)
     core = pos_ref[2]
@@ -294,11 +328,18 @@
             notes[pl.ds(start, size), :] = note[j * size : (j + 1) * size, :]
     flat = jnp.transpose(notes[...])
     rows, live_rows = notes.shape[0], s_ref.shape[0]
+    n = rows // 128
+    lines = [flat[0:1, j * 128 : (j + 1) * 128] for j in range(n)]
+    live = jnp.concatenate(lines + [jnp.zeros((16 - n, 128), f32)], axis=0)
+    earlier = lax.broadcasted_iota(jnp.int32, (128, 128), 0) < lax.broadcasted_iota(jnp.int32, (128, 128), 1)
+    inside = jnp.dot(live.astype(bf16), earlier.astype(f32).astype(bf16), preferred_element_type=f32)
+    count = jnp.sum(live, axis=1, keepdims=True)
+    base, ranks = jnp.zeros((1, 1), f32), []
+    for j in range(n):
+        ranks.append(jnp.where(lines[j] > 0, inside[j : j + 1, :] + base, float(rows)))
+        base += count[j : j + 1, :]
+    rank = jnp.broadcast_to(jnp.concatenate(ranks, axis=1), (16, rows))
     first = lax.broadcasted_iota(jnp.int32, (rows, rows), 0)
-    earlier = first < lax.broadcasted_iota(jnp.int32, (rows, rows), 1)
-    live = jnp.broadcast_to(flat[0:1, :], (16, rows))
-    rank = jnp.dot(live.astype(bf16), earlier.astype(f32).astype(bf16), preferred_element_type=f32)
-    rank = jnp.where(live > 0, rank, float(rows))
     rank_ref[...] = rank[0:1, :].astype(jnp.int32)
     target = (flat[1:2, :] * 32.0 + flat[2:3, :]).astype(jnp.int32)
     high = jnp.floor(rank / 32.0)
@@ -417,25 +458,6 @@
     )(x)
 
 
-def norm_kernel(x_ref, norm_ref, loss_ref):
-    s_norm, t_norm, cross = merged(x_ref[...])
-    loss_ref[...] = jnp.sum(cross - t_norm + s_norm, keepdims=True) / s_norm.shape[1]
-    norm_ref[...] = jnp.concatenate([s_norm, t_norm], axis=1)
-
-
-def norms(x):
-    n = x.shape[2] // 3
-    return pl.pallas_call(
-        norm_kernel,
-        grid=(1,),
-        in_specs=[once(x.shape)],
-        out_specs=[whole((1, 2 * n)), whole((1, 1))],
-        out_shape=[jax.ShapeDtypeStruct((1, 2 * n), f32), jax.ShapeDtypeStruct((1, 1), f32)],
-        compiler_params=params(),
-        name="norms",
-    )(x)
-
-
 def column(line):
     return jnp.concatenate(
         [
@@ -446,10 +468,13 @@
     )
 
 
-def gap_kernel(grad_scale, tok, pos_ref, s_ref, t_ref, norm_ref, rank_ref, send_ref, keep_ref, own_ref, other_ref, full, part):
+def gap_kernel(
+    grad_scale, tok, pos_ref, s_ref, t_ref, x_ref, rank_ref, send_ref, keep_ref, own_ref, other_ref, loss_ref, full, part
+):
     live, rows = s_ref.shape[0], full.shape[0]
-    norm = norm_ref[...]
-    gap = jnp.exp(s_ref[...] - column(norm[:, :live])) - jnp.exp(t_ref[...] - column(norm[:, live:]))
+    s_norm, t_norm, cross = merged(x_ref[...])
+    loss_ref[...] = jnp.sum(cross - t_norm + s_norm, keepdims=True) / live
+    gap = jnp.exp(s_ref[...] - column(s_norm)) - jnp.exp(t_ref[...] - column(t_norm))
     rank = column(rank_ref[...].astype(f32))
     back = lax.broadcasted_iota(jnp.int32, (rows, live), 1).astype(f32) == rank
     full[...] = jnp.dot(
@@ -472,16 +497,17 @@
                 ref[at : at + size, :] = full[pl.ds(start, size), :].astype(bf16)
 
 
-def logit_gap(pos, s, t, norm, rank, grad_scale, tok):
+def logit_gap(pos, s, t, x, rank, grad_scale, tok):
     cols, rows = s.shape[1], rank.shape[1]
     half = (rows // 2, cols)
-    args = (s, t, norm, rank)
+    args = (s, t, x, rank)
     return pl.pallas_call(
         functools.partial(gap_kernel, grad_scale, tok),
         grid=(1,),
         in_specs=[SMEM] + [once(v.shape) for v in args],
-        out_specs=[whole(half), whole(half), whole((rows, cols)), whole((rows, cols))],
-        out_shape=[jax.ShapeDtypeStruct(v, bf16) for v in (half, half, (rows, cols), (rows, cols))],
+        out_specs=[whole(half), whole(half), whole((rows, cols)), whole((rows, cols)), whole((1, 1))],
+        out_shape=[jax.ShapeDtypeStruct(v, bf16) for v in (half, half, (rows, cols), (rows, cols))]
+        + [jax.ShapeDtypeStruct((1, 1), f32)],
         scratch_shapes=[pltpu.VMEM((rows, cols), f32), pltpu.VMEM(half, f32)],
         compiler_params=params(20),
         name="logit_gap",
@@ -540,7 +566,7 @@
         out_specs=HBM,
         out_shape=pltpu.HBM((rows, depth), bf16),
         scratch_shapes=[pltpu.VMEM((chunks, rows, kb), bf16), pltpu.SemaphoreType.DMA((chunks,))],
-        compiler_params=params(),
+        compiler_params=params(16),
         cost_estimate=cost(0, 0),
         name="grad_hidden",
     )(keep, got, own_w, other_w)
@@ -635,20 +661,23 @@
     own = [table, student_hidden, teacher_hidden]
     a, b = pair(pos, own, [other(v) for v in own], meta)
     s_pieces, t_pieces, t_last_half, student_other, teacher_other, heads = gathered(
-        a, b, pos, student_head, teacher_head, other, shards
+        a, b, student_head, teacher_head, other, shards
     )
 
     s_near, s_send, near = partial_logits(
         near_kernel, "student_near", pos, s_pieces[:3], meta, student_head, student_other
     )
     s_near_got = other(s_send)
-    t_near, t_send = partial_logits(
-        near_kernel, "teacher_near", pos, t_pieces[:3], 0, teacher_head, teacher_other, t_last_half, flops=1e11
+    s_far, s_send, far, t_near, t_send = middle_logits(
+        pos,
+        s_pieces[3:],
+        t_pieces[:3],
+        (student_head, student_other),
+        (teacher_head, teacher_other),
+        meta,
+        t_last_half,
     )
     t_near_got = other(t_send)
-    s_far, s_send, far = partial_logits(
-        far_kernel, "student_far", pos, s_pieces[3:], meta, student_head, student_other, t_last_half
-    )
     s, s_lse, slot, rank = student_logits(
         pos, s_near, s_far, s_near_got, other(s_send), near, far, s_half, meta
     )
@@ -660,14 +689,16 @@
 
     stats = lax.all_to_all(stats, "dp", 0, 0)
     stats = lax.all_to_all(merge(stats, slices), "vocab", 0, 0)
-    norm, loss = norms(stats)
-
-    send, keep, own_g, other_g = logit_gap(pos, s, t, norm, rank, loss_scale / live_total, tok)
-    mine = grad_hidden_of(keep, other(send), *heads, 7)
+
+    send, keep, own_g, other_g, loss = logit_gap(pos, s, t, stats, rank, loss_scale / live_total, tok)
+    got = other(send)
+    mine = grad_hidden_of(keep, got, *heads, 2)
     parts = lax.all_to_all(
         mine.reshape(SIDE, SIDE * tok, depth), "dp", 0, 0, axis_index_groups=lines(0)
     )
-    grad_head, done = grad_head_of(pos, near, far, other(near), other(far), own_g, other_g, s_half)
+    grad_head, done = grad_head_of(
+        pos, near, far, other(after(near, mine)), other(after(far, mine)), own_g, other_g, s_half
+    )
     groups = [[i * slices + z for i in line for z in range(slices)] for line in lines(1)]
     parts = lax.all_to_all(summed(parts, slices, done), ("dp", "vocab"), 0, 0, axis_index_groups=groups)
     grad_hidden = jnp.sum(parts.astype(f32), axis=0).astype(bf16)

time: 164 us -> 160 us (0.976)
  Pallas kernels: 45 us -> 37.6 us
  waiting for transfers between devices: 18.9 us -> 21.7 us
    pallas_call x4 -> x2, Pallas kernels: 14.1 us -> 5.81 us  [partial_logits(): pl.pallas_call(functools.partial(logits_kernel, kernel, len(pieces)), gri...]
    ppermute x16, waiting for transfers between devices: 8.13 us -> 12.3 us  [ways(): return lambda a, b: [lax.ppermute(a, 'dp', up), lax.ppermute(b, 'dp', down)]]
    pallas_call x2 -> x1, Pallas kernels: 1.45 us -> 5.48 us  [middle_logits(): pl.pallas_call(middle_kernel, grid_spec=pltpu.PrefetchScalarGridSpec(num_...]
    pallas_call x1, Pallas kernels: 5.77 us -> 2.76 us  [turned(): pl.pallas_call(turn_kernel, grid=(chunks,), in_specs=[pl.BlockSpec((kb, c...]
    unnamed x18 -> x16, local copies, waits for them, and re-layouts: 4.13 us -> 4.12 us
  transfers between devices with their start and end apart: 29 -> 29, of which waited for: 11 -> 9; matrix products, arithmetic and copies ran while one was open for 0% -> 1% of each run, Pallas kernels for 24% -> 17%
where the time goes in v6:
time: 160 us; the launch traced here: 159 us
  blocking collectives  53.3 us (33%)
  starting transfers between devices  38.7 us (24%)
  Pallas kernels  37.6 us (24%)
  waiting for transfers between devices  21.7 us (14%)
  local copies, waits for them, and re-layouts  4.13 us (3%)
  between operations  2.19 us (1%)
    all_to_all x1, blocking collectives, per_device(): lax.all_to_all(summed(parts, slices, done), ('dp', 'vocab'), 0, 0, axis_i...  25.4 us
    ppermute x16, starting transfers between devices, ways(): return lambda a, b: [lax.ppermute(a, 'dp', up), lax.ppermute(b, 'dp', down)]  22.1 us
    all_to_all x1, blocking collectives, per_device(): stats = lax.all_to_all(stats, 'dp', 0, 0)  14.6 us
    all_to_all x1, blocking collectives, per_device(): stats = lax.all_to_all(merge(stats, slices), 'vocab', 0, 0)  13.4 us
    ppermute x12, starting transfers between devices, per_device(): other = lambda v: lax.ppermute(v, 'dp', swap)  12.9 us
    ppermute x16, waiting for transfers between devices, ways(): return lambda a, b: [lax.ppermute(a, 'dp', up), lax.ppermute(b, 'dp', down)]  12.3 us
    pallas_call x1, Pallas kernels, grad_head_of(): pl.pallas_call(head_kernel, grid_spec=pltpu.PrefetchScalarGridSpec(num_sc...  8.33 us
    pallas_call x2, Pallas kernels, partial_logits(): pl.pallas_call(functools.partial(logits_kernel, kernel, len(pieces)), gri...  5.81 us
  transfers between devices with their start and end apart: 29, of which 9 were waited for; matrix products, arithmetic and copies ran while one was open for 1% of the time, Pallas kernels for 17%

profile of v6, /device:TPU:1, one launch (start us, length us, event | category | flops | bytes accessed | tf_op | source)
XLA Modules:
  0.0 159.2 jit_solution(13352641488053879617)
XLA Ops:
  0.6 3.3 %collective-permute-start.2 = (bf16[24,4608]{1,0:T(8,128)(2,1)}, bf16[24,4608]{1,0:T(8,128)(2,1)S(1)}, u32[]{:S(2)}, u32[]{:S(2)}) collective-permute-start(bf16[24,4608]{1,0:T(8,128)(2,1)} %t_ref.1), channel_id=1, source_target_pairs={{0,8},{8,0},{16,24},{24,16},{32,40},{40,32},{48,56},{56,48},{64,72... | collective-permute-start | bytes 663560 | tf_op jit(solution)/shard_map/ppermute | solution.py:657
  10.0 2.7 %collective-permute-start.9 = (bf16[48,2304]{1,0:T(8,128)(2,1)S(1)}, bf16[48,2304]{1,0:T(8,128)(2,1)S(1)}, u32[]{:S(2)}, u32[]{:S(2)}) collective-permute-start(bf16[48,2304]{1,0:T(8,128)(2,1)S(1)} %get-tuple-element.51.block), channel_id=1, source_target_pairs={{0,192},{8,56},{16,208},{24,8},{32,224},{40,24},{48,240},{56,40},{... | collective-permute-start | bytes 663560 | tf_op jit(solution)/shard_map/ppermute | solution.py:106
  12.7 2.7 %collective-permute-start.4 = (bf16[48,1920]{1,0:T(8,128)(2,1)S(1)}, bf16[48,1920]{1,0:T(8,128)(2,1)S(1)}, u32[]{:S(2)}, u32[]{:S(2)}) collective-permute-start(bf16[48,1920]{1,0:T(8,128)(2,1)S(1)} %get-tuple-element.47.block), channel_id=1, source_target_pairs={{0,192},{8,56},{16,208},{24,8},{32,224},{40,24},{48,240},{56,40},{... | collective-permute-start | bytes 552968 | tf_op jit(solution)/shard_map/ppermute | solution.py:106
  15.4 3.2 %collective-permute-done.3.before = bf16[48,1920]{1,0:T(8,128)(2,1)S(1)} collective-permute-done((bf16[48,1920]{1,0:T(8,128)(2,1)S(1)}, bf16[48,1920]{1,0:T(8,128)(2,1)S(1)}, u32[]{:S(2)}, u32[]{:S(2)}) %collective-permute-start.3) | collective-permute-done | bytes 184352 | tf_op jit(solution)/shard_map/ppermute | solution.py:106
  18.8 2.7 %collective-permute-start.13 = (bf16[48,1152]{1,0:T(8,128)(2,1)S(1)}, bf16[48,1152]{1,0:T(8,128)(2,1)S(1)}, u32[]{:S(2)}, u32[]{:S(2)}) collective-permute-start(bf16[48,1152]{1,0:T(8,128)(2,1)S(1)} %get-tuple-element.52.refs_0_), channel_id=1, source_target_pairs={{0,192},{8,56},{16,208},{24,8},{32,224},{40,24},{48,240},{56,40},{... | collective-permute-start | bytes 331784 | tf_op jit(solution)/shard_map/ppermute | solution.py:106
  21.4 2.7 %collective-permute-start.7 = (bf16[48,896]{1,0:T(8,128)(2,1)S(1)}, bf16[48,896]{1,0:T(8,128)(2,1)S(1)}, u32[]{:S(2)}, u32[]{:S(2)}) collective-permute-start(bf16[48,896]{1,0:T(8,128)(2,1)S(1)} %get-tuple-element.50.refs_0_), channel_id=1, source_target_pairs={{0,192},{8,56},{16,208},{24,8},{32,224},{40,24},{48,240},{56,40},{... | collective-permute-start | bytes 258056 | tf_op jit(solution)/shard_map/ppermute | solution.py:106
  26.3 3.7 %collective-permute-start.18 = (bf16[4608,512]{1,0:T(8,128)(2,1)S(1)}, bf16[4608,512]{1,0:T(8,128)(2,1)S(1)}, u32[]{:S(2)}, u32[]{:S(2)}) collective-permute-start(bf16[4608,512]{1,0:T(8,128)(2,1)S(1)} %copy-done.1), channel_id=1, source_target_pairs={{0,8},{8,0},{16,24},{24,16},{32,40},{40,32},{48,56},{56,48},{64,72... | collective-permute-start | bytes 14155784 | tf_op jit(solution)/shard_map/ppermute | solution.py:657
  30.0 2.8 %collective-permute-start.11 = (bf16[192,1920]{1,0:T(8,128)(2,1)S(1)}, bf16[192,1920]{1,0:T(8,128)(2,1)S(1)}, u32[]{:S(2)}, u32[]{:S(2)}) collective-permute-start(bf16[192,1920]{1,0:T(8,128)(2,1)S(1)} %join.2.refs_0_), channel_id=1, source_target_pairs={{0,48},{8,200},{16,0},{24,216},{32,16},{40,232},{48,32},{56,248},{... | collective-permute-start | bytes 2211848 | tf_op jit(solution)/shard_map/ppermute | solution.py:106
  32.8 2.7 %collective-permute-start.17 = (bf16[192,2304]{1,0:T(8,128)(2,1)S(1)}, bf16[192,2304]{1,0:T(8,128)(2,1)S(1)}, u32[]{:S(2)}, u32[]{:S(2)}) collective-permute-start(bf16[192,2304]{1,0:T(8,128)(2,1)S(1)} %join.3.refs_0_.t0), channel_id=1, source_target_pairs={{0,48},{8,200},{16,0},{24,216},{32,16},{40,232},{48,32},{56,248},{... | collective-permute-start | bytes 2654216 | tf_op jit(solution)/shard_map/ppermute | solution.py:106
  35.5 2.8 %turn.1 = (bf16[512,3584]{1,0:T(8,128)(2,1)S(1)}, bf16[512,3584]{1,0:T(8,128)(2,1)S(1)}, f32[8,128]{1,0:T(8,128)S(1)}) custom-call(bf16[3584,512]{1,0:T(8,128)(2,1)S(1)} %copy-done, bf16[3584,512]{1,0:T(8,128)(2,1)S(1)} %collective-permute-done.5.refs_0_.refs_4_.other_ref.s_w_other), custom_call_target="tpu_custom_call" | custom-call | bytes 29360128 | tf_op jit(solution)/shard_map/turn/pallas_call | solution.py:526
  38.3 3.7 %collective-permute-done.10.refs_1_.before = bf16[192,1920]{1,0:T(8,128)(2,1)S(1)} collective-permute-done((bf16[192,1920]{1,0:T(8,128)(2,1)S(1)}, bf16[192,1920]{1,0:T(8,128)(2,1)S(1)}, u32[]{:S(2)}, u32[]{:S(2)}) %collective-permute-start.10) | collective-permute-done | bytes 737312 | tf_op jit(solution)/shard_map/ppermute | solution.py:106
  44.8 3.6 %student_near.1 = (f32[576,512]{1,0:T(8,128)S(1)}, f32[576,512]{1,0:T(8,128)S(1)}, bf16[576,1920]{1,0:T(8,128)(2,1)}) custom-call(s32[3]{0:T(128)S(1)} %pad_add_fusion.pos_ref, bf16[192,1920]{1,0:T(8,128)(2,1)S(1)} %join.2.refs_0_, bf16[192,1920]{1,0:T(8,128)(2,1)S(1)} %collective-permute-done.10.refs_1_.before, ...), custom_call_target="tpu_custom_call" | custom-call | tf_op jit(solution)/shard_map/student_near/pallas_call | solution.py:233
  48.5 3.0 %collective-permute-done.16.before.t1 = bf16[192,2304]{1,0:T(8,128)(2,1)S(1)} collective-permute-done((bf16[192,2304]{1,0:T(8,128)(2,1)S(1)}, bf16[192,2304]{1,0:T(8,128)(2,1)S(1)}, u32[]{:S(2)}, u32[]{:S(2)}) %collective-permute-start.16) | collective-permute-done | bytes 884768 | tf_op jit(solution)/shard_map/ppermute | solution.py:106
  52.4 2.9 %collective-permute-start.22 = (bf16[192,1152]{1,0:T(8,128)(2,1)S(1)}, bf16[192,1152]{1,0:T(8,128)(2,1)S(1)}, u32[]{:S(2)}, u32[]{:S(2)}) collective-permute-start(bf16[192,1152]{1,0:T(8,128)(2,1)S(1)} %get-tuple-element.59.refs_0_), channel_id=1, source_target_pairs={{0,48},{8,200},{16,0},{24,216},{32,16},{40,232},{48,32},{56,248},{... | collective-permute-start | bytes 1327112 | tf_op jit(solution)/shard_map/ppermute | solution.py:106
  55.6 5.5 %middle_logits.1 = (f32[192,512]{1,0:T(8,128)S(1)}, f32[192,512]{1,0:T(8,128)S(1)}, bf16[192,1920]{1,0:T(8,128)(2,1)S(1)}, f32[576,512]{1,0:T(8,128)S(1)}, f32[576,512]{1,0:T(8,128)S(1)}) custom-call(s32[3]{0:T(128)S(1)} %pad_add_fusion.pos_ref, bf16[192,1024]{1,0:T(8,128)(2,1)S(1)} %collective-permute-done.14.s_left, ...), custom_call_target="tpu_custom_call" | custom-call | flops 99999997952 | tf_op jit(solution)/shard_map/middle_logits/pallas_call | solution.py:284
  65.1 3.4 %student_logits.1 = (f32[384,512]{1,0:T(8,128)S(1)}, f32[384,128]{1,0:T(8,128)S(1)}, s32[1,768]{1,0:T(1,128)S(1)}, s32[1,768]{1,0:T(1,128)S(1)}) custom-call(s32[3]{0:T(128)S(1)} %pad_add_fusion.pos_ref, f32[576,512]{1,0:T(8,128)S(1)} %get-tuple-element.53.near, f32[192,512]{1,0:T(8,128)S(1)} %get-tuple-element.60.far, ...), custom_call_target="tpu_custom_call" | custom-call | flops 99999997952 | tf_op jit(solution)/shard_map/student_logits/pallas_call | solution.py:365
  70.9 14.6 %all_to_all.20.x_ref = f32[32,1,1152]{2,1,0:T(1,128)S(1)} all-to-all(f32[32,1,1152]{2,1,0:T(1,128)S(1)} %get-tuple-element.74), channel_id=1, replica_groups=mesh['dp'=32,'vocab'=8] {'dp'}, dimensions={0} | all-to-all | bytes 294912 | tf_op jit(solution)/shard_map/all_to_all | solution.py:690
  85.7 13.4 %all_to_all.21.x_ref = f32[8,1,1152]{2,1,0:T(1,128)S(1)} all-to-all(f32[8,1,1152]{2,1,0:T(1,128)S(1)} %merge_stats.1), channel_id=1, replica_groups=mesh['dp'=32,'vocab'=8] {'vocab'}, dimensions={0} | all-to-all | bytes 73728 | tf_op jit(solution)/shard_map/all_to_all | solution.py:691
  99.0 2.4 %logit_gap.1 = (bf16[384,512]{1,0:T(8,128)(2,1)S(1)}, bf16[384,512]{1,0:T(8,128)(2,1)S(1)}, bf16[768,512]{1,0:T(8,128)(2,1)S(1)}, bf16[768,512]{1,0:T(8,128)(2,1)S(1)}, f32[1,1]{1,0:T(1,128)}) custom-call(s32[3]{0:T(128)S(1)} %pad_add_fusion.pos_ref, f32[384,512]{1,0:T(8,128)S(1)} %get-tuple-element.65.s_ref, f32[384,512]{1,0:T(8,128)S(1)} %get-tuple-element.73.t_ref, ...), custom_call_target="tpu_custom_call" | custom-call | tf_op jit(solution)/shard_map/logit_gap/pallas_call | solution.py:504
  104.5 4.9 %grad_hidden.1 = bf16[384,3584]{1,0:T(8,128)(2,1)} custom-call(bf16[384,512]{1,0:T(8,128)(2,1)S(1)} %get-tuple-element.77.keep_ref, bf16[384,512]{1,0:T(8,128)(2,1)S(1)} %collective-permute-done.25.got_ref, bf16[512,3584]{1,0:T(8,128)(2,1)S(1)} %get-tuple-element.79.own_w, bf16[512,3584]{1,0:T(8,128)(2,1)S(1)} %get-tuple-element.80.other_w), custom_call_target="tpu_custom_call" | custom-call | tf_op jit(solution)/shard_map/grad_hidden/pallas_call | solution.py:562
  109.9 3.7 %all-to-all-start.2 = ((bf16[4,96,3584]{2,1,0:T(8,128)(2,1)}), bf16[4,96,3584]{2,1,0:T(8,128)(2,1)S(1)}, u32[]{:S(2)}, u32[]{:S(2)}) async-start(bf16[4,96,3584]{2,1,0:T(8,128)(2,1)} %bitcast.7), calls=%async_computation.2 | async-start | bytes 5505024 | tf_op jit(solution)/shard_map/all_to_all | solution.py:696
  118.6 8.3 %grad_head.1 = (bf16[3584,512]{1,0:T(8,128)(2,1)}, f32[8,128]{1,0:T(8,128)S(1)}) custom-call(s32[3]{0:T(128)S(1)} %pad_add_fusion.pos_ref, bf16[576,1920]{1,0:T(8,128)(2,1)} %get-tuple-element.81.near_note.near, bf16[192,1920]{1,0:T(8,128)(2,1)S(1)} %copy-done.5, bf16[576,1920]{1,0:T(8,128)(2,1)} %collective-permute-done.26.near_got, ...), custom_call_target="tpu_custom_call" | custom-call | tf_op jit(solution)/shard_map/grad_head/pallas_call | solution.py:623
  126.9 5.8 %all-to-all-done.2.x_ref = bf16[4,96,3584]{2,1,0:T(8,128)(2,1)S(1)} async-done(((bf16[4,96,3584]{2,1,0:T(8,128)(2,1)}), bf16[4,96,3584]{2,1,0:T(8,128)(2,1)S(1)}, u32[]{:S(2)}, u32[]{:S(2)}) %all-to-all-start.2) | async-done | bytes 2752544 | tf_op jit(solution)/shard_map/all_to_all | solution.py:696
  133.1 25.4 %all_to_all.22 = bf16[32,24,448]{2,1,0:T(8,128)(2,1)S(1)} all-to-all(bf16[32,24,448]{2,1,0:T(8,128)(2,1)S(1)} %sum_parts.1), channel_id=1, replica_groups={{0,1,2,3,4,5,6,7,16,17,18,19,20,21,22,23,32,33,34,35,36,37,38,39,48,49,..., dimensions={0} | all-to-all | bytes 1376256 | tf_op jit(solution)/shard_map/all_to_all | solution.py:703
  (76 shorter events, 27.5 us)
Async XLA Ops:
  0.6 8.5 %collective-permute-start.2 = (bf16[24,4608]{1,0:T(8,128)(2,1)}, bf16[24,4608]{1,0:T(8,128)(2,1)S(1)}, u32[]{:S(2)}, u32[]{:S(2)}) collective-permute-start(bf16[24,4608]{1,0:T(8,128)(2,1)} %t_ref.1), channel_id=1, source_target_pairs={{0,8},{8,0},{16,24},{24,16},{32,40},{40,32},{48,56},{56,48},{64,72... | collective-permute-start | bytes 663560 | tf_op jit(solution)/shard_map/ppermute | solution.py:657
  4.0 5.1 %collective-permute-start.1 = (bf16[24,3584]{1,0:T(8,128)(2,1)}, bf16[24,3584]{1,0:T(8,128)(2,1)S(1)}, u32[]{:S(2)}, u32[]{:S(2)}) collective-permute-start(bf16[24,3584]{1,0:T(8,128)(2,1)} %s_ref.1), channel_id=1, source_target_pairs={{0,8},{8,0},{16,24},{24,16},{32,40},{40,32},{48,56},{56,48},{64,72... | collective-permute-start | bytes 516104 | tf_op jit(solution)/shard_map/ppermute | solution.py:657
  9.8 8.8 %collective-permute-start.5 = (bf16[3584,512]{1,0:T(8,128)(2,1)}, bf16[3584,512]{1,0:T(8,128)(2,1)S(1)}, u32[]{:S(2)}, u32[]{:S(2)}) collective-permute-start(bf16[3584,512]{1,0:T(8,128)(2,1)} %s_w.1), channel_id=1, source_target_pairs={{0,8},{8,0},{16,24},{24,16},{32,40},{40,32},{48,56},{56,48},{64,72... | collective-permute-start | bytes 11010056 | tf_op jit(solution)/shard_map/ppermute | solution.py:657
  10.0 8.6 %collective-permute-start.8 = (bf16[48,2304]{1,0:T(8,128)(2,1)S(1)}, bf16[48,2304]{1,0:T(8,128)(2,1)S(1)}, u32[]{:S(2)}, u32[]{:S(2)}) collective-permute-start(bf16[48,2304]{1,0:T(8,128)(2,1)S(1)} %get-tuple-element.51.block), channel_id=1, source_target_pairs={{0,64},{8,24},{16,80},{24,40},{32,96},{40,56},{48,112},{56,8},{64,... | collective-permute-start | bytes 663560 | tf_op jit(solution)/shard_map/ppermute | solution.py:106
  10.0 8.6 %collective-permute-start.9 = (bf16[48,2304]{1,0:T(8,128)(2,1)S(1)}, bf16[48,2304]{1,0:T(8,128)(2,1)S(1)}, u32[]{:S(2)}, u32[]{:S(2)}) collective-permute-start(bf16[48,2304]{1,0:T(8,128)(2,1)S(1)} %get-tuple-element.51.block), channel_id=1, source_target_pairs={{0,192},{8,56},{16,208},{24,8},{32,224},{40,24},{48,240},{56,40},{... | collective-permute-start | bytes 663560 | tf_op jit(solution)/shard_map/ppermute | solution.py:106
  12.7 5.9 %collective-permute-start.3 = (bf16[48,1920]{1,0:T(8,128)(2,1)S(1)}, bf16[48,1920]{1,0:T(8,128)(2,1)S(1)}, u32[]{:S(2)}, u32[]{:S(2)}) collective-permute-start(bf16[48,1920]{1,0:T(8,128)(2,1)S(1)} %get-tuple-element.47.block), channel_id=1, source_target_pairs={{0,64},{8,24},{16,80},{24,40},{32,96},{40,56},{48,112},{56,8},{64,... | collective-permute-start | bytes 552968 | tf_op jit(solution)/shard_map/ppermute | solution.py:106
  12.7 5.9 %collective-permute-start.4 = (bf16[48,1920]{1,0:T(8,128)(2,1)S(1)}, bf16[48,1920]{1,0:T(8,128)(2,1)S(1)}, u32[]{:S(2)}, u32[]{:S(2)}) collective-permute-start(bf16[48,1920]{1,0:T(8,128)(2,1)S(1)} %get-tuple-element.47.block), channel_id=1, source_target_pairs={{0,192},{8,56},{16,208},{24,8},{32,224},{40,24},{48,240},{56,40},{... | collective-permute-start | bytes 552968 | tf_op jit(solution)/shard_map/ppermute | solution.py:106
  18.7 7.5 %collective-permute-start.12 = (bf16[48,1152]{1,0:T(8,128)(2,1)S(1)}, bf16[48,1152]{1,0:T(8,128)(2,1)S(1)}, u32[]{:S(2)}, u32[]{:S(2)}) collective-permute-start(bf16[48,1152]{1,0:T(8,128)(2,1)S(1)} %get-tuple-element.54), channel_id=1, source_target_pairs={{0,64},{8,24},{16,80},{24,40},{32,96},{40,56},{48,112},{56,8},{64,... | collective-permute-start | bytes 331784 | tf_op jit(solution)/shard_map/ppermute | solution.py:106
  18.8 7.4 %collective-permute-start.13 = (bf16[48,1152]{1,0:T(8,128)(2,1)S(1)}, bf16[48,1152]{1,0:T(8,128)(2,1)S(1)}, u32[]{:S(2)}, u32[]{:S(2)}) collective-permute-start(bf16[48,1152]{1,0:T(8,128)(2,1)S(1)} %get-tuple-element.52.refs_0_), channel_id=1, source_target_pairs={{0,192},{8,56},{16,208},{24,8},{32,224},{40,24},{48,240},{56,40},{... | collective-permute-start | bytes 331784 | tf_op jit(solution)/shard_map/ppermute | solution.py:106
  21.4 4.7 %collective-permute-start.6 = (bf16[48,1024]{1,0:T(8,128)(2,1)S(1)}, bf16[48,1024]{1,0:T(8,128)(2,1)S(1)}, u32[]{:S(2)}, u32[]{:S(2)}) collective-permute-start(bf16[48,1024]{1,0:T(8,128)(2,1)S(1)} %get-tuple-element.49), channel_id=1, source_target_pairs={{0,64},{8,24},{16,80},{24,40},{32,96},{40,56},{48,112},{56,8},{64,... | collective-permute-start | bytes 294920 | tf_op jit(solution)/shard_map/ppermute | solution.py:106
  21.4 4.2 %collective-permute-start.7 = (bf16[48,896]{1,0:T(8,128)(2,1)S(1)}, bf16[48,896]{1,0:T(8,128)(2,1)S(1)}, u32[]{:S(2)}, u32[]{:S(2)}) collective-permute-start(bf16[48,896]{1,0:T(8,128)(2,1)S(1)} %get-tuple-element.50.refs_0_), channel_id=1, source_target_pairs={{0,192},{8,56},{16,208},{24,8},{32,224},{40,24},{48,240},{56,40},{... | collective-permute-start | bytes 258056 | tf_op jit(solution)/shard_map/ppermute | solution.py:106
  26.3 25.9 %collective-permute-start.18 = (bf16[4608,512]{1,0:T(8,128)(2,1)S(1)}, bf16[4608,512]{1,0:T(8,128)(2,1)S(1)}, u32[]{:S(2)}, u32[]{:S(2)}) collective-permute-start(bf16[4608,512]{1,0:T(8,128)(2,1)S(1)} %copy-done.1), channel_id=1, source_target_pairs={{0,8},{8,0},{16,24},{24,16},{32,40},{40,32},{48,56},{56,48},{64,72... | collective-permute-start | bytes 14155784 | tf_op jit(solution)/shard_map/ppermute | solution.py:657
  30.0 12.0 %collective-permute-start.10 = (bf16[192,1920]{1,0:T(8,128)(2,1)S(1)}, bf16[192,1920]{1,0:T(8,128)(2,1)S(1)}, u32[]{:S(2)}, u32[]{:S(2)}) collective-permute-start(bf16[192,1920]{1,0:T(8,128)(2,1)S(1)} %join.2.refs_0_), channel_id=1, source_target_pairs={{0,16},{8,72},{16,32},{24,88},{32,48},{40,104},{48,0},{56,120},{64... | collective-permute-start | bytes 2211848 | tf_op jit(solution)/shard_map/ppermute | solution.py:106
  30.0 12.0 %collective-permute-start.11 = (bf16[192,1920]{1,0:T(8,128)(2,1)S(1)}, bf16[192,1920]{1,0:T(8,128)(2,1)S(1)}, u32[]{:S(2)}, u32[]{:S(2)}) collective-permute-start(bf16[192,1920]{1,0:T(8,128)(2,1)S(1)} %join.2.refs_0_), channel_id=1, source_target_pairs={{0,48},{8,200},{16,0},{24,216},{32,16},{40,232},{48,32},{56,248},{... | collective-permute-start | bytes 2211848 | tf_op jit(solution)/shard_map/ppermute | solution.py:106
  32.8 18.6 %collective-permute-start.16 = (bf16[192,2304]{1,0:T(8,128)(2,1)S(1)}, bf16[192,2304]{1,0:T(8,128)(2,1)S(1)}, u32[]{:S(2)}, u32[]{:S(2)}) collective-permute-start(bf16[192,2304]{1,0:T(8,128)(2,1)S(1)} %join.3.refs_0_.t0), channel_id=1, source_target_pairs={{0,16},{8,72},{16,32},{24,88},{32,48},{40,104},{48,0},{56,120},{64... | collective-permute-start | bytes 2654216 | tf_op jit(solution)/shard_map/ppermute | solution.py:106
  32.8 19.4 %collective-permute-start.17 = (bf16[192,2304]{1,0:T(8,128)(2,1)S(1)}, bf16[192,2304]{1,0:T(8,128)(2,1)S(1)}, u32[]{:S(2)}, u32[]{:S(2)}) collective-permute-start(bf16[192,2304]{1,0:T(8,128)(2,1)S(1)} %join.3.refs_0_.t0), channel_id=1, source_target_pairs={{0,48},{8,200},{16,0},{24,216},{32,16},{40,232},{48,32},{56,248},{... | collective-permute-start | bytes 2654216 | tf_op jit(solution)/shard_map/ppermute | solution.py:106
  42.0 13.6 %collective-permute-start.14 = (bf16[192,1024]{1,0:T(8,128)(2,1)S(1)}, bf16[192,1024]{1,0:T(8,128)(2,1)S(1)}, u32[]{:S(2)}, u32[]{:S(2)}) collective-permute-start(bf16[192,1024]{1,0:T(8,128)(2,1)S(1)} %get-tuple-element.56), channel_id=1, source_target_pairs={{0,16},{8,72},{16,32},{24,88},{32,48},{40,104},{48,0},{56,120},{64... | collective-permute-start | bytes 1179656 | tf_op jit(solution)/shard_map/ppermute | solution.py:106
  42.9 12.4 %collective-permute-start.15 = (bf16[192,896]{1,0:T(8,128)(2,1)S(1)}, bf16[192,896]{1,0:T(8,128)(2,1)S(1)}, u32[]{:S(2)}, u32[]{:S(2)}) collective-permute-start(bf16[192,896]{1,0:T(8,128)(2,1)S(1)} %get-tuple-element.57), channel_id=1, source_target_pairs={{0,48},{8,200},{16,0},{24,216},{32,16},{40,232},{48,32},{56,248},{... | collective-permute-start | bytes 1032200 | tf_op jit(solution)/shard_map/ppermute | solution.py:106
  51.4 13.6 %collective-permute-start.19 = (f32[576,512]{1,0:T(8,128)S(1)}, f32[576,512]{1,0:T(8,128)S(1)}, u32[]{:S(2)}, u32[]{:S(2)}) collective-permute-start(f32[576,512]{1,0:T(8,128)S(1)} %get-tuple-element.61), channel_id=1, source_target_pairs={{0,8},{8,0},{16,24},{24,16},{32,40},{40,32},{48,56},{56,48},{64,72... | collective-permute-start | bytes 3538952 | tf_op jit(solution)/shard_map/ppermute | solution.py:657
  52.3 9.8 %collective-permute-start.21 = (bf16[192,1152]{1,0:T(8,128)(2,1)S(1)}, bf16[192,1152]{1,0:T(8,128)(2,1)S(1)}, u32[]{:S(2)}, u32[]{:S(2)}) collective-permute-start(bf16[192,1152]{1,0:T(8,128)(2,1)S(1)} %get-tuple-element.67), channel_id=1, source_target_pairs={{0,16},{8,72},{16,32},{24,88},{32,48},{40,104},{48,0},{56,120},{64... | collective-permute-start | bytes 1327112 | tf_op jit(solution)/shard_map/ppermute | solution.py:106
  52.4 9.7 %collective-permute-start.22 = (bf16[192,1152]{1,0:T(8,128)(2,1)S(1)}, bf16[192,1152]{1,0:T(8,128)(2,1)S(1)}, u32[]{:S(2)}, u32[]{:S(2)}) collective-permute-start(bf16[192,1152]{1,0:T(8,128)(2,1)S(1)} %get-tuple-element.59.refs_0_), channel_id=1, source_target_pairs={{0,48},{8,200},{16,0},{24,216},{32,16},{40,232},{48,32},{56,248},{... | collective-permute-start | bytes 1327112 | tf_op jit(solution)/shard_map/ppermute | solution.py:106
  62.0 6.5 %collective-permute-start.23 = (f32[576,512]{1,0:T(8,128)S(1)}, f32[576,512]{1,0:T(8,128)S(1)}, u32[]{:S(2)}, u32[]{:S(2)}) collective-permute-start(f32[576,512]{1,0:T(8,128)S(1)} %get-tuple-element.69), channel_id=1, source_target_pairs={{0,8},{8,0},{16,24},{24,16},{32,40},{40,32},{48,56},{56,48},{64,72... | collective-permute-start | bytes 3538952 | tf_op jit(solution)/shard_map/ppermute | solution.py:657
  109.4 6.9 %collective-permute-start.26 = (bf16[576,1920]{1,0:T(8,128)(2,1)}, bf16[576,1920]{1,0:T(8,128)(2,1)}, u32[]{:S(2)}, u32[]{:S(2)}) collective-permute-start(bf16[576,1920]{1,0:T(8,128)(2,1)} %get-tuple-element.81.near_note.near), channel_id=1, source_target_pairs={{0,8},{8,0},{16,24},{24,16},{32,40},{40,32},{48,56},{56,48},{64,72... | collective-permute-start | bytes 6635528 | tf_op jit(solution)/shard_map/ppermute | solution.py:657
  109.9 22.8 %all-to-all-start.2 = ((bf16[4,96,3584]{2,1,0:T(8,128)(2,1)}), bf16[4,96,3584]{2,1,0:T(8,128)(2,1)S(1)}, u32[]{:S(2)}, u32[]{:S(2)}) async-start(bf16[4,96,3584]{2,1,0:T(8,128)(2,1)} %bitcast.7), calls=%async_computation.2 | async-start | bytes 5505024 | tf_op jit(solution)/shard_map/all_to_all | solution.py:696
  (13 other events, 57.5 us)

commit v7 on v6

--- a/solution.py
+++ b/solution.py
@@ -155,7 +155,12 @@
     return jnp.concatenate([s, notes_of(table[...], tok)], axis=1), t
 
 
-def keep_kernel(pos_ref, table, s_ref, t_ref, a_ref, b_ref):
+def keep_kernel(pos_ref, table, s_hbm, t_hbm, a_ref, b_ref, s_ref, t_ref, sem):
+    loads = [pltpu.make_async_copy(s_hbm, s_ref, sem.at[0]), pltpu.make_async_copy(t_hbm, t_ref, sem.at[1])]
+    for load in loads:
+        load.start()
+    for load in loads:
+        load.wait()
     a_ref[...], b_ref[...] = halves(pos_ref, table, s_ref, t_ref)
 
 
@@ -173,12 +178,13 @@
     kept = pl.pallas_call(
         keep_kernel,
         grid=(1,),
-        in_specs=[SMEM] + [once(v.shape) for v in own],
+        in_specs=[SMEM, once(own[0].shape), HBM, HBM],
         out_specs=[whole((tok, v)) for v in widths],
         out_shape=[jax.ShapeDtypeStruct((tok, v), f32) for v in widths],
+        scratch_shapes=[pltpu.VMEM(v.shape, v.dtype) for v in own[1:]] + [pltpu.SemaphoreType.DMA((2,))],
         compiler_params=params(),
         name="keep",
-    )(pos, *own)
+    )(pos, own[0], *[pltpu.with_memory_space_constraint(v, pltpu.HBM) for v in own[1:]])
     args = [*kept, *got]
     return pl.pallas_call(
         pair_kernel,
@@ -469,7 +475,7 @@
 
 
 def gap_kernel(
-    grad_scale, tok, pos_ref, s_ref, t_ref, x_ref, rank_ref, send_ref, keep_ref, own_ref, other_ref, loss_ref, full, part
+    grad_scale, tok, pos_ref, s_ref, t_ref, x_ref, rank_ref, send_ref, keep_ref, all_ref, loss_ref, full, part
 ):
     live, rows = s_ref.shape[0], full.shape[0]
     s_norm, t_norm, cross = merged(x_ref[...])
@@ -488,13 +494,7 @@
             start = pl.multiple_of(2 * tok * block + tok * c, 8)
             part[tok * j : tok * (j + 1), :] = full[pl.ds(start, tok), :]
         ref[...] = part[...].astype(bf16)
-    size = 2 * tok
-    for ref, c in ((own_ref, core), (other_ref, 1 - core)):
-        for i in range(SIDE):
-            for j in range(SIDE):
-                at = (i * SIDE + j) * size
-                start = block_start(pos_ref, i, j, c, size)
-                ref[at : at + size, :] = full[pl.ds(start, size), :].astype(bf16)
+    all_ref[...] = full[...].astype(bf16)
 
 
 def logit_gap(pos, s, t, x, rank, grad_scale, tok):
@@ -505,8 +505,8 @@
         functools.partial(gap_kernel, grad_scale, tok),
         grid=(1,),
         in_specs=[SMEM] + [once(v.shape) for v in args],
-        out_specs=[whole(half), whole(half), whole((rows, cols)), whole((rows, cols)), whole((1, 1))],
-        out_shape=[jax.ShapeDtypeStruct(v, bf16) for v in (half, half, (rows, cols), (rows, cols))]
+        out_specs=[whole(half), whole(half), whole((rows, cols)), whole((1, 1))],
+        out_shape=[jax.ShapeDtypeStruct(v, bf16) for v in (half, half, (rows, cols))]
         + [jax.ShapeDtypeStruct((1, 1), f32)],
         scratch_shapes=[pltpu.VMEM((rows, cols), f32), pltpu.VMEM(half, f32)],
         compiler_params=params(20),
@@ -535,16 +535,19 @@
     )(own, other)
 
 
-def hidden_kernel(keep_ref, got_ref, own_w, other_w, out_hbm, done, sem):
+def hidden_own_kernel(keep_ref, own_w, out_ref):
+    out_ref[...] = jnp.dot(keep_ref[...], own_w[...], preferred_element_type=f32)
+
+
+def hidden_kernel(part_ref, got_ref, other_w, out_hbm, done, sem):
     k = pl.program_id(0)
-    kb = own_w.shape[1]
+    kb = other_w.shape[1]
 
     def store(i):
         return pltpu.make_async_copy(done.at[i], out_hbm.at[:, pl.ds(pl.multiple_of(i * kb, kb), kb)], sem.at[i])
 
     done[k] = (
-        jnp.dot(keep_ref[...], own_w[...], preferred_element_type=f32)
-        + jnp.dot(got_ref[...], other_w[...], preferred_element_type=f32)
+        part_ref[...] + jnp.dot(got_ref[...], other_w[...], preferred_element_type=f32)
     ).astype(bf16)
     store(k).start()
 
@@ -559,17 +562,28 @@
     depth = own_w.shape[1]
     kb = depth // chunks
     head = pl.BlockSpec((cols, kb), lambda k: (0, k))
+    wide = pl.BlockSpec((rows, kb), lambda k: (0, k))
+    part = pl.pallas_call(
+        hidden_own_kernel,
+        grid=(chunks,),
+        in_specs=[once((rows, cols)), head],
+        out_specs=wide,
+        out_shape=jax.ShapeDtypeStruct((rows, depth), f32),
+        compiler_params=params(16),
+        cost_estimate=cost(2 * rows * depth * cols, 0),
+        name="grad_hidden_own",
+    )(keep, own_w)
     return pl.pallas_call(
         hidden_kernel,
         grid=(chunks,),
-        in_specs=[once((rows, cols)), once((rows, cols)), head, head],
+        in_specs=[wide, once((rows, cols)), head],
         out_specs=HBM,
         out_shape=pltpu.HBM((rows, depth), bf16),
         scratch_shapes=[pltpu.VMEM((chunks, rows, kb), bf16), pltpu.SemaphoreType.DMA((chunks,))],
-        compiler_params=params(16),
+        compiler_params=params(20),
         cost_estimate=cost(0, 0),
         name="grad_hidden",
-    )(keep, got, own_w, other_w)
+    )(part, got, other_w)
 
 
 def sum_kernel(x_ref, wait_ref, out_ref):
@@ -595,31 +609,37 @@
     )(parts, wait)
 
 
-def head_kernel(pos_ref, near, far, near_got, far_got, own_g, other_g, out_ref, done_ref):
+def head_kernel(pos_ref, near, far, near_got, far_got, g_ref, out_ref, done_ref, rows):
     done_ref[...] = jnp.zeros_like(done_ref)
-    own = pl.program_id(0) == pos_ref[2]
-    depth = out_ref.shape[0]
-
-    def write(near, far, g):
-        n = near.shape[0]
+    depth, n = out_ref.shape[0], near.shape[0]
+    size = rows.shape[0] // (SIDE * SIDE)
+    for i in range(SIDE):
+        for j in range(SIDE):
+            at = (i * SIDE + j) * size
+            start = block_start(pos_ref, i, j, pl.program_id(0), size)
+            rows[at : at + size, :] = g_ref[pl.ds(start, size), :]
+
+    def write(near, far):
         down = (((0,), (0,)), ((), ()))
         out_ref[...] = (
-            lax.dot_general(near[:, :depth], g[:n, :], down, preferred_element_type=f32)
-            + lax.dot_general(far[:, :depth], g[n:, :], down, preferred_element_type=f32)
+            lax.dot_general(near[:, :depth], rows[:n, :], down, preferred_element_type=f32)
+            + lax.dot_general(far[:, :depth], rows[n:, :], down, preferred_element_type=f32)
         ).astype(bf16)
+
+    own = pl.program_id(0) == pos_ref[2]
 
     @pl.when(own)
     def _():
-        write(near, far, own_g)
+        write(near, far)
 
     @pl.when(jnp.logical_not(own))
     def _():
-        write(near_got, far_got, other_g)
-
-
-def grad_head_of(pos, near, far, near_got, far_got, own_g, other_g, depth):
-    rows, cols = own_g.shape
-    args = (near, far, near_got, far_got, own_g, other_g)
+        write(near_got, far_got)
+
+
+def grad_head_of(pos, near, far, near_got, far_got, g, depth):
+    rows, cols = g.shape
+    args = (near, far, near_got, far_got, g)
     return pl.pallas_call(
         head_kernel,
         grid_spec=pltpu.PrefetchScalarGridSpec(
@@ -627,6 +647,7 @@
             grid=(2,),
             in_specs=[once(v.shape) for v in args],
             out_specs=[pl.BlockSpec((depth, cols), lambda k, pos: (k, 0)), whole((8, 128))],
+            scratch_shapes=[pltpu.VMEM((rows, cols), bf16)],
         ),
         out_shape=[jax.ShapeDtypeStruct((2 * depth, cols), bf16), jax.ShapeDtypeStruct((8, 128), f32)],
         compiler_params=params(24),
@@ -690,14 +711,14 @@
     stats = lax.all_to_all(stats, "dp", 0, 0)
     stats = lax.all_to_all(merge(stats, slices), "vocab", 0, 0)
 
-    send, keep, own_g, other_g, loss = logit_gap(pos, s, t, stats, rank, loss_scale / live_total, tok)
+    send, keep, g, loss = logit_gap(pos, s, t, stats, rank, loss_scale / live_total, tok)
     got = other(send)
     mine = grad_hidden_of(keep, got, *heads, 2)
     parts = lax.all_to_all(
         mine.reshape(SIDE, SIDE * tok, depth), "dp", 0, 0, axis_index_groups=lines(0)
     )
     grad_head, done = grad_head_of(
-        pos, near, far, other(after(near, mine)), other(after(far, mine)), own_g, other_g, s_half
+        pos, near, far, other(after(near, mine)), other(after(far, mine)), g, s_half
     )
     groups = [[i * slices + z for i in line for z in range(slices)] for line in lines(1)]
     parts = lax.all_to_all(summed(parts, slices, done), ("dp", "vocab"), 0, 0, axis_index_groups=groups)

time: 160 us -> 158 us (0.988)
  local copies, waits for them, and re-layouts: 4.13 us -> 1.14 us
  Pallas kernels: 37.6 us -> 39.3 us
    unnamed x16 -> x8, local copies, waits for them, and re-layouts: 4.12 us -> 1.13 us
    pallas_call x2 -> x3, Pallas kernels: 5.49 us -> 7.57 us  [the longest x1 3.51 us: grad_hidden_of(): pl.pallas_call(hidden_kernel, grid=(chunks,), in_specs=[wide, once((rows,...]
  transfers between devices with their start and end apart: 29 -> 29, of which waited for: 9 -> 8; matrix products, arithmetic and copies ran while one was open for 1% -> 1% of each run, Pallas kernels for 17% -> 19%
where the time goes in v7:
time: 158 us; the launch traced here: 157 us
  blocking collectives  53.5 us (34%)
  Pallas kernels  39.3 us (25%)
  starting transfers between devices  38.7 us (24%)
  waiting for transfers between devices  20.9 us (13%)
  between operations  2.21 us (1%)
    all_to_all x1, blocking collectives, per_device(): lax.all_to_all(summed(parts, slices, done), ('dp', 'vocab'), 0, 0, axis_i...  25.6 us
    ppermute x16, starting transfers between devices, ways(): return lambda a, b: [lax.ppermute(a, 'dp', up), lax.ppermute(b, 'dp', down)]  22.1 us
    all_to_all x1, blocking collectives, per_device(): stats = lax.all_to_all(stats, 'dp', 0, 0)  14.6 us
    all_to_all x1, blocking collectives, per_device(): stats = lax.all_to_all(merge(stats, slices), 'vocab', 0, 0)  13.4 us
    ppermute x12, starting transfers between devices, per_device(): other = lambda v: lax.ppermute(v, 'dp', swap)  13 us
    ppermute x16, waiting for transfers between devices, ways(): return lambda a, b: [lax.ppermute(a, 'dp', up), lax.ppermute(b, 'dp', down)]  12.3 us
    pallas_call x1, Pallas kernels, grad_head_of(): pl.pallas_call(head_kernel, grid_spec=pltpu.PrefetchScalarGridSpec(num_sc...  8.55 us
    all_to_all x1, waiting for transfers between devices, per_device(): lax.all_to_all(mine.reshape(SIDE, SIDE * tok, depth), 'dp', 0, 0, axis_in...  6.58 us
  transfers between devices with their start and end apart: 29, of which 8 were waited for; matrix products, arithmetic and copies ran while one was open for 1% of the time, Pallas kernels for 19%

profile of v7, /device:TPU:1, one launch (start us, length us, event | category | flops | bytes accessed | tf_op | source)
XLA Modules:
  0.0 157.4 jit_solution(1478181076479194087)
XLA Ops:
  0.6 3.3 %collective-permute-start.2 = (bf16[24,4608]{1,0:T(8,128)(2,1)}, bf16[24,4608]{1,0:T(8,128)(2,1)S(1)}, u32[]{:S(2)}, u32[]{:S(2)}) collective-permute-start(bf16[24,4608]{1,0:T(8,128)(2,1)} %t_hbm.1), channel_id=1, source_target_pairs={{0,8},{8,0},{16,24},{24,16},{32,40},{40,32},{48,56},{56,48},{64,72... | collective-permute-start | bytes 663560 | tf_op jit(solution)/shard_map/ppermute | solution.py:678
  9.2 2.7 %collective-permute-start.9 = (bf16[48,2304]{1,0:T(8,128)(2,1)S(1)}, bf16[48,2304]{1,0:T(8,128)(2,1)S(1)}, u32[]{:S(2)}, u32[]{:S(2)}) collective-permute-start(bf16[48,2304]{1,0:T(8,128)(2,1)S(1)} %get-tuple-element.50.block), channel_id=1, source_target_pairs={{0,192},{8,56},{16,208},{24,8},{32,224},{40,24},{48,240},{56,40},{... | collective-permute-start | bytes 663560 | tf_op jit(solution)/shard_map/ppermute | solution.py:106
  11.9 2.7 %collective-permute-start.4 = (bf16[48,1920]{1,0:T(8,128)(2,1)S(1)}, bf16[48,1920]{1,0:T(8,128)(2,1)S(1)}, u32[]{:S(2)}, u32[]{:S(2)}) collective-permute-start(bf16[48,1920]{1,0:T(8,128)(2,1)S(1)} %get-tuple-element.46.block), channel_id=1, source_target_pairs={{0,192},{8,56},{16,208},{24,8},{32,224},{40,24},{48,240},{56,40},{... | collective-permute-start | bytes 552968 | tf_op jit(solution)/shard_map/ppermute | solution.py:106
  14.6 3.2 %collective-permute-done.3.before = bf16[48,1920]{1,0:T(8,128)(2,1)S(1)} collective-permute-done((bf16[48,1920]{1,0:T(8,128)(2,1)S(1)}, bf16[48,1920]{1,0:T(8,128)(2,1)S(1)}, u32[]{:S(2)}, u32[]{:S(2)}) %collective-permute-start.3) | collective-permute-done | bytes 184352 | tf_op jit(solution)/shard_map/ppermute | solution.py:106
  18.0 2.7 %collective-permute-start.13 = (bf16[48,1152]{1,0:T(8,128)(2,1)S(1)}, bf16[48,1152]{1,0:T(8,128)(2,1)S(1)}, u32[]{:S(2)}, u32[]{:S(2)}) collective-permute-start(bf16[48,1152]{1,0:T(8,128)(2,1)S(1)} %get-tuple-element.51.refs_0_), channel_id=1, source_target_pairs={{0,192},{8,56},{16,208},{24,8},{32,224},{40,24},{48,240},{56,40},{... | collective-permute-start | bytes 331784 | tf_op jit(solution)/shard_map/ppermute | solution.py:106
  20.6 2.7 %collective-permute-start.7 = (bf16[48,896]{1,0:T(8,128)(2,1)S(1)}, bf16[48,896]{1,0:T(8,128)(2,1)S(1)}, u32[]{:S(2)}, u32[]{:S(2)}) collective-permute-start(bf16[48,896]{1,0:T(8,128)(2,1)S(1)} %get-tuple-element.49.refs_0_), channel_id=1, source_target_pairs={{0,192},{8,56},{16,208},{24,8},{32,224},{40,24},{48,240},{56,40},{... | collective-permute-start | bytes 258056 | tf_op jit(solution)/shard_map/ppermute | solution.py:106
  25.5 3.7 %collective-permute-start.18 = (bf16[4608,512]{1,0:T(8,128)(2,1)S(1)}, bf16[4608,512]{1,0:T(8,128)(2,1)S(1)}, u32[]{:S(2)}, u32[]{:S(2)}) collective-permute-start(bf16[4608,512]{1,0:T(8,128)(2,1)S(1)} %copy-done.1), channel_id=1, source_target_pairs={{0,8},{8,0},{16,24},{24,16},{32,40},{40,32},{48,56},{56,48},{64,72... | collective-permute-start | bytes 14155784 | tf_op jit(solution)/shard_map/ppermute | solution.py:678
  29.2 2.8 %collective-permute-start.11 = (bf16[192,1920]{1,0:T(8,128)(2,1)S(1)}, bf16[192,1920]{1,0:T(8,128)(2,1)S(1)}, u32[]{:S(2)}, u32[]{:S(2)}) collective-permute-start(bf16[192,1920]{1,0:T(8,128)(2,1)S(1)} %join.2.refs_0_), channel_id=1, source_target_pairs={{0,48},{8,200},{16,0},{24,216},{32,16},{40,232},{48,32},{56,248},{... | collective-permute-start | bytes 2211848 | tf_op jit(solution)/shard_map/ppermute | solution.py:106
  32.0 2.7 %collective-permute-start.17 = (bf16[192,2304]{1,0:T(8,128)(2,1)S(1)}, bf16[192,2304]{1,0:T(8,128)(2,1)S(1)}, u32[]{:S(2)}, u32[]{:S(2)}) collective-permute-start(bf16[192,2304]{1,0:T(8,128)(2,1)S(1)} %join.3.refs_0_.t0), channel_id=1, source_target_pairs={{0,48},{8,200},{16,0},{24,216},{32,16},{40,232},{48,32},{56,248},{... | collective-permute-start | bytes 2654216 | tf_op jit(solution)/shard_map/ppermute | solution.py:106
  34.7 2.8 %turn.1 = (bf16[512,3584]{1,0:T(8,128)(2,1)S(1)}, bf16[512,3584]{1,0:T(8,128)(2,1)S(1)}, f32[8,128]{1,0:T(8,128)S(1)}) custom-call(bf16[3584,512]{1,0:T(8,128)(2,1)S(1)} %copy-done, bf16[3584,512]{1,0:T(8,128)(2,1)S(1)} %collective-permute-done.5.refs_0_.refs_4_.other_ref.s_w_other), custom_call_target="tpu_custom_call" | custom-call | bytes 29360128 | tf_op jit(solution)/shard_map/turn/pallas_call | solution.py:526
  37.5 3.7 %collective-permute-done.10.refs_1_.before = bf16[192,1920]{1,0:T(8,128)(2,1)S(1)} collective-permute-done((bf16[192,1920]{1,0:T(8,128)(2,1)S(1)}, bf16[192,1920]{1,0:T(8,128)(2,1)S(1)}, u32[]{:S(2)}, u32[]{:S(2)}) %collective-permute-start.10) | collective-permute-done | bytes 737312 | tf_op jit(solution)/shard_map/ppermute | solution.py:106
  44.1 3.6 %student_near.1 = (f32[576,512]{1,0:T(8,128)S(1)}, f32[576,512]{1,0:T(8,128)S(1)}, bf16[576,1920]{1,0:T(8,128)(2,1)}) custom-call(s32[3]{0:T(128)S(1)} %pad_add_fusion.pos_ref, bf16[192,1920]{1,0:T(8,128)(2,1)S(1)} %join.2.refs_0_, bf16[192,1920]{1,0:T(8,128)(2,1)S(1)} %collective-permute-done.10.refs_1_.before, ...), custom_call_target="tpu_custom_call" | custom-call | tf_op jit(solution)/shard_map/student_near/pallas_call | solution.py:239
  47.7 2.9 %collective-permute-done.16.before.t1 = bf16[192,2304]{1,0:T(8,128)(2,1)S(1)} collective-permute-done((bf16[192,2304]{1,0:T(8,128)(2,1)S(1)}, bf16[192,2304]{1,0:T(8,128)(2,1)S(1)}, u32[]{:S(2)}, u32[]{:S(2)}) %collective-permute-start.16) | collective-permute-done | bytes 884768 | tf_op jit(solution)/shard_map/ppermute | solution.py:106
  51.6 2.9 %collective-permute-start.22 = (bf16[192,1152]{1,0:T(8,128)(2,1)S(1)}, bf16[192,1152]{1,0:T(8,128)(2,1)S(1)}, u32[]{:S(2)}, u32[]{:S(2)}) collective-permute-start(bf16[192,1152]{1,0:T(8,128)(2,1)S(1)} %get-tuple-element.58.refs_0_), channel_id=1, source_target_pairs={{0,48},{8,200},{16,0},{24,216},{32,16},{40,232},{48,32},{56,248},{... | collective-permute-start | bytes 1327112 | tf_op jit(solution)/shard_map/ppermute | solution.py:106
  54.8 5.5 %middle_logits.1 = (f32[192,512]{1,0:T(8,128)S(1)}, f32[192,512]{1,0:T(8,128)S(1)}, bf16[192,1920]{1,0:T(8,128)(2,1)S(1)}, f32[576,512]{1,0:T(8,128)S(1)}, f32[576,512]{1,0:T(8,128)S(1)}) custom-call(s32[3]{0:T(128)S(1)} %pad_add_fusion.pos_ref, bf16[192,1024]{1,0:T(8,128)(2,1)S(1)} %collective-permute-done.14.s_left, ...), custom_call_target="tpu_custom_call" | custom-call | flops 99999997952 | tf_op jit(solution)/shard_map/middle_logits/pallas_call | solution.py:290
  64.3 3.4 %student_logits.1 = (f32[384,512]{1,0:T(8,128)S(1)}, f32[384,128]{1,0:T(8,128)S(1)}, s32[1,768]{1,0:T(1,128)S(1)}, s32[1,768]{1,0:T(1,128)S(1)}) custom-call(s32[3]{0:T(128)S(1)} %pad_add_fusion.pos_ref, f32[576,512]{1,0:T(8,128)S(1)} %get-tuple-element.52.near, f32[192,512]{1,0:T(8,128)S(1)} %get-tuple-element.59.far, ...), custom_call_target="tpu_custom_call" | custom-call | flops 99999997952 | tf_op jit(solution)/shard_map/student_logits/pallas_call | solution.py:371
  70.1 14.6 %all_to_all.20.x_ref = f32[32,1,1152]{2,1,0:T(1,128)S(1)} all-to-all(f32[32,1,1152]{2,1,0:T(1,128)S(1)} %get-tuple-element.73), channel_id=1, replica_groups=mesh['dp'=32,'vocab'=8] {'dp'}, dimensions={0} | all-to-all | bytes 294912 | tf_op jit(solution)/shard_map/all_to_all | solution.py:711
  84.9 13.4 %all_to_all.21.x_ref = f32[8,1,1152]{2,1,0:T(1,128)S(1)} all-to-all(f32[8,1,1152]{2,1,0:T(1,128)S(1)} %merge_stats.1), channel_id=1, replica_groups=mesh['dp'=32,'vocab'=8] {'vocab'}, dimensions={0} | all-to-all | bytes 73728 | tf_op jit(solution)/shard_map/all_to_all | solution.py:712
  101.8 2.4 %grad_hidden_own.1.part_ref = f32[384,3584]{1,0:T(8,128)S(1)} custom-call(bf16[384,512]{1,0:T(8,128)(2,1)S(1)} %get-tuple-element.76.keep_ref, bf16[512,3584]{1,0:T(8,128)(2,1)S(1)} %get-tuple-element.77.own_w), custom_call_target="tpu_custom_call" | custom-call | flops 1409286144 | tf_op jit(solution)/shard_map/grad_hidden_own/pallas_call | solution.py:566
  104.2 3.5 %grad_hidden.1 = bf16[384,3584]{1,0:T(8,128)(2,1)} custom-call(f32[384,3584]{1,0:T(8,128)S(1)} %grad_hidden_own.1.part_ref, bf16[384,512]{1,0:T(8,128)(2,1)S(1)} %collective-permute-done.25.got_ref, bf16[512,3584]{1,0:T(8,128)(2,1)S(1)} %get-tuple-element.79.other_w), custom_call_target="tpu_custom_call" | custom-call | tf_op jit(solution)/shard_map/grad_hidden/pallas_call | solution.py:576
  107.8 3.7 %all-to-all-start.2 = ((bf16[4,96,3584]{2,1,0:T(8,128)(2,1)}), bf16[4,96,3584]{2,1,0:T(8,128)(2,1)S(1)}, u32[]{:S(2)}, u32[]{:S(2)}) async-start(bf16[4,96,3584]{2,1,0:T(8,128)(2,1)} %bitcast.7), calls=%async_computation.2 | async-start | bytes 5505024 | tf_op jit(solution)/shard_map/all_to_all | solution.py:717
  115.5 8.5 %grad_head.1 = (bf16[3584,512]{1,0:T(8,128)(2,1)}, f32[8,128]{1,0:T(8,128)S(1)}) custom-call(s32[3]{0:T(128)S(1)} %pad_add_fusion.pos_ref, bf16[576,1920]{1,0:T(8,128)(2,1)} %get-tuple-element.80.near_note.near, bf16[192,1920]{1,0:T(8,128)(2,1)S(1)} %copy-done.3, bf16[576,1920]{1,0:T(8,128)(2,1)} %collective-permute-done.26.near_got, ...), custom_call_target="tpu_custom_call" | custom-call | tf_op jit(solution)/shard_map/grad_head/pallas_call | solution.py:643
  124.1 6.6 %all-to-all-done.2.x_ref = bf16[4,96,3584]{2,1,0:T(8,128)(2,1)S(1)} async-done(((bf16[4,96,3584]{2,1,0:T(8,128)(2,1)}), bf16[4,96,3584]{2,1,0:T(8,128)(2,1)S(1)}, u32[]{:S(2)}, u32[]{:S(2)}) %all-to-all-start.2) | async-done | bytes 2752544 | tf_op jit(solution)/shard_map/all_to_all | solution.py:717
  131.0 25.6 %all_to_all.22 = bf16[32,24,448]{2,1,0:T(8,128)(2,1)S(1)} all-to-all(bf16[32,24,448]{2,1,0:T(8,128)(2,1)S(1)} %sum_parts.1), channel_id=1, replica_groups={{0,1,2,3,4,5,6,7,16,17,18,19,20,21,22,23,32,33,34,35,36,37,38,39,48,49,..., dimensions={0} | all-to-all | bytes 1376256 | tf_op jit(solution)/shard_map/all_to_all | solution.py:724
  (69 shorter events, 25.8 us)
Async XLA Ops:
  0.6 7.7 %collective-permute-start.2 = (bf16[24,4608]{1,0:T(8,128)(2,1)}, bf16[24,4608]{1,0:T(8,128)(2,1)S(1)}, u32[]{:S(2)}, u32[]{:S(2)}) collective-permute-start(bf16[24,4608]{1,0:T(8,128)(2,1)} %t_hbm.1), channel_id=1, source_target_pairs={{0,8},{8,0},{16,24},{24,16},{32,40},{40,32},{48,56},{56,48},{64,72... | collective-permute-start | bytes 663560 | tf_op jit(solution)/shard_map/ppermute | solution.py:678
  4.0 4.3 %collective-permute-start.1 = (bf16[24,3584]{1,0:T(8,128)(2,1)}, bf16[24,3584]{1,0:T(8,128)(2,1)S(1)}, u32[]{:S(2)}, u32[]{:S(2)}) collective-permute-start(bf16[24,3584]{1,0:T(8,128)(2,1)} %s_hbm.1), channel_id=1, source_target_pairs={{0,8},{8,0},{16,24},{24,16},{32,40},{40,32},{48,56},{56,48},{64,72... | collective-permute-start | bytes 516104 | tf_op jit(solution)/shard_map/ppermute | solution.py:678
  9.0 8.8 %collective-permute-start.5 = (bf16[3584,512]{1,0:T(8,128)(2,1)}, bf16[3584,512]{1,0:T(8,128)(2,1)S(1)}, u32[]{:S(2)}, u32[]{:S(2)}) collective-permute-start(bf16[3584,512]{1,0:T(8,128)(2,1)} %s_w.1), channel_id=1, source_target_pairs={{0,8},{8,0},{16,24},{24,16},{32,40},{40,32},{48,56},{56,48},{64,72... | collective-permute-start | bytes 11010056 | tf_op jit(solution)/shard_map/ppermute | solution.py:678
  9.2 8.6 %collective-permute-start.8 = (bf16[48,2304]{1,0:T(8,128)(2,1)S(1)}, bf16[48,2304]{1,0:T(8,128)(2,1)S(1)}, u32[]{:S(2)}, u32[]{:S(2)}) collective-permute-start(bf16[48,2304]{1,0:T(8,128)(2,1)S(1)} %get-tuple-element.50.block), channel_id=1, source_target_pairs={{0,64},{8,24},{16,80},{24,40},{32,96},{40,56},{48,112},{56,8},{64,... | collective-permute-start | bytes 663560 | tf_op jit(solution)/shard_map/ppermute | solution.py:106
  9.2 8.6 %collective-permute-start.9 = (bf16[48,2304]{1,0:T(8,128)(2,1)S(1)}, bf16[48,2304]{1,0:T(8,128)(2,1)S(1)}, u32[]{:S(2)}, u32[]{:S(2)}) collective-permute-start(bf16[48,2304]{1,0:T(8,128)(2,1)S(1)} %get-tuple-element.50.block), channel_id=1, source_target_pairs={{0,192},{8,56},{16,208},{24,8},{32,224},{40,24},{48,240},{56,40},{... | collective-permute-start | bytes 663560 | tf_op jit(solution)/shard_map/ppermute | solution.py:106
  11.9 5.9 %collective-permute-start.3 = (bf16[48,1920]{1,0:T(8,128)(2,1)S(1)}, bf16[48,1920]{1,0:T(8,128)(2,1)S(1)}, u32[]{:S(2)}, u32[]{:S(2)}) collective-permute-start(bf16[48,1920]{1,0:T(8,128)(2,1)S(1)} %get-tuple-element.46.block), channel_id=1, source_target_pairs={{0,64},{8,24},{16,80},{24,40},{32,96},{40,56},{48,112},{56,8},{64,... | collective-permute-start | bytes 552968 | tf_op jit(solution)/shard_map/ppermute | solution.py:106
  11.9 5.9 %collective-permute-start.4 = (bf16[48,1920]{1,0:T(8,128)(2,1)S(1)}, bf16[48,1920]{1,0:T(8,128)(2,1)S(1)}, u32[]{:S(2)}, u32[]{:S(2)}) collective-permute-start(bf16[48,1920]{1,0:T(8,128)(2,1)S(1)} %get-tuple-element.46.block), channel_id=1, source_target_pairs={{0,192},{8,56},{16,208},{24,8},{32,224},{40,24},{48,240},{56,40},{... | collective-permute-start | bytes 552968 | tf_op jit(solution)/shard_map/ppermute | solution.py:106
  17.9 7.5 %collective-permute-start.12 = (bf16[48,1152]{1,0:T(8,128)(2,1)S(1)}, bf16[48,1152]{1,0:T(8,128)(2,1)S(1)}, u32[]{:S(2)}, u32[]{:S(2)}) collective-permute-start(bf16[48,1152]{1,0:T(8,128)(2,1)S(1)} %get-tuple-element.53), channel_id=1, source_target_pairs={{0,64},{8,24},{16,80},{24,40},{32,96},{40,56},{48,112},{56,8},{64,... | collective-permute-start | bytes 331784 | tf_op jit(solution)/shard_map/ppermute | solution.py:106
  18.0 7.4 %collective-permute-start.13 = (bf16[48,1152]{1,0:T(8,128)(2,1)S(1)}, bf16[48,1152]{1,0:T(8,128)(2,1)S(1)}, u32[]{:S(2)}, u32[]{:S(2)}) collective-permute-start(bf16[48,1152]{1,0:T(8,128)(2,1)S(1)} %get-tuple-element.51.refs_0_), channel_id=1, source_target_pairs={{0,192},{8,56},{16,208},{24,8},{32,224},{40,24},{48,240},{56,40},{... | collective-permute-start | bytes 331784 | tf_op jit(solution)/shard_map/ppermute | solution.py:106
  20.6 4.7 %collective-permute-start.6 = (bf16[48,1024]{1,0:T(8,128)(2,1)S(1)}, bf16[48,1024]{1,0:T(8,128)(2,1)S(1)}, u32[]{:S(2)}, u32[]{:S(2)}) collective-permute-start(bf16[48,1024]{1,0:T(8,128)(2,1)S(1)} %get-tuple-element.48), channel_id=1, source_target_pairs={{0,64},{8,24},{16,80},{24,40},{32,96},{40,56},{48,112},{56,8},{64,... | collective-permute-start | bytes 294920 | tf_op jit(solution)/shard_map/ppermute | solution.py:106
  25.5 25.9 %collective-permute-start.18 = (bf16[4608,512]{1,0:T(8,128)(2,1)S(1)}, bf16[4608,512]{1,0:T(8,128)(2,1)S(1)}, u32[]{:S(2)}, u32[]{:S(2)}) collective-permute-start(bf16[4608,512]{1,0:T(8,128)(2,1)S(1)} %copy-done.1), channel_id=1, source_target_pairs={{0,8},{8,0},{16,24},{24,16},{32,40},{40,32},{48,56},{56,48},{64,72... | collective-permute-start | bytes 14155784 | tf_op jit(solution)/shard_map/ppermute | solution.py:678
  29.2 12.0 %collective-permute-start.10 = (bf16[192,1920]{1,0:T(8,128)(2,1)S(1)}, bf16[192,1920]{1,0:T(8,128)(2,1)S(1)}, u32[]{:S(2)}, u32[]{:S(2)}) collective-permute-start(bf16[192,1920]{1,0:T(8,128)(2,1)S(1)} %join.2.refs_0_), channel_id=1, source_target_pairs={{0,16},{8,72},{16,32},{24,88},{32,48},{40,104},{48,0},{56,120},{64... | collective-permute-start | bytes 2211848 | tf_op jit(solution)/shard_map/ppermute | solution.py:106
  29.2 12.0 %collective-permute-start.11 = (bf16[192,1920]{1,0:T(8,128)(2,1)S(1)}, bf16[192,1920]{1,0:T(8,128)(2,1)S(1)}, u32[]{:S(2)}, u32[]{:S(2)}) collective-permute-start(bf16[192,1920]{1,0:T(8,128)(2,1)S(1)} %join.2.refs_0_), channel_id=1, source_target_pairs={{0,48},{8,200},{16,0},{24,216},{32,16},{40,232},{48,32},{56,248},{... | collective-permute-start | bytes 2211848 | tf_op jit(solution)/shard_map/ppermute | solution.py:106
  32.0 18.6 %collective-permute-start.16 = (bf16[192,2304]{1,0:T(8,128)(2,1)S(1)}, bf16[192,2304]{1,0:T(8,128)(2,1)S(1)}, u32[]{:S(2)}, u32[]{:S(2)}) collective-permute-start(bf16[192,2304]{1,0:T(8,128)(2,1)S(1)} %join.3.refs_0_.t0), channel_id=1, source_target_pairs={{0,16},{8,72},{16,32},{24,88},{32,48},{40,104},{48,0},{56,120},{64... | collective-permute-start | bytes 2654216 | tf_op jit(solution)/shard_map/ppermute | solution.py:106
  32.0 19.4 %collective-permute-start.17 = (bf16[192,2304]{1,0:T(8,128)(2,1)S(1)}, bf16[192,2304]{1,0:T(8,128)(2,1)S(1)}, u32[]{:S(2)}, u32[]{:S(2)}) collective-permute-start(bf16[192,2304]{1,0:T(8,128)(2,1)S(1)} %join.3.refs_0_.t0), channel_id=1, source_target_pairs={{0,48},{8,200},{16,0},{24,216},{32,16},{40,232},{48,32},{56,248},{... | collective-permute-start | bytes 2654216 | tf_op jit(solution)/shard_map/ppermute | solution.py:106
  41.2 13.6 %collective-permute-start.14 = (bf16[192,1024]{1,0:T(8,128)(2,1)S(1)}, bf16[192,1024]{1,0:T(8,128)(2,1)S(1)}, u32[]{:S(2)}, u32[]{:S(2)}) collective-permute-start(bf16[192,1024]{1,0:T(8,128)(2,1)S(1)} %get-tuple-element.55), channel_id=1, source_target_pairs={{0,16},{8,72},{16,32},{24,88},{32,48},{40,104},{48,0},{56,120},{64... | collective-permute-start | bytes 1179656 | tf_op jit(solution)/shard_map/ppermute | solution.py:106
  42.1 12.4 %collective-permute-start.15 = (bf16[192,896]{1,0:T(8,128)(2,1)S(1)}, bf16[192,896]{1,0:T(8,128)(2,1)S(1)}, u32[]{:S(2)}, u32[]{:S(2)}) collective-permute-start(bf16[192,896]{1,0:T(8,128)(2,1)S(1)} %get-tuple-element.56), channel_id=1, source_target_pairs={{0,48},{8,200},{16,0},{24,216},{32,16},{40,232},{48,32},{56,248},{... | collective-permute-start | bytes 1032200 | tf_op jit(solution)/shard_map/ppermute | solution.py:106
  50.6 13.6 %collective-permute-start.19 = (f32[576,512]{1,0:T(8,128)S(1)}, f32[576,512]{1,0:T(8,128)S(1)}, u32[]{:S(2)}, u32[]{:S(2)}) collective-permute-start(f32[576,512]{1,0:T(8,128)S(1)} %get-tuple-element.60), channel_id=1, source_target_pairs={{0,8},{8,0},{16,24},{24,16},{32,40},{40,32},{48,56},{56,48},{64,72... | collective-permute-start | bytes 3538952 | tf_op jit(solution)/shard_map/ppermute | solution.py:678
  51.5 9.8 %collective-permute-start.21 = (bf16[192,1152]{1,0:T(8,128)(2,1)S(1)}, bf16[192,1152]{1,0:T(8,128)(2,1)S(1)}, u32[]{:S(2)}, u32[]{:S(2)}) collective-permute-start(bf16[192,1152]{1,0:T(8,128)(2,1)S(1)} %get-tuple-element.66), channel_id=1, source_target_pairs={{0,16},{8,72},{16,32},{24,88},{32,48},{40,104},{48,0},{56,120},{64... | collective-permute-start | bytes 1327112 | tf_op jit(solution)/shard_map/ppermute | solution.py:106
  51.6 9.7 %collective-permute-start.22 = (bf16[192,1152]{1,0:T(8,128)(2,1)S(1)}, bf16[192,1152]{1,0:T(8,128)(2,1)S(1)}, u32[]{:S(2)}, u32[]{:S(2)}) collective-permute-start(bf16[192,1152]{1,0:T(8,128)(2,1)S(1)} %get-tuple-element.58.refs_0_), channel_id=1, source_target_pairs={{0,48},{8,200},{16,0},{24,216},{32,16},{40,232},{48,32},{56,248},{... | collective-permute-start | bytes 1327112 | tf_op jit(solution)/shard_map/ppermute | solution.py:106
  61.2 6.5 %collective-permute-start.23 = (f32[576,512]{1,0:T(8,128)S(1)}, f32[576,512]{1,0:T(8,128)S(1)}, u32[]{:S(2)}, u32[]{:S(2)}) collective-permute-start(f32[576,512]{1,0:T(8,128)S(1)} %get-tuple-element.68), channel_id=1, source_target_pairs={{0,8},{8,0},{16,24},{24,16},{32,40},{40,32},{48,56},{56,48},{64,72... | collective-permute-start | bytes 3538952 | tf_op jit(solution)/shard_map/ppermute | solution.py:678
  100.0 4.2 %collective-permute-start.25 = (bf16[384,512]{1,0:T(8,128)(2,1)S(1)}, bf16[384,512]{1,0:T(8,128)(2,1)S(1)}, u32[]{:S(2)}, u32[]{:S(2)}) collective-permute-start(bf16[384,512]{1,0:T(8,128)(2,1)S(1)} %get-tuple-element.78), channel_id=1, source_target_pairs={{0,8},{8,0},{16,24},{24,16},{32,40},{40,32},{48,56},{56,48},{64,72... | collective-permute-start | bytes 1179656 | tf_op jit(solution)/shard_map/ppermute | solution.py:678
  107.7 6.7 %collective-permute-start.26 = (bf16[576,1920]{1,0:T(8,128)(2,1)}, bf16[576,1920]{1,0:T(8,128)(2,1)}, u32[]{:S(2)}, u32[]{:S(2)}) collective-permute-start(bf16[576,1920]{1,0:T(8,128)(2,1)} %get-tuple-element.80.near_note.near), channel_id=1, source_target_pairs={{0,8},{8,0},{16,24},{24,16},{32,40},{40,32},{48,56},{56,48},{64,72... | collective-permute-start | bytes 6635528 | tf_op jit(solution)/shard_map/ppermute | solution.py:678
  107.8 22.8 %all-to-all-start.2 = ((bf16[4,96,3584]{2,1,0:T(8,128)(2,1)}), bf16[4,96,3584]{2,1,0:T(8,128)(2,1)S(1)}, u32[]{:S(2)}, u32[]{:S(2)}) async-start(bf16[4,96,3584]{2,1,0:T(8,128)(2,1)} %bitcast.7), calls=%async_computation.2 | async-start | bytes 5505024 | tf_op jit(solution)/shard_map/all_to_all | solution.py:717
  (9 other events, 47.0 us)

commit v8 on v7

--- a/solution.py
+++ b/solution.py
@@ -155,12 +155,7 @@
     return jnp.concatenate([s, notes_of(table[...], tok)], axis=1), t
 
 
-def keep_kernel(pos_ref, table, s_hbm, t_hbm, a_ref, b_ref, s_ref, t_ref, sem):
-    loads = [pltpu.make_async_copy(s_hbm, s_ref, sem.at[0]), pltpu.make_async_copy(t_hbm, t_ref, sem.at[1])]
-    for load in loads:
-        load.start()
-    for load in loads:
-        load.wait()
+def keep_kernel(pos_ref, table, s_ref, t_ref, a_ref, b_ref):
     a_ref[...], b_ref[...] = halves(pos_ref, table, s_ref, t_ref)
 
 
@@ -178,10 +173,9 @@
     kept = pl.pallas_call(
         keep_kernel,
         grid=(1,),
-        in_specs=[SMEM, once(own[0].shape), HBM, HBM],
+        in_specs=[SMEM] + [once(v.shape) for v in own],
         out_specs=[whole((tok, v)) for v in widths],
         out_shape=[jax.ShapeDtypeStruct((tok, v), f32) for v in widths],
-        scratch_shapes=[pltpu.VMEM(v.shape, v.dtype) for v in own[1:]] + [pltpu.SemaphoreType.DMA((2,))],
         compiler_params=params(),
         name="keep",
     )(pos, own[0], *[pltpu.with_memory_space_constraint(v, pltpu.HBM) for v in own[1:]])
@@ -586,27 +580,30 @@
     )(part, got, other_w)
 
 
-def sum_kernel(x_ref, wait_ref, out_ref):
+def sum_kernel(x_ref, wait_ref, out_ref, blocks):
     total = jnp.sum(x_ref[...].astype(f32), axis=0)
-    n, tok, width = out_ref.shape
-    slices = total.shape[1] // width
-    for i in range(n):
+    n, width = x_ref.shape[0], out_ref.shape[1]
+    tok, slices = total.shape[0] // n, total.shape[1] // width
+    for i in range(n * slices):
         j, z = i // slices, i % slices
-        out_ref[i] = total[j * tok : (j + 1) * tok, z * width : (z + 1) * width].astype(bf16)
+        blocks[i * tok : (i + 1) * tok, :] = total[j * tok : (j + 1) * tok, z * width : (z + 1) * width]
+    out_ref[...] = blocks[...].astype(bf16)
 
 
 def summed(parts, slices, wait):
     n, rows, depth = parts.shape
-    out = (n * slices, rows // n, depth // slices)
-    return pl.pallas_call(
+    out = (rows * slices, depth // slices)
+    flat = pl.pallas_call(
         sum_kernel,
         grid=(1,),
         in_specs=[once(parts.shape), AFTER],
         out_specs=whole(out),
         out_shape=jax.ShapeDtypeStruct(out, bf16),
+        scratch_shapes=[pltpu.VMEM(out, f32)],
         compiler_params=params(20),
         name="sum_parts",
     )(parts, wait)
+    return flat.reshape(n * slices, rows // n, depth // slices)
 
 
 def head_kernel(pos_ref, near, far, near_got, far_got, g_ref, out_ref, done_ref, rows):

time: 158 us -> 157 us (level)
  no operation moved by 1% of the time
where the time goes in v8:
time: 157 us
  blocking collectives  53.5 us (34%)
  Pallas kernels  38.9 us (25%)
  starting transfers between devices  38.8 us (25%)
  waiting for transfers between devices  20.9 us (13%)
  between operations  2.2 us (1%)
    all_to_all x1, blocking collectives, per_device(): lax.all_to_all(summed(parts, slices, done), ('dp', 'vocab'), 0, 0, axis_i...  25.6 us
    ppermute x16, starting transfers between devices, ways(): return lambda a, b: [lax.ppermute(a, 'dp', up), lax.ppermute(b, 'dp', down)]  22.1 us
    all_to_all x1, blocking collectives, per_device(): stats = lax.all_to_all(stats, 'dp', 0, 0)  14.5 us
    all_to_all x1, blocking collectives, per_device(): stats = lax.all_to_all(merge(stats, slices), 'vocab', 0, 0)  13.4 us
    ppermute x12, starting transfers between devices, per_device(): other = lambda v: lax.ppermute(v, 'dp', swap)  13 us
    ppermute x16, waiting for transfers between devices, ways(): return lambda a, b: [lax.ppermute(a, 'dp', up), lax.ppermute(b, 'dp', down)]  12.3 us
    pallas_call x1, Pallas kernels, grad_head_of(): pl.pallas_call(head_kernel, grid_spec=pltpu.PrefetchScalarGridSpec(num_sc...  8.57 us
    all_to_all x1, waiting for transfers between devices, per_device(): lax.all_to_all(mine.reshape(SIDE, SIDE * tok, depth), 'dp', 0, 0, axis_in...  6.55 us
  transfers between devices with their start and end apart: 29, of which 8 were waited for; matrix products, arithmetic and copies ran while one was open for 1% of the time, Pallas kernels for 19%

profile of v8, /device:TPU:1, one launch (start us, length us, event | category | flops | bytes accessed | tf_op | source)
XLA Modules:
  0.0 157.0 jit_solution(17640799611660256787)
XLA Ops:
  0.6 3.3 %collective-permute-start.2 = (bf16[24,4608]{1,0:T(8,128)(2,1)}, bf16[24,4608]{1,0:T(8,128)(2,1)S(1)}, u32[]{:S(2)}, u32[]{:S(2)}) collective-permute-start(bf16[24,4608]{1,0:T(8,128)(2,1)} %t_ref.1), channel_id=1, source_target_pairs={{0,8},{8,0},{16,24},{24,16},{32,40},{40,32},{48,56},{56,48},{64,72... | collective-permute-start | bytes 663560 | tf_op jit(solution)/shard_map/ppermute | solution.py:675
  8.6 2.7 %collective-permute-start.9 = (bf16[48,2304]{1,0:T(8,128)(2,1)S(1)}, bf16[48,2304]{1,0:T(8,128)(2,1)S(1)}, u32[]{:S(2)}, u32[]{:S(2)}) collective-permute-start(bf16[48,2304]{1,0:T(8,128)(2,1)S(1)} %get-tuple-element.50.block), channel_id=1, source_target_pairs={{0,192},{8,56},{16,208},{24,8},{32,224},{40,24},{48,240},{56,40},{... | collective-permute-start | bytes 663560 | tf_op jit(solution)/shard_map/ppermute | solution.py:106
  11.3 2.7 %collective-permute-start.4 = (bf16[48,1920]{1,0:T(8,128)(2,1)S(1)}, bf16[48,1920]{1,0:T(8,128)(2,1)S(1)}, u32[]{:S(2)}, u32[]{:S(2)}) collective-permute-start(bf16[48,1920]{1,0:T(8,128)(2,1)S(1)} %get-tuple-element.46.block), channel_id=1, source_target_pairs={{0,192},{8,56},{16,208},{24,8},{32,224},{40,24},{48,240},{56,40},{... | collective-permute-start | bytes 552968 | tf_op jit(solution)/shard_map/ppermute | solution.py:106
  14.0 3.2 %collective-permute-done.3.before = bf16[48,1920]{1,0:T(8,128)(2,1)S(1)} collective-permute-done((bf16[48,1920]{1,0:T(8,128)(2,1)S(1)}, bf16[48,1920]{1,0:T(8,128)(2,1)S(1)}, u32[]{:S(2)}, u32[]{:S(2)}) %collective-permute-start.3) | collective-permute-done | bytes 184352 | tf_op jit(solution)/shard_map/ppermute | solution.py:106
  17.4 2.7 %collective-permute-start.13 = (bf16[48,1152]{1,0:T(8,128)(2,1)S(1)}, bf16[48,1152]{1,0:T(8,128)(2,1)S(1)}, u32[]{:S(2)}, u32[]{:S(2)}) collective-permute-start(bf16[48,1152]{1,0:T(8,128)(2,1)S(1)} %get-tuple-element.51.refs_0_), channel_id=1, source_target_pairs={{0,192},{8,56},{16,208},{24,8},{32,224},{40,24},{48,240},{56,40},{... | collective-permute-start | bytes 331784 | tf_op jit(solution)/shard_map/ppermute | solution.py:106
  20.1 2.7 %collective-permute-start.7 = (bf16[48,896]{1,0:T(8,128)(2,1)S(1)}, bf16[48,896]{1,0:T(8,128)(2,1)S(1)}, u32[]{:S(2)}, u32[]{:S(2)}) collective-permute-start(bf16[48,896]{1,0:T(8,128)(2,1)S(1)} %get-tuple-element.49.refs_0_), channel_id=1, source_target_pairs={{0,192},{8,56},{16,208},{24,8},{32,224},{40,24},{48,240},{56,40},{... | collective-permute-start | bytes 258056 | tf_op jit(solution)/shard_map/ppermute | solution.py:106
  24.9 3.7 %collective-permute-start.18 = (bf16[4608,512]{1,0:T(8,128)(2,1)S(1)}, bf16[4608,512]{1,0:T(8,128)(2,1)S(1)}, u32[]{:S(2)}, u32[]{:S(2)}) collective-permute-start(bf16[4608,512]{1,0:T(8,128)(2,1)S(1)} %copy-done.1), channel_id=1, source_target_pairs={{0,8},{8,0},{16,24},{24,16},{32,40},{40,32},{48,56},{56,48},{64,72... | collective-permute-start | bytes 14155784 | tf_op jit(solution)/shard_map/ppermute | solution.py:675
  28.6 2.8 %collective-permute-start.11 = (bf16[192,1920]{1,0:T(8,128)(2,1)S(1)}, bf16[192,1920]{1,0:T(8,128)(2,1)S(1)}, u32[]{:S(2)}, u32[]{:S(2)}) collective-permute-start(bf16[192,1920]{1,0:T(8,128)(2,1)S(1)} %join.2.refs_0_), channel_id=1, source_target_pairs={{0,48},{8,200},{16,0},{24,216},{32,16},{40,232},{48,32},{56,248},{... | collective-permute-start | bytes 2211848 | tf_op jit(solution)/shard_map/ppermute | solution.py:106
  31.4 2.7 %collective-permute-start.17 = (bf16[192,2304]{1,0:T(8,128)(2,1)S(1)}, bf16[192,2304]{1,0:T(8,128)(2,1)S(1)}, u32[]{:S(2)}, u32[]{:S(2)}) collective-permute-start(bf16[192,2304]{1,0:T(8,128)(2,1)S(1)} %join.3.refs_0_.t0), channel_id=1, source_target_pairs={{0,48},{8,200},{16,0},{24,216},{32,16},{40,232},{48,32},{56,248},{... | collective-permute-start | bytes 2654216 | tf_op jit(solution)/shard_map/ppermute | solution.py:106
  34.1 2.8 %turn.1 = (bf16[512,3584]{1,0:T(8,128)(2,1)S(1)}, bf16[512,3584]{1,0:T(8,128)(2,1)S(1)}, f32[8,128]{1,0:T(8,128)S(1)}) custom-call(bf16[3584,512]{1,0:T(8,128)(2,1)S(1)} %copy-done, bf16[3584,512]{1,0:T(8,128)(2,1)S(1)} %collective-permute-done.5.refs_0_.refs_4_.other_ref.s_w_other), custom_call_target="tpu_custom_call" | custom-call | bytes 29360128 | tf_op jit(solution)/shard_map/turn/pallas_call | solution.py:520
  36.9 3.7 %collective-permute-done.10.refs_1_.before = bf16[192,1920]{1,0:T(8,128)(2,1)S(1)} collective-permute-done((bf16[192,1920]{1,0:T(8,128)(2,1)S(1)}, bf16[192,1920]{1,0:T(8,128)(2,1)S(1)}, u32[]{:S(2)}, u32[]{:S(2)}) %collective-permute-start.10) | collective-permute-done | bytes 737312 | tf_op jit(solution)/shard_map/ppermute | solution.py:106
  43.5 3.6 %student_near.1 = (f32[576,512]{1,0:T(8,128)S(1)}, f32[576,512]{1,0:T(8,128)S(1)}, bf16[576,1920]{1,0:T(8,128)(2,1)}) custom-call(s32[3]{0:T(128)S(1)} %pad_add_fusion.pos_ref, bf16[192,1920]{1,0:T(8,128)(2,1)S(1)} %join.2.refs_0_, bf16[192,1920]{1,0:T(8,128)(2,1)S(1)} %collective-permute-done.10.refs_1_.before, ...), custom_call_target="tpu_custom_call" | custom-call | tf_op jit(solution)/shard_map/student_near/pallas_call | solution.py:233
  47.1 2.9 %collective-permute-done.16.before.t1 = bf16[192,2304]{1,0:T(8,128)(2,1)S(1)} collective-permute-done((bf16[192,2304]{1,0:T(8,128)(2,1)S(1)}, bf16[192,2304]{1,0:T(8,128)(2,1)S(1)}, u32[]{:S(2)}, u32[]{:S(2)}) %collective-permute-start.16) | collective-permute-done | bytes 884768 | tf_op jit(solution)/shard_map/ppermute | solution.py:106
  51.1 2.9 %collective-permute-start.22 = (bf16[192,1152]{1,0:T(8,128)(2,1)S(1)}, bf16[192,1152]{1,0:T(8,128)(2,1)S(1)}, u32[]{:S(2)}, u32[]{:S(2)}) collective-permute-start(bf16[192,1152]{1,0:T(8,128)(2,1)S(1)} %get-tuple-element.58.refs_0_), channel_id=1, source_target_pairs={{0,48},{8,200},{16,0},{24,216},{32,16},{40,232},{48,32},{56,248},{... | collective-permute-start | bytes 1327112 | tf_op jit(solution)/shard_map/ppermute | solution.py:106
  54.3 5.5 %middle_logits.1 = (f32[192,512]{1,0:T(8,128)S(1)}, f32[192,512]{1,0:T(8,128)S(1)}, bf16[192,1920]{1,0:T(8,128)(2,1)S(1)}, f32[576,512]{1,0:T(8,128)S(1)}, f32[576,512]{1,0:T(8,128)S(1)}) custom-call(s32[3]{0:T(128)S(1)} %pad_add_fusion.pos_ref, bf16[192,1024]{1,0:T(8,128)(2,1)S(1)} %collective-permute-done.14.s_left, ...), custom_call_target="tpu_custom_call" | custom-call | flops 99999997952 | tf_op jit(solution)/shard_map/middle_logits/pallas_call | solution.py:284
  63.7 3.4 %student_logits.1 = (f32[384,512]{1,0:T(8,128)S(1)}, f32[384,128]{1,0:T(8,128)S(1)}, s32[1,768]{1,0:T(1,128)S(1)}, s32[1,768]{1,0:T(1,128)S(1)}) custom-call(s32[3]{0:T(128)S(1)} %pad_add_fusion.pos_ref, f32[576,512]{1,0:T(8,128)S(1)} %get-tuple-element.52.near, f32[192,512]{1,0:T(8,128)S(1)} %get-tuple-element.59.far, ...), custom_call_target="tpu_custom_call" | custom-call | flops 99999997952 | tf_op jit(solution)/shard_map/student_logits/pallas_call | solution.py:365
  67.2 2.4 %teacher_logits.1 = (f32[384,512]{1,0:T(8,128)S(1)}, f32[32,1,1152]{2,1,0:T(1,128)S(1)}) custom-call(s32[3]{0:T(128)S(1)} %pad_add_fusion.pos_ref, f32[576,512]{1,0:T(8,128)S(1)} %get-tuple-element.65.near, f32[192,512]{1,0:T(8,128)S(1)} %get-tuple-element.67.far, f32[576,512]{1,0:T(8,128)S(1)} %collective-permute-done.23.near_got, ...), custom_call_target="tpu_custom_call" | custom-call | tf_op jit(solution)/shard_map/teacher_logits/pallas_call | solution.py:415
  69.5 14.5 %all_to_all.20.x_ref = f32[32,1,1152]{2,1,0:T(1,128)S(1)} all-to-all(f32[32,1,1152]{2,1,0:T(1,128)S(1)} %get-tuple-element.73), channel_id=1, replica_groups=mesh['dp'=32,'vocab'=8] {'dp'}, dimensions={0} | all-to-all | bytes 294912 | tf_op jit(solution)/shard_map/all_to_all | solution.py:708
  84.3 13.4 %all_to_all.21.x_ref = f32[8,1,1152]{2,1,0:T(1,128)S(1)} all-to-all(f32[8,1,1152]{2,1,0:T(1,128)S(1)} %merge_stats.1), channel_id=1, replica_groups=mesh['dp'=32,'vocab'=8] {'vocab'}, dimensions={0} | all-to-all | bytes 73728 | tf_op jit(solution)/shard_map/all_to_all | solution.py:709
  103.6 3.6 %grad_hidden.1 = bf16[384,3584]{1,0:T(8,128)(2,1)} custom-call(f32[384,3584]{1,0:T(8,128)S(1)} %grad_hidden_own.1.part_ref, bf16[384,512]{1,0:T(8,128)(2,1)S(1)} %collective-permute-done.25.got_ref, bf16[512,3584]{1,0:T(8,128)(2,1)S(1)} %get-tuple-element.79.other_w), custom_call_target="tpu_custom_call" | custom-call | tf_op jit(solution)/shard_map/grad_hidden/pallas_call | solution.py:570
  107.3 3.7 %all-to-all-start.2 = ((bf16[4,96,3584]{2,1,0:T(8,128)(2,1)}), bf16[4,96,3584]{2,1,0:T(8,128)(2,1)S(1)}, u32[]{:S(2)}, u32[]{:S(2)}) async-start(bf16[4,96,3584]{2,1,0:T(8,128)(2,1)} %bitcast.9), calls=%async_computation.2 | async-start | bytes 5505024 | tf_op jit(solution)/shard_map/all_to_all | solution.py:714
  115.0 8.6 %grad_head.1 = (bf16[3584,512]{1,0:T(8,128)(2,1)}, f32[8,128]{1,0:T(8,128)S(1)}) custom-call(s32[3]{0:T(128)S(1)} %pad_add_fusion.pos_ref, bf16[576,1920]{1,0:T(8,128)(2,1)} %get-tuple-element.80.near_note.near, bf16[192,1920]{1,0:T(8,128)(2,1)S(1)} %copy-done.3, bf16[576,1920]{1,0:T(8,128)(2,1)} %collective-permute-done.26.near_got, ...), custom_call_target="tpu_custom_call" | custom-call | tf_op jit(solution)/shard_map/grad_head/pallas_call | solution.py:640
  123.6 6.6 %all-to-all-done.2.x_ref = bf16[4,96,3584]{2,1,0:T(8,128)(2,1)S(1)} async-done(((bf16[4,96,3584]{2,1,0:T(8,128)(2,1)}), bf16[4,96,3584]{2,1,0:T(8,128)(2,1)S(1)}, u32[]{:S(2)}, u32[]{:S(2)}) %all-to-all-start.2) | async-done | bytes 2752544 | tf_op jit(solution)/shard_map/all_to_all | solution.py:714
  130.6 25.6 %all_to_all.22 = bf16[32,24,448]{2,1,0:T(8,128)(2,1)S(1)} all-to-all(bf16[32,24,448]{2,1,0:T(8,128)(2,1)S(1)} %bitcast.8), channel_id=1, replica_groups={{0,1,2,3,4,5,6,7,16,17,18,19,20,21,22,23,32,33,34,35,36,37,38,39,48,49,..., dimensions={0} | all-to-all | bytes 1376256 | tf_op jit(solution)/shard_map/all_to_all | solution.py:721
  (69 shorter events, 25.3 us)
Async XLA Ops:
  0.6 7.1 %collective-permute-start.2 = (bf16[24,4608]{1,0:T(8,128)(2,1)}, bf16[24,4608]{1,0:T(8,128)(2,1)S(1)}, u32[]{:S(2)}, u32[]{:S(2)}) collective-permute-start(bf16[24,4608]{1,0:T(8,128)(2,1)} %t_ref.1), channel_id=1, source_target_pairs={{0,8},{8,0},{16,24},{24,16},{32,40},{40,32},{48,56},{56,48},{64,72... | collective-permute-start | bytes 663560 | tf_op jit(solution)/shard_map/ppermute | solution.py:675
  8.5 8.8 %collective-permute-start.5 = (bf16[3584,512]{1,0:T(8,128)(2,1)}, bf16[3584,512]{1,0:T(8,128)(2,1)S(1)}, u32[]{:S(2)}, u32[]{:S(2)}) collective-permute-start(bf16[3584,512]{1,0:T(8,128)(2,1)} %s_w.1), channel_id=1, source_target_pairs={{0,8},{8,0},{16,24},{24,16},{32,40},{40,32},{48,56},{56,48},{64,72... | collective-permute-start | bytes 11010056 | tf_op jit(solution)/shard_map/ppermute | solution.py:675
  8.6 8.6 %collective-permute-start.8 = (bf16[48,2304]{1,0:T(8,128)(2,1)S(1)}, bf16[48,2304]{1,0:T(8,128)(2,1)S(1)}, u32[]{:S(2)}, u32[]{:S(2)}) collective-permute-start(bf16[48,2304]{1,0:T(8,128)(2,1)S(1)} %get-tuple-element.50.block), channel_id=1, source_target_pairs={{0,64},{8,24},{16,80},{24,40},{32,96},{40,56},{48,112},{56,8},{64,... | collective-permute-start | bytes 663560 | tf_op jit(solution)/shard_map/ppermute | solution.py:106
  8.6 8.6 %collective-permute-start.9 = (bf16[48,2304]{1,0:T(8,128)(2,1)S(1)}, bf16[48,2304]{1,0:T(8,128)(2,1)S(1)}, u32[]{:S(2)}, u32[]{:S(2)}) collective-permute-start(bf16[48,2304]{1,0:T(8,128)(2,1)S(1)} %get-tuple-element.50.block), channel_id=1, source_target_pairs={{0,192},{8,56},{16,208},{24,8},{32,224},{40,24},{48,240},{56,40},{... | collective-permute-start | bytes 663560 | tf_op jit(solution)/shard_map/ppermute | solution.py:106
  11.3 5.9 %collective-permute-start.3 = (bf16[48,1920]{1,0:T(8,128)(2,1)S(1)}, bf16[48,1920]{1,0:T(8,128)(2,1)S(1)}, u32[]{:S(2)}, u32[]{:S(2)}) collective-permute-start(bf16[48,1920]{1,0:T(8,128)(2,1)S(1)} %get-tuple-element.46.block), channel_id=1, source_target_pairs={{0,64},{8,24},{16,80},{24,40},{32,96},{40,56},{48,112},{56,8},{64,... | collective-permute-start | bytes 552968 | tf_op jit(solution)/shard_map/ppermute | solution.py:106
  11.3 5.9 %collective-permute-start.4 = (bf16[48,1920]{1,0:T(8,128)(2,1)S(1)}, bf16[48,1920]{1,0:T(8,128)(2,1)S(1)}, u32[]{:S(2)}, u32[]{:S(2)}) collective-permute-start(bf16[48,1920]{1,0:T(8,128)(2,1)S(1)} %get-tuple-element.46.block), channel_id=1, source_target_pairs={{0,192},{8,56},{16,208},{24,8},{32,224},{40,24},{48,240},{56,40},{... | collective-permute-start | bytes 552968 | tf_op jit(solution)/shard_map/ppermute | solution.py:106
  17.3 7.5 %collective-permute-start.12 = (bf16[48,1152]{1,0:T(8,128)(2,1)S(1)}, bf16[48,1152]{1,0:T(8,128)(2,1)S(1)}, u32[]{:S(2)}, u32[]{:S(2)}) collective-permute-start(bf16[48,1152]{1,0:T(8,128)(2,1)S(1)} %get-tuple-element.53), channel_id=1, source_target_pairs={{0,64},{8,24},{16,80},{24,40},{32,96},{40,56},{48,112},{56,8},{64,... | collective-permute-start | bytes 331784 | tf_op jit(solution)/shard_map/ppermute | solution.py:106
  17.4 7.4 %collective-permute-start.13 = (bf16[48,1152]{1,0:T(8,128)(2,1)S(1)}, bf16[48,1152]{1,0:T(8,128)(2,1)S(1)}, u32[]{:S(2)}, u32[]{:S(2)}) collective-permute-start(bf16[48,1152]{1,0:T(8,128)(2,1)S(1)} %get-tuple-element.51.refs_0_), channel_id=1, source_target_pairs={{0,192},{8,56},{16,208},{24,8},{32,224},{40,24},{48,240},{56,40},{... | collective-permute-start | bytes 331784 | tf_op jit(solution)/shard_map/ppermute | solution.py:106
  20.1 4.7 %collective-permute-start.6 = (bf16[48,1024]{1,0:T(8,128)(2,1)S(1)}, bf16[48,1024]{1,0:T(8,128)(2,1)S(1)}, u32[]{:S(2)}, u32[]{:S(2)}) collective-permute-start(bf16[48,1024]{1,0:T(8,128)(2,1)S(1)} %get-tuple-element.48), channel_id=1, source_target_pairs={{0,64},{8,24},{16,80},{24,40},{32,96},{40,56},{48,112},{56,8},{64,... | collective-permute-start | bytes 294920 | tf_op jit(solution)/shard_map/ppermute | solution.py:106
  20.1 4.2 %collective-permute-start.7 = (bf16[48,896]{1,0:T(8,128)(2,1)S(1)}, bf16[48,896]{1,0:T(8,128)(2,1)S(1)}, u32[]{:S(2)}, u32[]{:S(2)}) collective-permute-start(bf16[48,896]{1,0:T(8,128)(2,1)S(1)} %get-tuple-element.49.refs_0_), channel_id=1, source_target_pairs={{0,192},{8,56},{16,208},{24,8},{32,224},{40,24},{48,240},{56,40},{... | collective-permute-start | bytes 258056 | tf_op jit(solution)/shard_map/ppermute | solution.py:106
  24.9 25.9 %collective-permute-start.18 = (bf16[4608,512]{1,0:T(8,128)(2,1)S(1)}, bf16[4608,512]{1,0:T(8,128)(2,1)S(1)}, u32[]{:S(2)}, u32[]{:S(2)}) collective-permute-start(bf16[4608,512]{1,0:T(8,128)(2,1)S(1)} %copy-done.1), channel_id=1, source_target_pairs={{0,8},{8,0},{16,24},{24,16},{32,40},{40,32},{48,56},{56,48},{64,72... | collective-permute-start | bytes 14155784 | tf_op jit(solution)/shard_map/ppermute | solution.py:675
  28.6 12.0 %collective-permute-start.10 = (bf16[192,1920]{1,0:T(8,128)(2,1)S(1)}, bf16[192,1920]{1,0:T(8,128)(2,1)S(1)}, u32[]{:S(2)}, u32[]{:S(2)}) collective-permute-start(bf16[192,1920]{1,0:T(8,128)(2,1)S(1)} %join.2.refs_0_), channel_id=1, source_target_pairs={{0,16},{8,72},{16,32},{24,88},{32,48},{40,104},{48,0},{56,120},{64... | collective-permute-start | bytes 2211848 | tf_op jit(solution)/shard_map/ppermute | solution.py:106
  28.6 12.0 %collective-permute-start.11 = (bf16[192,1920]{1,0:T(8,128)(2,1)S(1)}, bf16[192,1920]{1,0:T(8,128)(2,1)S(1)}, u32[]{:S(2)}, u32[]{:S(2)}) collective-permute-start(bf16[192,1920]{1,0:T(8,128)(2,1)S(1)} %join.2.refs_0_), channel_id=1, source_target_pairs={{0,48},{8,200},{16,0},{24,216},{32,16},{40,232},{48,32},{56,248},{... | collective-permute-start | bytes 2211848 | tf_op jit(solution)/shard_map/ppermute | solution.py:106
  31.4 18.6 %collective-permute-start.16 = (bf16[192,2304]{1,0:T(8,128)(2,1)S(1)}, bf16[192,2304]{1,0:T(8,128)(2,1)S(1)}, u32[]{:S(2)}, u32[]{:S(2)}) collective-permute-start(bf16[192,2304]{1,0:T(8,128)(2,1)S(1)} %join.3.refs_0_.t0), channel_id=1, source_target_pairs={{0,16},{8,72},{16,32},{24,88},{32,48},{40,104},{48,0},{56,120},{64... | collective-permute-start | bytes 2654216 | tf_op jit(solution)/shard_map/ppermute | solution.py:106
  31.4 19.4 %collective-permute-start.17 = (bf16[192,2304]{1,0:T(8,128)(2,1)S(1)}, bf16[192,2304]{1,0:T(8,128)(2,1)S(1)}, u32[]{:S(2)}, u32[]{:S(2)}) collective-permute-start(bf16[192,2304]{1,0:T(8,128)(2,1)S(1)} %join.3.refs_0_.t0), channel_id=1, source_target_pairs={{0,48},{8,200},{16,0},{24,216},{32,16},{40,232},{48,32},{56,248},{... | collective-permute-start | bytes 2654216 | tf_op jit(solution)/shard_map/ppermute | solution.py:106
  40.6 13.6 %collective-permute-start.14 = (bf16[192,1024]{1,0:T(8,128)(2,1)S(1)}, bf16[192,1024]{1,0:T(8,128)(2,1)S(1)}, u32[]{:S(2)}, u32[]{:S(2)}) collective-permute-start(bf16[192,1024]{1,0:T(8,128)(2,1)S(1)} %get-tuple-element.55), channel_id=1, source_target_pairs={{0,16},{8,72},{16,32},{24,88},{32,48},{40,104},{48,0},{56,120},{64... | collective-permute-start | bytes 1179656 | tf_op jit(solution)/shard_map/ppermute | solution.py:106
  41.6 12.4 %collective-permute-start.15 = (bf16[192,896]{1,0:T(8,128)(2,1)S(1)}, bf16[192,896]{1,0:T(8,128)(2,1)S(1)}, u32[]{:S(2)}, u32[]{:S(2)}) collective-permute-start(bf16[192,896]{1,0:T(8,128)(2,1)S(1)} %get-tuple-element.56), channel_id=1, source_target_pairs={{0,48},{8,200},{16,0},{24,216},{32,16},{40,232},{48,32},{56,248},{... | collective-permute-start | bytes 1032200 | tf_op jit(solution)/shard_map/ppermute | solution.py:106
  50.1 13.6 %collective-permute-start.19 = (f32[576,512]{1,0:T(8,128)S(1)}, f32[576,512]{1,0:T(8,128)S(1)}, u32[]{:S(2)}, u32[]{:S(2)}) collective-permute-start(f32[576,512]{1,0:T(8,128)S(1)} %get-tuple-element.60), channel_id=1, source_target_pairs={{0,8},{8,0},{16,24},{24,16},{32,40},{40,32},{48,56},{56,48},{64,72... | collective-permute-start | bytes 3538952 | tf_op jit(solution)/shard_map/ppermute | solution.py:675
  50.9 9.8 %collective-permute-start.21 = (bf16[192,1152]{1,0:T(8,128)(2,1)S(1)}, bf16[192,1152]{1,0:T(8,128)(2,1)S(1)}, u32[]{:S(2)}, u32[]{:S(2)}) collective-permute-start(bf16[192,1152]{1,0:T(8,128)(2,1)S(1)} %get-tuple-element.66), channel_id=1, source_target_pairs={{0,16},{8,72},{16,32},{24,88},{32,48},{40,104},{48,0},{56,120},{64... | collective-permute-start | bytes 1327112 | tf_op jit(solution)/shard_map/ppermute | solution.py:106
  51.1 9.7 %collective-permute-start.22 = (bf16[192,1152]{1,0:T(8,128)(2,1)S(1)}, bf16[192,1152]{1,0:T(8,128)(2,1)S(1)}, u32[]{:S(2)}, u32[]{:S(2)}) collective-permute-start(bf16[192,1152]{1,0:T(8,128)(2,1)S(1)} %get-tuple-element.58.refs_0_), channel_id=1, source_target_pairs={{0,48},{8,200},{16,0},{24,216},{32,16},{40,232},{48,32},{56,248},{... | collective-permute-start | bytes 1327112 | tf_op jit(solution)/shard_map/ppermute | solution.py:106
  60.7 6.5 %collective-permute-start.23 = (f32[576,512]{1,0:T(8,128)S(1)}, f32[576,512]{1,0:T(8,128)S(1)}, u32[]{:S(2)}, u32[]{:S(2)}) collective-permute-start(f32[576,512]{1,0:T(8,128)S(1)} %get-tuple-element.68), channel_id=1, source_target_pairs={{0,8},{8,0},{16,24},{24,16},{32,40},{40,32},{48,56},{56,48},{64,72... | collective-permute-start | bytes 3538952 | tf_op jit(solution)/shard_map/ppermute | solution.py:675
  99.4 4.2 %collective-permute-start.25 = (bf16[384,512]{1,0:T(8,128)(2,1)S(1)}, bf16[384,512]{1,0:T(8,128)(2,1)S(1)}, u32[]{:S(2)}, u32[]{:S(2)}) collective-permute-start(bf16[384,512]{1,0:T(8,128)(2,1)S(1)} %get-tuple-element.78), channel_id=1, source_target_pairs={{0,8},{8,0},{16,24},{24,16},{32,40},{40,32},{48,56},{56,48},{64,72... | collective-permute-start | bytes 1179656 | tf_op jit(solution)/shard_map/ppermute | solution.py:675
  107.2 6.7 %collective-permute-start.26 = (bf16[576,1920]{1,0:T(8,128)(2,1)}, bf16[576,1920]{1,0:T(8,128)(2,1)}, u32[]{:S(2)}, u32[]{:S(2)}) collective-permute-start(bf16[576,1920]{1,0:T(8,128)(2,1)} %get-tuple-element.80.near_note.near), channel_id=1, source_target_pairs={{0,8},{8,0},{16,24},{24,16},{32,40},{40,32},{48,56},{56,48},{64,72... | collective-permute-start | bytes 6635528 | tf_op jit(solution)/shard_map/ppermute | solution.py:675
  107.3 22.8 %all-to-all-start.2 = ((bf16[4,96,3584]{2,1,0:T(8,128)(2,1)}), bf16[4,96,3584]{2,1,0:T(8,128)(2,1)S(1)}, u32[]{:S(2)}, u32[]{:S(2)}) async-start(bf16[4,96,3584]{2,1,0:T(8,128)(2,1)} %bitcast.9), calls=%async_computation.2 | async-start | bytes 5505024 | tf_op jit(solution)/shard_map/all_to_all | solution.py:714
  (9 other events, 46.0 us)
